TPU v7x, 512 devices: a whole 4x4x16 slice. The times are simulated.
512 devices in a mesh: view: 2 (over core), gz: 32 (over z_lo, y), gy: 8 (over x, z_hi).
Axes of the slice: x: 4, y: 4, z: 16 (z_hi: 2, z_lo: 8; z = z_hi * 8 + z_lo), core: 2. Of those that a mesh axis runs over, the one named last changes fastest.
Arguments:
- observed: float32 [2, 2048, 128, 256], P('view', 'gz', 'gy'), may hold values from 0.5 to 4
- start: float32 [2048, 128, 256], P('gz', 'gy'), may hold values from 0.5 to 2
- spread_z: float32 [2, 31], P('view'), may hold values from 0.05 to 1
- spread_y: float32 [2, 7], P('view'), may hold values from 0.1 to 1
- spread_x: float32 [2, 7], P('view'), may hold values from 0.1 to 1
Outputs:
- estimate: float32 [2048, 128, 256], P('gz', 'gy')
All inputs are finite; a program needn't handle non-finite values.
Results may differ from a plain program's by a relative error of at most 0.0001.
Values sent between devices are 32-bit elements; how exact they have to be, the bound alone decides.
No kernel may reach another device: no remote copies, remote signals or barrier semaphores. Data moves between devices by JAX's collectives and lax.ppermute only.
A program may use at most 64 MiB of HBM per device.

v0:
```python
import jax
import jax.numpy as jnp
from jax import lax
from jax.sharding import PartitionSpec as P

KZ = 31
KY = 7
KX = 7
ITERS = 2


def padded_2(x, sides, width):
    for axis, dim in sides:
        peers, length = (lax.axis_size(axis), x.shape[dim])
        up = [(i, (i + 1) % peers) for i in range(peers - 1)]
        down = [(j, i) for i, j in up]
        last = lax.slice_in_dim(x, length - width, length, axis=dim)
        first = lax.slice_in_dim(x, 0, width, axis=dim)
        before = lax.ppermute(last, axis, up)
        after = lax.ppermute(first, axis, down)
        x = jnp.concatenate([before, x, after], axis=dim)
    return x


def split_up(x, dim, peers):
    before, after = (x.shape[:dim], x.shape[dim + 1 :])
    return jnp.moveaxis(x.reshape(*before, peers, -1, *after), dim, 0)


def sent_and_summed(x, axis, dim):
    pieces = split_up(x, dim, lax.axis_size(axis))
    arrived = lax.all_to_all(pieces, axis, split_axis=0, concat_axis=0, tiled=True)
    return arrived.sum(axis=0)


def copy_for_each(x, axis):
    peers = lax.axis_size(axis)
    return lax.all_to_all(jnp.broadcast_to(x[None], (peers, *x.shape)), axis, 0, 0, tiled=True)


def in_order(pieces, dim):
    pieces = jnp.moveaxis(pieces, 0, dim)
    shape = pieces.shape
    return pieces.reshape(*shape[:dim], shape[dim] * shape[dim + 1], *shape[dim + 2 :])


def gathered_copies(x, axis, dim):
    pieces = copy_for_each(x, axis)
    return in_order(pieces, dim)


def correlate(field, weights, along, margin):
    padding = [(0, 0), (0, 0), (0, 0)]
    padding[along] = (margin, margin)
    padded = jnp.pad(field, padding)
    taps = weights.shape[0]
    length = padded.shape[along] - taps + 1
    total = weights[0] * lax.slice_in_dim(padded, 0, length, 1, along)
    for offset in range(1, taps):
        total = total + weights[offset] * lax.slice_in_dim(
            padded, offset, offset + length, 1, along
        )
    return total


def blur_local(field, weight_z, weight_y, weight_x):
    padded = padded_2(field, (("gz", 0),), KZ // 2)
    field = correlate(padded, weight_z, 0, 0)
    padded = padded_2(field, (("gy", 1),), KY // 2)
    field = correlate(padded, weight_y, 1, 0)
    return correlate(field, weight_x, 2, KX // 2)


def on_device(observed, start, spread_z, spread_y, spread_x):
    recorded = observed[0]
    weight_z = spread_z[0] / jnp.sum(spread_z[0])
    weight_y = spread_y[0] / jnp.sum(spread_y[0])
    weight_x = spread_x[0] / jnp.sum(spread_x[0])
    estimate = start
    for sweep in range(ITERS):
        blurred = blur_local(estimate, weight_z, weight_y, weight_x)
        quotient = recorded / blurred
        correction = blur_local(quotient, weight_z[::-1], weight_y[::-1], weight_x[::-1])
        share = sent_and_summed(correction, "view", 0)
        planes = share.shape[0]
        own_part = lax.dynamic_slice_in_dim(estimate, lax.axis_index("view") * planes, planes, 0)
        estimate = gathered_copies(own_part * (0.5 * share), "view", 0)
    return estimate


def solution(mesh):
    return jax.shard_map(
        on_device,
        mesh=mesh,
        in_specs=(
            P("view", "gz", "gy", None),
            P("gz", "gy", None),
            P("view", None),
            P("view", None),
            P("view", None),
        ),
        out_specs=P("gz", "gy", None),
        check_vma=False,
    )
```

profile of v0, /device:TPU:63, one launch (start us, length us, event | category | flops | bytes accessed | tf_op | source)
XLA Modules:
  0.0 435.2 jit_solution(896753772274731695)
XLA Ops:
  0.0 1.2 fusion.415
  1.2 3.2 collective-permute-start
  4.4 2.1 collective-permute-start.1
  6.5 1.3 reduce_sum.47
  7.8 0.7 reverse.11
  8.5 1.3 broadcast_divide_fusion
  9.8 0.7 fusion.422
  10.5 1.3 reduce_sum.46
  11.8 0.7 reverse.10
  12.5 1.3 broadcast_divide_fusion.2
  13.8 0.7 fusion.423
  14.6 1.3 reduce_sum.45
  15.8 0.7 reverse.9
  16.6 1.3 broadcast_divide_fusion.4
  18.2 23.5 %fusion.378 = f32[64,16,256]{2,1,0:T(8,128)S(1)} fusion(f32[79,16,256]{2,1,0:T(8,128)S(1)} %constant_dynamic-update-slice_fusion.2, f32[79,16,256]{2,1,0:T(8,128)S(1)} %get-tuple-element.19, f32[64,16,256]{2,1,0:T(8,128)S(1)} %copy-done, f32[]{:T(128)} %bitcast.39, f32[]{:T(128)} %bitcast.38, f32[]{:T(128)} %bitcast.37, f32[]{:T(128)} %bitcast.36, ...), kind=kLoop, calls=%fused_computation.617 | loop fusion | flops 15990784 | bytes 33554556 | tf_op jit(solution)/shard_map/add | solution.py:60
  41.9 14.8 %collective-permute-start.3 = (f32[64,3,256]{2,1,0:T(4,128)S(1)}, f32[64,3,256]{2,1,0:T(4,128)S(1)}, u32[]{:S(2)}, u32[]{:S(2)}) collective-permute-start(f32[64,3,256]{2,1,0:T(4,128)S(1)} %get-tuple-element.18), channel_id=1, source_target_pairs={{1,0},{2,1},{3,2},{4,3},{5,4},{6,5},{7,6},{9,8},{10,9},{11,10},{12... | collective-permute-start | bytes 589832 | tf_op jit(solution)/shard_map/ppermute | solution.py:20
  56.7 1.9 collective-permute-start.2
  59.9 19.0 %collective-permute-done.3 = f32[64,3,256]{2,1,0:T(4,128)S(1)} collective-permute-done((f32[64,3,256]{2,1,0:T(4,128)S(1)}, f32[64,3,256]{2,1,0:T(4,128)S(1)}, u32[]{:S(2)}, u32[]{:S(2)}) %collective-permute-start.3) | collective-permute-done | bytes 196640 | tf_op jit(solution)/shard_map/ppermute | solution.py:20
  79.0 22.6 %collective-permute-done.2 = f32[64,3,256]{2,1,0:T(4,128)S(1)} collective-permute-done((f32[64,3,256]{2,1,0:T(4,128)S(1)}, f32[64,3,256]{2,1,0:T(4,128)S(1)}, u32[]{:S(2)}, u32[]{:S(2)}) %collective-permute-start.2) | collective-permute-done | bytes 196640 | tf_op jit(solution)/shard_map/ppermute | solution.py:19
  101.5 5.6 %fusion.45 = f32[64,16,256]{2,1,0:T(8,128)S(1)} fusion(f32[64,16,256]{2,1,0:T(8,128)S(1)} %fusion.378, f32[64,3,256]{2,1,0:T(4,128)S(1)} %collective-permute-done.3, f32[64,3,256]{2,1,0:T(4,128)S(1)} %collective-permute-done.2, f32[]{:T(128)} %bitcast.45, f32[]{:T(128)} %bitcast.44, f32[]{:T(128)} %bitcast.43, f32[]{:T(128)} %bitcast.42, f32[]{:T(128)} %bitcast.41, ...), kind=kLoop, calls=%fused_computation.269 | loop fusion | flops 4980736 | bytes 2490396 | tf_op jit(solution)/shard_map/add | solution.py:60
  107.1 5.9 %fusion.321 = f32[64,16,256]{2,1,0:T(8,128)S(1)} fusion(f32[64,16,256]{2,1,0:T(8,128)S(1)} %fusion.45, f32[1,64,16,256]{3,2,1,0:T(8,128)S(1)} %copy-done.1, f32[]{:T(128)} %bitcast.51, f32[]{:T(128)} %bitcast.50, f32[]{:T(128)} %bitcast.49, f32[]{:T(128)} %bitcast.48, f32[]{:T(128)} %bitcast.47, f32[]{:T(128)} %bitcast.46, f32[]{:T(128)} %bitcast.7), kind=kLoop, calls=%fused_computation.545 | loop fusion | flops 3670016 | bytes 3145756 | tf_op jit(solution)/shard_map/div | solution.py:82
  113.1 0.8 fusion.413
  113.9 2.8 collective-permute-start.5
  116.7 4.6 %collective-permute-start.4 = (f32[15,16,256]{2,1,0:T(8,128)}, f32[15,16,256]{2,1,0:T(8,128)}, u32[]{:S(2)}, u32[]{:S(2)}) collective-permute-start(f32[15,16,256]{2,1,0:T(8,128)} %get-tuple-element.15), channel_id=1, source_target_pairs={{0,8},{8,16},{16,24},{24,32},{32,40},{40,48},{48,56},{56,64},{64,7... | collective-permute-start | bytes 737288 | tf_op jit(solution)/shard_map/ppermute | solution.py:19
  121.3 0.7 fusion.419
  122.0 0.7 fusion.418
  122.7 0.9 collective-permute-done.5
  123.6 1.1 collective-permute-done.4
  124.7 25.9 %fusion.231 = f32[64,16,256]{2,1,0:T(8,128)S(1)} fusion(f32[64,16,256]{2,1,0:T(8,128)S(1)} %fusion.321, f32[15,16,256]{2,1,0:T(8,128)S(1)} %collective-permute-done.5, f32[15,16,256]{2,1,0:T(8,128)} %collective-permute-done.4, f32[]{:T(128)} %bitcast.81, f32[]{:T(128)} %bitcast.80, f32[]{:T(128)} %bitcast.79, f32[]{:T(128)} %bitcast.78, f32[]{:T(128)} %bitcast.77, ...), kind=kLoop, calls=%fused_computation.455 | loop fusion | flops 23855104 | bytes 2588796 | tf_op jit(solution)/shard_map/add | solution.py:60
  150.7 12.1 %collective-permute-start.7 = (f32[64,3,256]{2,1,0:T(4,128)S(1)}, f32[64,3,256]{2,1,0:T(4,128)S(1)}, u32[]{:S(2)}, u32[]{:S(2)}) collective-permute-start(f32[64,3,256]{2,1,0:T(4,128)S(1)} %get-tuple-element.14), channel_id=1, source_target_pairs={{1,0},{2,1},{3,2},{4,3},{5,4},{6,5},{7,6},{9,8},{10,9},{11,10},{12... | collective-permute-start | bytes 589832 | tf_op jit(solution)/shard_map/ppermute | solution.py:20
  162.9 1.9 collective-permute-start.6
  166.1 11.2 %collective-permute-done.7 = f32[64,3,256]{2,1,0:T(4,128)S(1)} collective-permute-done((f32[64,3,256]{2,1,0:T(4,128)S(1)}, f32[64,3,256]{2,1,0:T(4,128)S(1)}, u32[]{:S(2)}, u32[]{:S(2)}) %collective-permute-start.7) | collective-permute-done | bytes 196640 | tf_op jit(solution)/shard_map/ppermute | solution.py:20
  177.4 26.9 %collective-permute-done.6 = f32[64,3,256]{2,1,0:T(4,128)S(1)} collective-permute-done((f32[64,3,256]{2,1,0:T(4,128)S(1)}, f32[64,3,256]{2,1,0:T(4,128)S(1)}, u32[]{:S(2)}, u32[]{:S(2)}) %collective-permute-start.6) | collective-permute-done | bytes 196640 | tf_op jit(solution)/shard_map/ppermute | solution.py:19
  204.3 5.6 %fusion.31 = f32[64,16,256]{2,1,0:T(8,128)S(1)} fusion(f32[64,16,256]{2,1,0:T(8,128)S(1)} %fusion.231, f32[64,3,256]{2,1,0:T(4,128)S(1)} %collective-permute-done.7, f32[64,3,256]{2,1,0:T(4,128)S(1)} %collective-permute-done.6, f32[]{:T(128)} %bitcast.87, f32[]{:T(128)} %bitcast.86, f32[]{:T(128)} %bitcast.85, f32[]{:T(128)} %bitcast.84, f32[]{:T(128)} %bitcast.83, ...), kind=kLoop, calls=%fused_computation.255 | loop fusion | flops 4980736 | bytes 2490396 | tf_op jit(solution)/shard_map/add | solution.py:60
  210.0 6.0 %fusion.333 = f32[64,16,256]{2,1,0:T(8,128)S(1)} fusion(f32[64,16,256]{2,1,0:T(8,128)S(1)} %fusion.31, f32[]{:T(128)} %bitcast.93, f32[]{:T(128)} %bitcast.92, f32[]{:T(128)} %bitcast.91, f32[]{:T(128)} %bitcast.90, f32[]{:T(128)} %bitcast.89, f32[]{:T(128)} %bitcast.88, f32[]{:T(128)} %bitcast.1), kind=kLoop, calls=%fused_computation.557 | loop fusion | flops 3407872 | bytes 2097180 | tf_op jit(solution)/shard_map/add | solution.py:60
  216.0 4.8 %all_to_all.20 = f32[2,32,16,256]{3,2,1,0:T(8,128)S(1)} all-to-all(f32[2,32,16,256]{3,2,1,0:T(8,128)S(1)} %bitcast.107), channel_id=1, replica_groups=mesh['view'=2,'gz'=32,'gy'=8] {'view'}, dimensions={0} | all-to-all | bytes 2097152 | tf_op jit(solution)/shard_map/all_to_all | solution.py:32
  220.7 0.9 reduce_sum.48
  221.6 1.1 multiply_multiply_fusion.1
  222.9 4.6 %all_to_all.21 = f32[2,32,16,256]{3,2,1,0:T(8,128)S(1)} all-to-all(f32[2,32,16,256]{3,2,1,0:T(8,128)S(1)} %broadcast_in_dim.4), channel_id=1, replica_groups=mesh['view'=2,'gz'=32,'gy'=8] {'view'}, dimensions={0} | all-to-all | bytes 2097152 | tf_op jit(solution)/shard_map/all_to_all | solution.py:38
  227.5 1.9 collective-permute-start.9
  229.5 5.7 %collective-permute-start.8 = (f32[15,16,256]{2,1,0:T(8,128)S(1)}, f32[15,16,256]{2,1,0:T(8,128)S(1)}, u32[]{:S(2)}, u32[]{:S(2)}) collective-permute-start(f32[15,16,256]{2,1,0:T(8,128)S(1)} %get-tuple-element.11), channel_id=1, source_target_pairs={{0,8},{8,16},{16,24},{24,32},{32,40},{40,48},{48,56},{56,64},{64,7... | collective-permute-start | bytes 737288 | tf_op jit(solution)/shard_map/ppermute | solution.py:19
  235.1 3.6 collective-permute-done.9
  238.7 0.9 collective-permute-done.8
  239.6 23.7 %fusion.145 = f32[64,16,256]{2,1,0:T(8,128)S(1)} fusion(f32[64,16,256]{2,1,0:T(8,128)S(1)} %bitcast.104, f32[15,16,256]{2,1,0:T(8,128)S(1)} %collective-permute-done.9, f32[15,16,256]{2,1,0:T(8,128)S(1)} %collective-permute-done.8, f32[]{:T(128)} %bitcast.39, f32[]{:T(128)} %bitcast.38, f32[]{:T(128)} %bitcast.37, f32[]{:T(128)} %bitcast.36, f32[]{:T(128)} %bitcast.35, ...), kind=kLoop, calls=%fused_computation.369 | loop fusion | flops 23855104 | bytes 2588796 | tf_op jit(solution)/shard_map/add | solution.py:60
  263.4 10.8 %collective-permute-start.11 = (f32[64,3,256]{2,1,0:T(4,128)S(1)}, f32[64,3,256]{2,1,0:T(4,128)S(1)}, u32[]{:S(2)}, u32[]{:S(2)}) collective-permute-start(f32[64,3,256]{2,1,0:T(4,128)S(1)} %get-tuple-element.10), channel_id=1, source_target_pairs={{1,0},{2,1},{3,2},{4,3},{5,4},{6,5},{7,6},{9,8},{10,9},{11,10},{12... | collective-permute-start | bytes 589832 | tf_op jit(solution)/shard_map/ppermute | solution.py:20
  274.2 3.2 collective-permute-start.10
  277.4 10.8 %collective-permute-done.11 = f32[64,3,256]{2,1,0:T(4,128)S(1)} collective-permute-done((f32[64,3,256]{2,1,0:T(4,128)S(1)}, f32[64,3,256]{2,1,0:T(4,128)S(1)}, u32[]{:S(2)}, u32[]{:S(2)}) %collective-permute-start.11) | collective-permute-done | bytes 196640 | tf_op jit(solution)/shard_map/ppermute | solution.py:20
  288.3 32.7 %collective-permute-done.10 = f32[64,3,256]{2,1,0:T(4,128)S(1)} collective-permute-done((f32[64,3,256]{2,1,0:T(4,128)S(1)}, f32[64,3,256]{2,1,0:T(4,128)S(1)}, u32[]{:S(2)}, u32[]{:S(2)}) %collective-permute-start.10) | collective-permute-done | bytes 196640 | tf_op jit(solution)/shard_map/ppermute | solution.py:19
  320.9 5.5 %fusion.17 = f32[64,16,256]{2,1,0:T(8,128)S(1)} fusion(f32[64,16,256]{2,1,0:T(8,128)S(1)} %fusion.145, f32[64,3,256]{2,1,0:T(4,128)S(1)} %collective-permute-done.11, f32[64,3,256]{2,1,0:T(4,128)S(1)} %collective-permute-done.10, f32[]{:T(128)} %bitcast.45, f32[]{:T(128)} %bitcast.44, f32[]{:T(128)} %bitcast.43, f32[]{:T(128)} %bitcast.42, f32[]{:T(128)} %bitcast.41, ...), kind=kLoop, calls=%fused_computation.241 | loop fusion | flops 4980736 | bytes 2490396 | tf_op jit(solution)/shard_map/add | solution.py:60
  326.4 5.9 %fusion.346 = f32[64,16,256]{2,1,0:T(8,128)S(1)} fusion(f32[64,16,256]{2,1,0:T(8,128)S(1)} %fusion.17, f32[1,64,16,256]{3,2,1,0:T(8,128)S(1)} %copy-done.1, f32[]{:T(128)} %bitcast.51, f32[]{:T(128)} %bitcast.50, f32[]{:T(128)} %bitcast.49, f32[]{:T(128)} %bitcast.48, f32[]{:T(128)} %bitcast.47, f32[]{:T(128)} %bitcast.46, f32[]{:T(128)} %bitcast.7), kind=kLoop, calls=%fused_computation.570 | loop fusion | flops 3670016 | bytes 3145756 | tf_op jit(solution)/shard_map/div | solution.py:82
  332.4 1.9 collective-permute-start.13
  334.3 5.5 %collective-permute-start.12 = (f32[15,16,256]{2,1,0:T(8,128)S(1)}, f32[15,16,256]{2,1,0:T(8,128)S(1)}, u32[]{:S(2)}, u32[]{:S(2)}) collective-permute-start(f32[15,16,256]{2,1,0:T(8,128)S(1)} %get-tuple-element.7), channel_id=1, source_target_pairs={{0,8},{8,16},{16,24},{24,32},{32,40},{40,48},{48,56},{56,64},{64,7... | collective-permute-start | bytes 737288 | tf_op jit(solution)/shard_map/ppermute | solution.py:19
  339.8 3.5 collective-permute-done.13
  343.3 0.9 collective-permute-done.12
  344.2 23.8 %fusion.59 = f32[64,16,256]{2,1,0:T(8,128)S(1)} fusion(f32[64,16,256]{2,1,0:T(8,128)S(1)} %fusion.346, f32[15,16,256]{2,1,0:T(8,128)S(1)} %collective-permute-done.13, f32[15,16,256]{2,1,0:T(8,128)S(1)} %collective-permute-done.12, f32[]{:T(128)} %bitcast.81, f32[]{:T(128)} %bitcast.80, f32[]{:T(128)} %bitcast.79, f32[]{:T(128)} %bitcast.78, f32[]{:T(128)} %bitcast.77, ...), kind=kLoop, calls=%fused_computation.283 | loop fusion | flops 23855104 | bytes 2588796 | tf_op jit(solution)/shard_map/add | solution.py:60
  368.0 3.7 collective-permute-start.15
  371.7 10.3 %collective-permute-start.14 = (f32[64,3,256]{2,1,0:T(4,128)S(1)}, f32[64,3,256]{2,1,0:T(4,128)S(1)}, u32[]{:S(2)}, u32[]{:S(2)}) collective-permute-start(f32[64,3,256]{2,1,0:T(4,128)S(1)} %get-tuple-element.5), channel_id=1, source_target_pairs={{0,1},{1,2},{2,3},{3,4},{4,5},{5,6},{6,7},{8,9},{9,10},{10,11},{11... | collective-permute-start | bytes 589832 | tf_op jit(solution)/shard_map/ppermute | solution.py:19
  382.1 13.1 %collective-permute-done.15 = f32[64,3,256]{2,1,0:T(4,128)S(1)} collective-permute-done((f32[64,3,256]{2,1,0:T(4,128)S(1)}, f32[64,3,256]{2,1,0:T(4,128)S(1)}, u32[]{:S(2)}, u32[]{:S(2)}) %collective-permute-start.15) | collective-permute-done | bytes 196640 | tf_op jit(solution)/shard_map/ppermute | solution.py:20
  395.2 17.0 %collective-permute-done.14 = f32[64,3,256]{2,1,0:T(4,128)S(1)} collective-permute-done((f32[64,3,256]{2,1,0:T(4,128)S(1)}, f32[64,3,256]{2,1,0:T(4,128)S(1)}, u32[]{:S(2)}, u32[]{:S(2)}) %collective-permute-start.14) | collective-permute-done | bytes 196640 | tf_op jit(solution)/shard_map/ppermute | solution.py:19
  412.2 5.7 %fusion.3 = f32[64,16,256]{2,1,0:T(8,128)S(1)} fusion(f32[64,16,256]{2,1,0:T(8,128)S(1)} %fusion.59, f32[64,3,256]{2,1,0:T(4,128)S(1)} %collective-permute-done.15, f32[64,3,256]{2,1,0:T(4,128)S(1)} %collective-permute-done.14, f32[]{:T(128)} %bitcast.87, f32[]{:T(128)} %bitcast.86, f32[]{:T(128)} %bitcast.85, f32[]{:T(128)} %bitcast.84, f32[]{:T(128)} %bitcast.83, ...), kind=kLoop, calls=%fused_computation.227 | loop fusion | flops 4980736 | bytes 2490396 | tf_op jit(solution)/shard_map/add | solution.py:60
  417.9 6.0 %fusion.358 = f32[64,16,256]{2,1,0:T(8,128)S(1)} fusion(f32[64,16,256]{2,1,0:T(8,128)S(1)} %fusion.3, f32[]{:T(128)} %bitcast.93, f32[]{:T(128)} %bitcast.92, f32[]{:T(128)} %bitcast.91, f32[]{:T(128)} %bitcast.90, f32[]{:T(128)} %bitcast.89, f32[]{:T(128)} %bitcast.88, f32[]{:T(128)} %bitcast.1), kind=kLoop, calls=%fused_computation.582 | loop fusion | flops 3407872 | bytes 2097180 | tf_op jit(solution)/shard_map/add | solution.py:60
  423.9 5.4 %all_to_all.22 = f32[2,32,16,256]{3,2,1,0:T(8,128)S(1)} all-to-all(f32[2,32,16,256]{3,2,1,0:T(8,128)S(1)} %bitcast.106), channel_id=1, replica_groups=mesh['view'=2,'gz'=32,'gy'=8] {'view'}, dimensions={0} | all-to-all | bytes 2097152 | tf_op jit(solution)/shard_map/all_to_all | solution.py:32
  429.6 4.6 %all_to_all.23 = f32[2,32,16,256]{3,2,1,0:T(8,128)S(1)} all-to-all(f32[2,32,16,256]{3,2,1,0:T(8,128)S(1)} %broadcast_in_dim.5), channel_id=1, replica_groups=mesh['view'=2,'gz'=32,'gy'=8] {'view'}, dimensions={0} | all-to-all | bytes 2097152 | tf_op jit(solution)/shard_map/all_to_all | solution.py:38
  434.2 1.0 copy.9
  (23 shorter events, 3.9 us)
Async XLA Ops:
  0.0 17.9 %copy-start = (f32[64,16,256]{2,1,0:T(8,128)S(1)}, f32[64,16,256]{2,1,0:T(8,128)}, u32[]{:S(2)}) copy-start(f32[64,16,256]{2,1,0:T(8,128)} %param.6) | copy-start | bytes 3145732
  1.2 16.7 %collective-permute-start = (f32[15,16,256]{2,1,0:T(8,128)S(1)}, f32[15,16,256]{2,1,0:T(8,128)S(1)}, u32[]{:S(2)}, u32[]{:S(2)}) collective-permute-start(f32[15,16,256]{2,1,0:T(8,128)S(1)} %get-tuple-element.21), channel_id=1, source_target_pairs={{0,8},{8,16},{16,24},{24,32},{32,40},{40,48},{48,56},{56,64},{64,7... | collective-permute-start | bytes 737288 | tf_op jit(solution)/shard_map/ppermute | solution.py:19
  4.4 13.8 %collective-permute-start.1 = (f32[15,16,256]{2,1,0:T(8,128)S(1)}, f32[15,16,256]{2,1,0:T(8,128)S(1)}, u32[]{:S(2)}, u32[]{:S(2)}) collective-permute-start(f32[15,16,256]{2,1,0:T(8,128)S(1)} %get-tuple-element.22), channel_id=1, source_target_pairs={{8,0},{16,8},{24,16},{32,24},{40,32},{48,40},{56,48},{64,56},{72,6... | collective-permute-start | bytes 737288 | tf_op jit(solution)/shard_map/ppermute | solution.py:20
  41.9 37.1 %collective-permute-start.3 = (f32[64,3,256]{2,1,0:T(4,128)S(1)}, f32[64,3,256]{2,1,0:T(4,128)S(1)}, u32[]{:S(2)}, u32[]{:S(2)}) collective-permute-start(f32[64,3,256]{2,1,0:T(4,128)S(1)} %get-tuple-element.18), channel_id=1, source_target_pairs={{1,0},{2,1},{3,2},{4,3},{5,4},{6,5},{7,6},{9,8},{10,9},{11,10},{12... | collective-permute-start | bytes 589832 | tf_op jit(solution)/shard_map/ppermute | solution.py:20
  56.7 44.8 %collective-permute-start.2 = (f32[64,3,256]{2,1,0:T(4,128)S(1)}, f32[64,3,256]{2,1,0:T(4,128)S(1)}, u32[]{:S(2)}, u32[]{:S(2)}) collective-permute-start(f32[64,3,256]{2,1,0:T(4,128)S(1)} %get-tuple-element.17), channel_id=1, source_target_pairs={{0,1},{1,2},{2,3},{3,4},{4,5},{5,6},{6,7},{8,9},{9,10},{10,11},{11... | collective-permute-start | bytes 589832 | tf_op jit(solution)/shard_map/ppermute | solution.py:19
  101.5 5.6 %copy-start.1 = (f32[1,64,16,256]{3,2,1,0:T(8,128)S(1)}, f32[1,64,16,256]{3,2,1,0:T(8,128)}, u32[]{:S(2)}) copy-start(f32[1,64,16,256]{3,2,1,0:T(8,128)} %param.5) | copy-start | bytes 3145732
  113.9 9.7 %collective-permute-start.5 = (f32[15,16,256]{2,1,0:T(8,128)}, f32[15,16,256]{2,1,0:T(8,128)S(1)}, u32[]{:S(2)}, u32[]{:S(2)}) collective-permute-start(f32[15,16,256]{2,1,0:T(8,128)} %get-tuple-element.16), channel_id=1, source_target_pairs={{8,0},{16,8},{24,16},{32,24},{40,32},{48,40},{56,48},{64,56},{72,6... | collective-permute-start | bytes 737288 | tf_op jit(solution)/shard_map/ppermute | solution.py:20
  116.7 8.0 %collective-permute-start.4 = (f32[15,16,256]{2,1,0:T(8,128)}, f32[15,16,256]{2,1,0:T(8,128)}, u32[]{:S(2)}, u32[]{:S(2)}) collective-permute-start(f32[15,16,256]{2,1,0:T(8,128)} %get-tuple-element.15), channel_id=1, source_target_pairs={{0,8},{8,16},{16,24},{24,32},{32,40},{40,48},{48,56},{56,64},{64,7... | collective-permute-start | bytes 737288 | tf_op jit(solution)/shard_map/ppermute | solution.py:19
  150.7 26.7 %collective-permute-start.7 = (f32[64,3,256]{2,1,0:T(4,128)S(1)}, f32[64,3,256]{2,1,0:T(4,128)S(1)}, u32[]{:S(2)}, u32[]{:S(2)}) collective-permute-start(f32[64,3,256]{2,1,0:T(4,128)S(1)} %get-tuple-element.14), channel_id=1, source_target_pairs={{1,0},{2,1},{3,2},{4,3},{5,4},{6,5},{7,6},{9,8},{10,9},{11,10},{12... | collective-permute-start | bytes 589832 | tf_op jit(solution)/shard_map/ppermute | solution.py:20
  162.9 41.5 %collective-permute-start.6 = (f32[64,3,256]{2,1,0:T(4,128)S(1)}, f32[64,3,256]{2,1,0:T(4,128)S(1)}, u32[]{:S(2)}, u32[]{:S(2)}) collective-permute-start(f32[64,3,256]{2,1,0:T(4,128)S(1)} %get-tuple-element.13), channel_id=1, source_target_pairs={{0,1},{1,2},{2,3},{3,4},{4,5},{5,6},{6,7},{8,9},{9,10},{10,11},{11... | collective-permute-start | bytes 589832 | tf_op jit(solution)/shard_map/ppermute | solution.py:19
  227.5 11.2 %collective-permute-start.9 = (f32[15,16,256]{2,1,0:T(8,128)S(1)}, f32[15,16,256]{2,1,0:T(8,128)S(1)}, u32[]{:S(2)}, u32[]{:S(2)}) collective-permute-start(f32[15,16,256]{2,1,0:T(8,128)S(1)} %get-tuple-element.12), channel_id=1, source_target_pairs={{8,0},{16,8},{24,16},{32,24},{40,32},{48,40},{56,48},{64,56},{72,6... | collective-permute-start | bytes 737288 | tf_op jit(solution)/shard_map/ppermute | solution.py:20
  229.5 10.1 %collective-permute-start.8 = (f32[15,16,256]{2,1,0:T(8,128)S(1)}, f32[15,16,256]{2,1,0:T(8,128)S(1)}, u32[]{:S(2)}, u32[]{:S(2)}) collective-permute-start(f32[15,16,256]{2,1,0:T(8,128)S(1)} %get-tuple-element.11), channel_id=1, source_target_pairs={{0,8},{8,16},{16,24},{24,32},{32,40},{40,48},{48,56},{56,64},{64,7... | collective-permute-start | bytes 737288 | tf_op jit(solution)/shard_map/ppermute | solution.py:19
  263.4 24.9 %collective-permute-start.11 = (f32[64,3,256]{2,1,0:T(4,128)S(1)}, f32[64,3,256]{2,1,0:T(4,128)S(1)}, u32[]{:S(2)}, u32[]{:S(2)}) collective-permute-start(f32[64,3,256]{2,1,0:T(4,128)S(1)} %get-tuple-element.10), channel_id=1, source_target_pairs={{1,0},{2,1},{3,2},{4,3},{5,4},{6,5},{7,6},{9,8},{10,9},{11,10},{12... | collective-permute-start | bytes 589832 | tf_op jit(solution)/shard_map/ppermute | solution.py:20
  274.2 46.7 %collective-permute-start.10 = (f32[64,3,256]{2,1,0:T(4,128)S(1)}, f32[64,3,256]{2,1,0:T(4,128)S(1)}, u32[]{:S(2)}, u32[]{:S(2)}) collective-permute-start(f32[64,3,256]{2,1,0:T(4,128)S(1)} %get-tuple-element.9), channel_id=1, source_target_pairs={{0,1},{1,2},{2,3},{3,4},{4,5},{5,6},{6,7},{8,9},{9,10},{10,11},{11... | collective-permute-start | bytes 589832 | tf_op jit(solution)/shard_map/ppermute | solution.py:19
  332.4 10.9 %collective-permute-start.13 = (f32[15,16,256]{2,1,0:T(8,128)S(1)}, f32[15,16,256]{2,1,0:T(8,128)S(1)}, u32[]{:S(2)}, u32[]{:S(2)}) collective-permute-start(f32[15,16,256]{2,1,0:T(8,128)S(1)} %get-tuple-element.8), channel_id=1, source_target_pairs={{8,0},{16,8},{24,16},{32,24},{40,32},{48,40},{56,48},{64,56},{72,6... | collective-permute-start | bytes 737288 | tf_op jit(solution)/shard_map/ppermute | solution.py:20
  334.3 9.8 %collective-permute-start.12 = (f32[15,16,256]{2,1,0:T(8,128)S(1)}, f32[15,16,256]{2,1,0:T(8,128)S(1)}, u32[]{:S(2)}, u32[]{:S(2)}) collective-permute-start(f32[15,16,256]{2,1,0:T(8,128)S(1)} %get-tuple-element.7), channel_id=1, source_target_pairs={{0,8},{8,16},{16,24},{24,32},{32,40},{40,48},{48,56},{56,64},{64,7... | collective-permute-start | bytes 737288 | tf_op jit(solution)/shard_map/ppermute | solution.py:19
  368.0 27.1 %collective-permute-start.15 = (f32[64,3,256]{2,1,0:T(4,128)S(1)}, f32[64,3,256]{2,1,0:T(4,128)S(1)}, u32[]{:S(2)}, u32[]{:S(2)}) collective-permute-start(f32[64,3,256]{2,1,0:T(4,128)S(1)} %get-tuple-element.6), channel_id=1, source_target_pairs={{1,0},{2,1},{3,2},{4,3},{5,4},{6,5},{7,6},{9,8},{10,9},{11,10},{12... | collective-permute-start | bytes 589832 | tf_op jit(solution)/shard_map/ppermute | solution.py:20
  371.7 40.5 %collective-permute-start.14 = (f32[64,3,256]{2,1,0:T(4,128)S(1)}, f32[64,3,256]{2,1,0:T(4,128)S(1)}, u32[]{:S(2)}, u32[]{:S(2)}) collective-permute-start(f32[64,3,256]{2,1,0:T(4,128)S(1)} %get-tuple-element.5), channel_id=1, source_target_pairs={{0,1},{1,2},{2,3},{3,4},{4,5},{5,6},{6,7},{8,9},{9,10},{10,11},{11... | collective-permute-start | bytes 589832 | tf_op jit(solution)/shard_map/ppermute | solution.py:19
where the time goes:
time: 438 us; the launch traced here: 435 us
  waiting for transfers between devices  164 us (37%)
  other arithmetic  153 us (35%)
  starting transfers between devices  86.4 us (20%)
  blocking collectives  19.3 us (4%)
  local copies, waits for them, and re-layouts  11.7 us (3%)
    add x10, other arithmetic, correlate(): total + weights[offset] * lax.slice_in_dim(padded, offset, offset + lengt...  131 us
    ppermute x8, waiting for transfers between devices, padded_2(): before = lax.ppermute(last, axis, up)  102 us
    ppermute x8, waiting for transfers between devices, padded_2(): after = lax.ppermute(first, axis, down)  62.2 us
    ppermute x8, starting transfers between devices, padded_2(): after = lax.ppermute(first, axis, down)  50.2 us
    ppermute x8, starting transfers between devices, padded_2(): before = lax.ppermute(last, axis, up)  36.3 us
    div x2, other arithmetic, on_device(): quotient = recorded / blurred  11.9 us
    all_to_all x2, blocking collectives, sent_and_summed(): lax.all_to_all(pieces, axis, split_axis=0, concat_axis=0, tiled=True)  10.1 us
    all_to_all x2, blocking collectives, copy_for_each(): lax.all_to_all(jnp.broadcast_to(x[None], (peers, *x.shape)), axis, 0, 0,...  9.15 us
  transfers between devices with their start and end apart: 16, of which 14 were waited for; matrix products, arithmetic and copies ran while one was open for 4% of the time, Pallas kernels for 0%

commit v1 on v0

v1 whole, which is shorter than its diff:
```python
import jax
import jax.numpy as jnp
from jax import lax
from jax.experimental import pallas as pl
from jax.experimental.pallas import tpu as pltpu
from jax.sharding import PartitionSpec as P

F32 = jnp.float32
BF16 = jnp.bfloat16
NX = 256
LIMIT = 56 * 1024 * 1024
VM = pl.BlockSpec(memory_space=pltpu.VMEM)
SM = pl.BlockSpec(memory_space=pltpu.SMEM)


def call(body, outs, *args, smem=1, flops=0, scratch=()):
    size = sum(a.size * a.dtype.itemsize for a in args)
    size += sum(4 * o.size for o in outs)
    return pl.pallas_call(
        body,
        out_shape=outs,
        in_specs=[SM] * smem + [VM] * (len(args) - smem),
        out_specs=[VM] * len(outs),
        scratch_shapes=list(scratch),
        compiler_params=pltpu.CompilerParams(vmem_limit_bytes=LIMIT),
        cost_estimate=pl.CostEstimate(flops=flops, bytes_accessed=size, transcendentals=0),
    )(*args)


def f32(*shape):
    return jax.ShapeDtypeStruct(shape, F32)


def b16(*shape):
    return jax.ShapeDtypeStruct(shape, BF16)


def parts(x):
    high = x.astype(BF16)
    return high, (x - high.astype(F32)).astype(BF16)


def dot(a, b):
    return jnp.dot(a, b, preferred_element_type=F32)


def rows_of(ref, half):
    return jnp.swapaxes(ref[:, 8 * half : 8 * half + 8, :], 0, 1)


def by_core(meta, body):
    for core in range(2):
        pl.when(meta[0] == core)(lambda core=core: body(core, lambda r: r % 8 if core == 0 else 7 - r % 8))


def far_body(meta, start, out_a, out_b):
    def body(core, at):
        rows = rows_of(start, core)
        for j in range(3):
            out_a[j] = rows[at(j), :32]
            out_b[j] = rows[at(j), 32:]

    by_core(meta, body)


def start_body(meta, start, e_a, e_b):
    def body(core, at):
        rows = (rows_of(start, core), rows_of(start, 1 - core))
        for j in range(11):
            e_a[j] = rows[j // 8][at(j), :32]
            e_b[j] = rows[j // 8][at(j), 32:]

    by_core(meta, body)


def observed_body(meta, observed, sz, sy, sx, mine, send):
    def body(core, at):
        rows, others = rows_of(observed, core), rows_of(observed, 1 - core)
        for j in range(8):
            mine[j] = rows[at(j)]
            send[64 * j : 64 * j + 64] = others[at(15 - j)]

    by_core(meta, body)
    send[512:520] = jnp.zeros((8, NX), F32)
    send[512:513, 0:31] = sz[...]
    send[513:514, 0:7] = sy[...]
    send[514:515, 0:7] = sx[...]


def edges_body(mine, recv, low, high):
    for j in range(8):
        low[j] = mine[j, 0:16]
        high[j] = mine[j, 48:64]
        low[8 + j] = recv[64 * j : 64 * j + 16]
        high[8 + j] = recv[64 * j + 48 : 64 * j + 64]


def weights_body(meta, own, other, zf, zb, xf, xb, yw):
    def band(shape, row, taps, place):
        d = lax.broadcasted_iota(jnp.int32, shape, 1) - lax.broadcasted_iota(jnp.int32, shape, 0)
        total = jnp.zeros(shape, F32)
        for t in range(taps):
            total = jnp.where(d == place(t), row[:, t : t + 1], total)
        return total

    for v, ref in enumerate((own, other)):
        w = ref[512:520]
        sums = jnp.sum(w, axis=1, keepdims=True)
        w = w / sums_or_one(sums)
        wz, wy, wx = w[0:1], w[1:2], w[2:3]
        high, low = parts(band((96, 128), wz, 31, lambda t: t + 1))
        zf[192 * v : 192 * v + 96, 0:128] = high
        zf[192 * v : 192 * v + 96, 128:256] = high
        zf[192 * v + 96 : 192 * v + 192, 0:128] = low
        zf[192 * v + 96 : 192 * v + 192, 128:256] = jnp.zeros((96, 128), BF16)
        high, low = parts(band((64, 96), wz, 31, lambda t: 31 - t))
        zb[v, 0:64] = jnp.concatenate([high, high], axis=1)
        zb[v, 64:128] = jnp.concatenate([low, jnp.zeros((64, 96), BF16)], axis=1)
        high, low = parts(band((256, 256), wx, 7, lambda t: 3 - t))
        xf[v, 0] = high
        xf[v, 1] = low
        high, low = parts(band((256, 256), wx, 7, lambda t: t - 3))
        xb[v, 0] = high
        xb[v, 1] = low
        for core in range(2):

            @pl.when(meta[0] == core)
            def _(core=core, v=v, wy=wy):
                for t in range(7):
                    s = t if core == 0 else 6 - t
                    yw[8 * v + t : 8 * v + t + 1, :] = jnp.broadcast_to(wy[:, s : s + 1], (1, NX))

        yw[8 * v + 7 : 8 * v + 8, :] = jnp.zeros((1, NX), F32)


def sums_or_one(sums):
    rows = lax.broadcasted_iota(jnp.int32, sums.shape, 0)
    return jnp.where(rows < 3, sums, 1.0)


def blur_z(zf, low, a, b, high):
    highs, lows = zip(*[parts(x) for x in (low, a, b, high)])
    both = dot(zf[...], jnp.concatenate(highs + lows, axis=0))
    return [both[192 * v : 192 * v + 96] + both[192 * v + 96 : 192 * v + 192] for v in range(2)]


def blur_x(x, weight, v):
    high, low = parts(x)
    return dot(high, weight[v, 0]) + dot(low, weight[v, 0]) + dot(high, weight[v, 1])


def row_result(meta, rows, recorded, yw, xf, xb, zb, v):
    total = yw[8 * v : 8 * v + 1] * rows[0]
    for t in range(1, 7):
        total = total + yw[8 * v + t : 8 * v + t + 1] * rows[t]
    blurred = blur_x(total, xf, v)
    at = lax.broadcasted_iota(jnp.int32, blurred.shape, 0)
    inside = (at >= meta[1]) & (at < meta[2])
    quotient = recorded / jnp.where(inside, blurred, 1.0)
    high, low = parts(quotient)
    both = dot(zb[v], jnp.concatenate([high, low], axis=0))
    return blur_x(both[0:64] + both[64:128], xb, v)


def recorded_row(mine, recv, o_low, o_high, j, v):
    middle = mine[j] if v == 0 else recv[64 * j : 64 * j + 64]
    return jnp.concatenate([o_low[8 * v + j], middle, o_high[8 * v + j]], axis=0)


def spread_back(yw, terms, row, planes=slice(0, 64)):
    total = None
    for v in range(2):
        for t in range(7):
            j = row + t - 3
            if 0 <= j <= 7:
                term = yw[8 * v + 6 - t : 8 * v + 7 - t] * terms(v, j)[planes]
                total = term if total is None else total + term
    return total


def early1_body(meta, e_a, e_b, e_low, e_high, mine, recv, o_low, o_high, zf, zb, xf, xb, yw, ze, bx, buf):
    for r in range(11):
        for v, x in enumerate(blur_z(zf, e_low[r], e_a[r], e_b[r], e_high[r])):
            buf[v, r] = x
            if r < 6:
                ze[v, r] = x
    for j in range(3, 8):
        for v in range(2):
            rec = recorded_row(mine, recv, o_low, o_high, j, v)
            bx[v, j - 3] = row_result(meta, [buf[v, j - 3 + t] for t in range(7)], rec, yw, xf, xb, zb, v)


def late1_body(meta, f_a, f_b, f_low, f_high, ze, bx, mine, recv, o_low, o_high, zf, zb, xf, xb, yw,
               c_far_a, c_far_b, c_mid, c_part, buf, new):
    for j in range(3):
        for v, x in enumerate(blur_z(zf, f_low[j], f_a[j], f_b[j], f_high[j])):
            buf[v, 2 - j] = x
    for j in range(3):
        for v in range(2):
            rows = [buf[v, j + t] if j + t < 3 else ze[v, j + t - 3] for t in range(7)]
            rec = recorded_row(mine, recv, o_low, o_high, j, v)
            new[v, j] = row_result(meta, rows, rec, yw, xf, xb, zb, v)

    def terms(v, j):
        return new[v, j] if j < 3 else bx[v, j - 3]

    for row in range(-3, 11):
        total = spread_back(yw, terms, row)
        if row < 3:
            c_far_a[row + 3] = total[:32]
            c_far_b[row + 3] = total[32:]
        elif row < 5:
            c_mid[row - 3] = total
        else:
            c_part[row - 5] = total


def update_mid_body(e_a, e_b, c_mid, c_part, got, out_a, out_b):
    for r in range(3, 11):
        c = c_mid[r - 3] if r < 5 else c_part[r - 5] + got[10 - r]
        out_a[r - 3] = e_a[r] * (0.5 * c[:32])
        out_b[r - 3] = e_b[r] * (0.5 * c[32:])


def update_far_body(far, e, c, got, out):
    for r in range(-3, 3):
        old = far[-1 - r] if r < 0 else e[r]
        out[r + 3] = old * (0.5 * (c[r + 3] + got[2 - r]))


def early2_body(meta, e_a, e_b, e_low, e_high, mine, recv, o_low, o_high, zf, zb, xf, xb, yw, ze, bx, buf):
    for r in range(8):
        for v, x in enumerate(blur_z(zf, e_low[r], e_a[r], e_b[r], e_high[r])):
            buf[v, r] = x
            if r < 6:
                ze[v, r] = x
    for j in (6, 7):
        for v in range(2):
            rec = recorded_row(mine, recv, o_low, o_high, j, v)
            bx[v, j - 6] = row_result(meta, [buf[v, j - 6 + t] for t in range(7)], rec, yw, xf, xb, zb, v)


def late2_body(meta, f_a, f_b, f_low, f_high, ze, mine, recv, o_low, o_high, zf, zb, xf, xb, yw,
               c_far, zn, bx):
    for r in range(6):
        for v, x in enumerate(blur_z(zf, f_low[r], f_a[r], f_b[r], f_high[r])):
            zn[v, r] = x
    for j in range(3):
        for v in range(2):
            rows = [zn[v, j + t] if j + t < 6 else ze[v, j + t - 6] for t in range(7)]
            rec = recorded_row(mine, recv, o_low, o_high, j, v)
            bx[v, j] = row_result(meta, rows, rec, yw, xf, xb, zb, v)
    for k in range(3):
        c_far[k] = spread_back(yw, lambda v, j: bx[v, j] if j < 3 else None, -1 - k)


def rest2_body(meta, zn, ze, bx0, bx6, mine, recv, o_low, o_high, zb, xf, xb, yw, c_own, c_part, new):
    for j in range(3, 6):
        for v in range(2):
            rows = [zn[v, j + t] if j + t < 6 else ze[v, j + t - 6] for t in range(7)]
            rec = recorded_row(mine, recv, o_low, o_high, j, v)
            new[v, j - 3] = row_result(meta, rows, rec, yw, xf, xb, zb, v)

    def terms(v, j):
        return bx0[v, j] if j < 3 else new[v, j - 3] if j < 6 else bx6[v, j - 6]

    for row in range(11):
        total = spread_back(yw, terms, row)
        if row < 8:
            c_own[row] = total
        else:
            c_part[row - 8] = total


def final_mid_body(e_a, e_b, c_own, got, out):
    for r in range(3, 8):
        c = c_own[r] if r < 5 else c_own[r] + got[7 - r]
        out[r - 3, :32] = e_a[r - 3] * (0.5 * c[:32])
        out[r - 3, 32:] = e_b[r - 3] * (0.5 * c[32:])


def final_far_body(f_a, f_b, c_own, got, out):
    for r in range(3):
        c = c_own[r] + got[r]
        out[r, :32] = f_a[r + 3] * (0.5 * c[:32])
        out[r, 32:] = f_b[r + 3] * (0.5 * c[32:])


def output_body(meta, far, mid, other_far, other_mid, out):
    def body(core, at):
        rows, others = [None] * 8, [None] * 8
        for r in range(8):
            rows[at(r)] = far[r] if r < 3 else mid[r - 3]
            others[at(15 - r)] = other_far[r] if r < 3 else other_mid[r - 3]
        for half, block in ((core, rows), (1 - core, others)):
            out[:, 8 * half : 8 * half + 8, :] = jnp.swapaxes(jnp.stack(block), 0, 1)

    by_core(meta, body)


def on_device(observed, start, spread_z, spread_y, spread_x):
    gy, gz = lax.axis_size("gy"), lax.axis_size("gz")
    across = [(gy + g, g + 1) for g in range(gy - 1)]
    across += [(b, a) for a, b in across]
    up = [(i, i + 1) for i in range(gz - 1)]
    down = [(j, i) for i, j in up]

    def far(x):
        return lax.ppermute(x, ("view", "gy"), across)

    def partner(x):
        return lax.ppermute(x, "view", [(0, 1), (1, 0)])

    def along_z(first, last):
        return lax.ppermute(last, "gz", up), lax.ppermute(first, "gz", down)

    at = lax.axis_index("gz")
    meta = jnp.stack(
        [lax.axis_index("view"), jnp.where(at == 0, 16, 0), jnp.where(at == gz - 1, 80, 96)]
    ).astype(jnp.int32)
    recorded = observed[0]

    send_a, send_b = call(far_body, [f32(3, 32, NX)] * 2, meta, start)
    f_a, f_b = far(send_a), far(send_b)
    mine, send = call(observed_body, [f32(8, 64, NX), f32(520, NX)], meta, recorded, spread_z, spread_y, spread_x)
    recv = partner(send)
    e_a, e_b = call(start_body, [f32(11, 32, NX)] * 2, meta, start)
    e_low, e_high = along_z(e_a, e_b)
    o_first, o_last = call(edges_body, [f32(16, 16, NX)] * 2, mine, recv, smem=0)
    o_low, o_high = along_z(o_first, o_last)
    zf, zb, xf, xb, yw = call(
        weights_body,
        [b16(384, 256), b16(2, 128, 192), b16(2, 2, 256, 256), b16(2, 2, 256, 256), f32(16, NX)],
        meta, send, recv,
    )
    obs = (mine, recv, o_low, o_high)
    f_low, f_high = along_z(f_a, f_b)

    ze, bx = call(
        early1_body, [f32(2, 6, 96, NX), f32(2, 5, 64, NX)],
        meta, e_a, e_b, e_low, e_high, *obs, zf, zb, xf, xb, yw,
        scratch=[pltpu.VMEM((2, 11, 96, NX), F32)],
    )
    c_far_a, c_far_b, c_mid, c_part = call(
        late1_body, [f32(6, 32, NX), f32(6, 32, NX), f32(2, 64, NX), f32(6, 64, NX)],
        meta, f_a, f_b, f_low, f_high, ze, bx, *obs, zf, zb, xf, xb, yw,
        scratch=[pltpu.VMEM((2, 3, 96, NX), F32), pltpu.VMEM((2, 3, 64, NX), F32)],
    )
    got_a, got_b = far(c_far_a), far(c_far_b)
    got = partner(c_part)
    m_a, m_b = call(update_mid_body, [f32(8, 32, NX)] * 2, e_a, e_b, c_mid, c_part, got, smem=0)
    m_low, m_high = along_z(m_a, m_b)
    ze, bx6 = call(
        early2_body, [f32(2, 6, 96, NX), f32(2, 2, 64, NX)],
        meta, m_a, m_b, m_low, m_high, *obs, zf, zb, xf, xb, yw,
        scratch=[pltpu.VMEM((2, 8, 96, NX), F32)],
    )
    (n_a,) = call(update_far_body, [f32(6, 32, NX)], f_a, e_a, c_far_a, got_a, smem=0)
    n_high = lax.ppermute(n_a, "gz", down)
    (n_b,) = call(update_far_body, [f32(6, 32, NX)], f_b, e_b, c_far_b, got_b, smem=0)
    n_low = lax.ppermute(n_b, "gz", up)
    c_far, zn, bx0 = call(
        late2_body, [f32(3, 64, NX), f32(2, 6, 96, NX), f32(2, 3, 64, NX)],
        meta, n_a, n_b, n_low, n_high, ze, *obs, zf, zb, xf, xb, yw,
    )
    got_far = far(c_far)
    c_own, c_part = call(
        rest2_body, [f32(8, 64, NX), f32(3, 64, NX)],
        meta, zn, ze, bx0, bx6, *obs, zb, xf, xb, yw,
        scratch=[pltpu.VMEM((2, 3, 64, NX), F32)],
    )
    got_part = partner(c_part)
    (mid,) = call(final_mid_body, [f32(5, 64, NX)], m_a, m_b, c_own, got_part, smem=0)
    other_mid = partner(mid)
    (last,) = call(final_far_body, [f32(3, 64, NX)], n_a, n_b, c_own, got_far, smem=0)
    other_last = partner(last)
    (out,) = call(output_body, [f32(64, 16, NX)], meta, last, mid, other_last, other_mid)
    return out


def solution(mesh):
    return jax.shard_map(
        on_device,
        mesh=mesh,
        in_specs=(
            P("view", "gz", "gy", None),
            P("gz", "gy", None),
            P("view", None),
            P("view", None),
            P("view", None),
        ),
        out_specs=P("gz", "gy", None),
        check_vma=False,
    )
```

time: 438 us -> 204 us (0.47)
  the two profiles are of different devices: /device:TPU:63 before, /device:TPU:37 now
where the time goes in v1:
time: 204 us; the launch traced here: 203 us
  starting transfers between devices  86.3 us (42%)
  waiting for transfers between devices  53.2 us (26%)
  Pallas kernels  52.9 us (26%)
  local copies, waits for them, and re-layouts  9.27 us (5%)
    pallas_call x16, Pallas kernels, call(): pl.pallas_call(body, out_shape=outs, in_specs=[SM] * smem + [VM] * (len(a...  52.9 us
    ppermute x5, waiting for transfers between devices, far(): return lax.ppermute(x, ('view', 'gy'), across)  51.5 us
    ppermute x5, starting transfers between devices, far(): return lax.ppermute(x, ('view', 'gy'), across)  41.1 us
    ppermute x8, starting transfers between devices, along_z(): return (lax.ppermute(last, 'gz', up), lax.ppermute(first, 'gz', down))  24.7 us
    ppermute x5, starting transfers between devices, partner(): return lax.ppermute(x, 'view', [(0, 1), (1, 0)])  15 us
    unnamed x42, local copies, waits for them, and re-layouts  9.27 us
  transfers between devices with their start and end apart: 20, of which 6 were waited for; matrix products, arithmetic and copies ran while one was open for 0% of the time, Pallas kernels for 15%

profile of v1, /device:TPU:37, one launch (start us, length us, event | category | flops | bytes accessed | tf_op | source)
XLA Modules:
  0.0 202.7 jit_solution(6629704095428790969)
XLA Ops:
  0.0 0.7 pad_add_fusion.meta
  0.7 2.5 %shard_map.57 = (f32[8,64,256]{2,1,0:T(8,128)}, f32[520,256]{1,0:T(8,128)}) custom-call(s32[3]{0:T(128)} %pad_add_fusion.meta, f32[64,16,256]{2,1,0:T(8,128)} %bitcast.4, f32[1,31]{1,0:T(1,128)} %sz.1, f32[1,7]{1,0:T(1,128)} %sy.1, f32[1,7]{1,0:T(1,128)} %sx.1), custom_call_target="tpu_custom_call" | custom-call | bytes 2105536 | tf_op jit(solution)/shard_map/pallas_call | solution.py:19
  3.1 2.6 %collective-permute-start.6 = (f32[520,256]{1,0:T(8,128)}, f32[520,256]{1,0:T(8,128)S(1)}, u32[]{:S(2)}, u32[]{:S(2)}) collective-permute-start(f32[520,256]{1,0:T(8,128)} %get-tuple-element.38.own), channel_id=1, source_target_pairs={{0,256},{256,0},{1,257},{257,1},{2,258},{258,2},{3,259},{259,3},{4... | collective-permute-start | bytes 1597448 | tf_op jit(solution)/shard_map/ppermute | solution.py:312
  5.7 2.3 %shard_map.56 = (f32[11,32,256]{2,1,0:T(8,128)}, f32[11,32,256]{2,1,0:T(8,128)}) custom-call(s32[3]{0:T(128)} %pad_add_fusion.meta, f32[64,16,256]{2,1,0:T(8,128)} %start.3), custom_call_target="tpu_custom_call" | custom-call | bytes 1769484 | tf_op jit(solution)/shard_map/pallas_call | solution.py:19
  8.0 4.2 %collective-permute-start.5 = (f32[11,32,256]{2,1,0:T(8,128)}, f32[11,32,256]{2,1,0:T(8,128)S(1)}, u32[]{:S(2)}, u32[]{:S(2)}) collective-permute-start(f32[11,32,256]{2,1,0:T(8,128)} %get-tuple-element.34.e_a.e), channel_id=1, source_target_pairs={{8,0},{16,8},{24,16},{32,24},{40,32},{48,40},{56,48},{64,56},{72,6... | collective-permute-start | bytes 1081352 | tf_op jit(solution)/shard_map/ppermute | solution.py:315
  12.2 1.9 collective-permute-start.4
  14.1 2.0 shard_map.55
  16.1 15.6 %collective-permute-start = (f32[3,32,256]{2,1,0:T(8,128)}, f32[3,32,256]{2,1,0:T(8,128)S(1)}, u32[]{:S(2)}, u32[]{:S(2)}) collective-permute-start(f32[3,32,256]{2,1,0:T(8,128)} %get-tuple-element.33), channel_id=1, source_target_pairs={{256,1},{257,2},{258,3},{259,4},{260,5},{261,6},{262,7},{1,256},{2... | collective-permute-start | bytes 294920 | tf_op jit(solution)/shard_map/ppermute | solution.py:309
  31.7 0.8 copy-done
  32.5 2.0 %shard_map.58 = (f32[16,16,256]{2,1,0:T(8,128)}, f32[16,16,256]{2,1,0:T(8,128)}) custom-call(f32[8,64,256]{2,1,0:T(8,128)} %get-tuple-element.37.mine, f32[520,256]{1,0:T(8,128)} %copy-done), custom_call_target="tpu_custom_call" | custom-call | bytes 1581056 | tf_op jit(solution)/shard_map/pallas_call | solution.py:19
  34.5 1.9 collective-permute-start.7
  36.4 5.8 %collective-permute-start.8 = (f32[16,16,256]{2,1,0:T(8,128)}, f32[16,16,256]{2,1,0:T(8,128)S(1)}, u32[]{:S(2)}, u32[]{:S(2)}) collective-permute-start(f32[16,16,256]{2,1,0:T(8,128)} %get-tuple-element.40), channel_id=1, source_target_pairs={{8,0},{16,8},{24,16},{32,24},{40,32},{48,40},{56,48},{64,56},{72,6... | collective-permute-start | bytes 786440 | tf_op jit(solution)/shard_map/ppermute | solution.py:315
  42.2 0.8 collective-permute-done.f_a.far
  43.0 5.3 %collective-permute-start.1 = (f32[3,32,256]{2,1,0:T(8,128)}, f32[3,32,256]{2,1,0:T(8,128)S(1)}, u32[]{:S(2)}, u32[]{:S(2)}) collective-permute-start(f32[3,32,256]{2,1,0:T(8,128)} %get-tuple-element.35), channel_id=1, source_target_pairs={{256,1},{257,2},{258,3},{259,4},{260,5},{261,6},{262,7},{1,256},{2... | collective-permute-start | bytes 294920 | tf_op jit(solution)/shard_map/ppermute | solution.py:309
  48.4 17.0 %collective-permute-done.1.f_b.far = f32[3,32,256]{2,1,0:T(8,128)S(1)} collective-permute-done((f32[3,32,256]{2,1,0:T(8,128)}, f32[3,32,256]{2,1,0:T(8,128)S(1)}, u32[]{:S(2)}, u32[]{:S(2)}) %collective-permute-start.1) | collective-permute-done | bytes 98336 | tf_op jit(solution)/shard_map/ppermute | solution.py:309
  65.3 1.9 collective-permute-start.3
  67.2 0.0 collective-permute-done.5.e_high
  67.3 3.4 %collective-permute-start.2 = (f32[3,32,256]{2,1,0:T(8,128)S(1)}, f32[3,32,256]{2,1,0:T(8,128)S(1)}, u32[]{:S(2)}, u32[]{:S(2)}) collective-permute-start(f32[3,32,256]{2,1,0:T(8,128)S(1)} %collective-permute-done.1.f_b.far), channel_id=1, source_target_pairs={{0,8},{8,16},{16,24},{24,32},{32,40},{40,48},{48,56},{56,64},{64,7... | collective-permute-start | bytes 294920 | tf_op jit(solution)/shard_map/ppermute | solution.py:315
  70.6 3.5 %shard_map.59 = (bf16[384,256]{1,0:T(8,128)(2,1)}, bf16[2,128,192]{2,1,0:T(8,128)(2,1)}, bf16[2,2,256,256]{3,2,1,0:T(8,128)(2,1)}, bf16[2,2,256,256]{3,2,1,0:T(8,128)(2,1)}, f32[16,256]{1,0:T(8,128)}) custom-call(s32[3]{0:T(128)} %pad_add_fusion.meta, f32[520,256]{1,0:T(8,128)} %get-tuple-element.38.own, f32[520,256]{1,0:T(8,128)} %copy-done), custom_call_target="tpu_custom_call" | custom-call | bytes 3768332 | tf_op jit(solution)/shard_map/pallas_call | solution.py:19
  74.2 0.0 collective-permute-done.7.o_low
  74.2 0.7 copy-done.7
  74.9 0.1 copy-done.1
  75.1 0.1 copy-done.2
  75.2 6.7 %shard_map.60 = (f32[2,6,96,256]{3,2,1,0:T(8,128)}, f32[2,5,64,256]{3,2,1,0:T(8,128)}) custom-call(s32[3]{0:T(128)} %pad_add_fusion.meta, f32[11,32,256]{2,1,0:T(8,128)} %get-tuple-element.34.e_a.e, f32[11,32,256]{2,1,0:T(8,128)} %get-tuple-element.36.e_b.e, f32[11,32,256]{2,1,0:T(8,128)} %copy-done.7, f32[11,32,256]{2,1,0:T(8,128)} %copy-done.6, ...), custom_call_target="tpu_custom_call" | custom-call | bytes 6217740 | tf_op jit(solution)/shard_map/pallas_call | solution.py:19
  81.9 0.6 copy-done.18
  82.5 0.0 copy-done.19
  82.6 5.8 %shard_map.61 = (f32[6,32,256]{2,1,0:T(8,128)}, f32[6,32,256]{2,1,0:T(8,128)}, f32[2,64,256]{2,1,0:T(8,128)}, f32[6,64,256]{2,1,0:T(8,128)}) custom-call(s32[3]{0:T(128)} %pad_add_fusion.meta, f32[3,32,256]{2,1,0:T(8,128)} %copy-done.4, f32[3,32,256]{2,1,0:T(8,128)} %copy-done.5, f32[3,32,256]{2,1,0:T(8,128)} %copy-done.19, f32[3,32,256]{2,1,0:T(8,128)} %copy-done.18, ...), custom_call_target="tpu_custom_call" | custom-call | bytes 6086668 | tf_op jit(solution)/shard_map/pallas_call | solution.py:19
  88.4 3.0 %collective-permute-start.13 = (f32[6,64,256]{2,1,0:T(8,128)}, f32[6,64,256]{2,1,0:T(8,128)S(1)}, u32[]{:S(2)}, u32[]{:S(2)}) collective-permute-start(f32[6,64,256]{2,1,0:T(8,128)} %get-tuple-element.51.c_part), channel_id=1, source_target_pairs={{0,256},{256,0},{1,257},{257,1},{2,258},{258,2},{3,259},{259,3},{4... | collective-permute-start | bytes 1179656 | tf_op jit(solution)/shard_map/ppermute | solution.py:312
  91.4 7.2 %collective-permute-start.9 = (f32[6,32,256]{2,1,0:T(8,128)}, f32[6,32,256]{2,1,0:T(8,128)S(1)}, u32[]{:S(2)}, u32[]{:S(2)}) collective-permute-start(f32[6,32,256]{2,1,0:T(8,128)} %get-tuple-element.48.c), channel_id=1, source_target_pairs={{256,1},{257,2},{258,3},{259,4},{260,5},{261,6},{262,7},{1,256},{2... | collective-permute-start | bytes 589832 | tf_op jit(solution)/shard_map/ppermute | solution.py:309
  98.6 7.1 %collective-permute-start.10 = (f32[6,32,256]{2,1,0:T(8,128)}, f32[6,32,256]{2,1,0:T(8,128)S(1)}, u32[]{:S(2)}, u32[]{:S(2)}) collective-permute-start(f32[6,32,256]{2,1,0:T(8,128)} %get-tuple-element.49.c), channel_id=1, source_target_pairs={{256,1},{257,2},{258,3},{259,4},{260,5},{261,6},{262,7},{1,256},{2... | collective-permute-start | bytes 589832 | tf_op jit(solution)/shard_map/ppermute | solution.py:309
  105.7 0.0 copy-start.3
  105.7 0.7 copy-done.3
  106.5 2.3 %shard_map.64 = (f32[8,32,256]{2,1,0:T(8,128)}, f32[8,32,256]{2,1,0:T(8,128)}) custom-call(f32[11,32,256]{2,1,0:T(8,128)} %get-tuple-element.34.e_a.e, f32[11,32,256]{2,1,0:T(8,128)} %get-tuple-element.36.e_b.e, f32[2,64,256]{2,1,0:T(8,128)} %get-tuple-element.50.c_mid, f32[6,64,256]{2,1,0:T(8,128)} %get-tuple-element.51.c_part, f32[6,64,256]{2,1,0:T(8,128)} %copy-done.3), custom_call_target="tpu_custom_call" | custom-call | bytes 2162688 | tf_op jit(solution)/shard_map/pallas_call | solution.py:19
  108.7 3.7 %collective-permute-start.15 = (f32[8,32,256]{2,1,0:T(8,128)}, f32[8,32,256]{2,1,0:T(8,128)S(1)}, u32[]{:S(2)}, u32[]{:S(2)}) collective-permute-start(f32[8,32,256]{2,1,0:T(8,128)} %get-tuple-element.52.e_a), channel_id=1, source_target_pairs={{8,0},{16,8},{24,16},{32,24},{40,32},{48,40},{56,48},{64,56},{72,6... | collective-permute-start | bytes 786440 | tf_op jit(solution)/shard_map/ppermute | solution.py:315
  112.5 1.9 collective-permute-start.14
  114.4 18.7 %collective-permute-done.9.got = f32[6,32,256]{2,1,0:T(8,128)S(1)} collective-permute-done((f32[6,32,256]{2,1,0:T(8,128)}, f32[6,32,256]{2,1,0:T(8,128)S(1)}, u32[]{:S(2)}, u32[]{:S(2)}) %collective-permute-start.9) | collective-permute-done | bytes 196640 | tf_op jit(solution)/shard_map/ppermute | solution.py:309
  133.1 0.7 copy-done.14
  133.8 1.9 shard_map.62.f_a
  135.7 1.9 collective-permute-start.12
  137.6 0.0 copy-start.13
  137.6 0.7 copy-done.13
  138.3 1.9 shard_map.63.f_b
  140.2 3.5 %collective-permute-start.11 = (f32[6,32,256]{2,1,0:T(8,128)}, f32[6,32,256]{2,1,0:T(8,128)S(1)}, u32[]{:S(2)}, u32[]{:S(2)}) collective-permute-start(f32[6,32,256]{2,1,0:T(8,128)} %shard_map.63.f_b), channel_id=1, source_target_pairs={{0,8},{8,16},{16,24},{24,32},{32,40},{40,48},{48,56},{56,64},{64,7... | collective-permute-start | bytes 589832 | tf_op jit(solution)/shard_map/ppermute | solution.py:361
  143.7 0.7 copy-done.9
  144.4 0.7 copy-done.10
  145.1 4.6 %shard_map.65 = (f32[2,6,96,256]{3,2,1,0:T(8,128)}, f32[2,2,64,256]{3,2,1,0:T(8,128)}) custom-call(s32[3]{0:T(128)} %pad_add_fusion.meta, f32[8,32,256]{2,1,0:T(8,128)} %get-tuple-element.52.e_a, f32[8,32,256]{2,1,0:T(8,128)} %get-tuple-element.53.e_b, f32[8,32,256]{2,1,0:T(8,128)} %copy-done.10, f32[8,32,256]{2,1,0:T(8,128)} %copy-done.9, ...), custom_call_target="tpu_custom_call" | custom-call | bytes 5431308 | tf_op jit(solution)/shard_map/pallas_call | solution.py:19
  149.7 0.4 collective-permute-done.11.f_low
  150.1 0.2 copy-done.11
  150.4 0.4 copy-done.12
  150.8 5.6 %shard_map.66 = (f32[3,64,256]{2,1,0:T(8,128)}, f32[2,6,96,256]{3,2,1,0:T(8,128)}, f32[2,3,64,256]{3,2,1,0:T(8,128)}) custom-call(s32[3]{0:T(128)} %pad_add_fusion.meta, f32[6,32,256]{2,1,0:T(8,128)} %shard_map.62.f_a, f32[6,32,256]{2,1,0:T(8,128)} %shard_map.63.f_b, f32[6,32,256]{2,1,0:T(8,128)} %copy-done.12, f32[6,32,256]{2,1,0:T(8,128)} %copy-done.11, ...), custom_call_target="tpu_custom_call" | custom-call | bytes 6676492 | tf_op jit(solution)/shard_map/pallas_call | solution.py:19
  156.4 5.5 %shard_map.67 = (f32[8,64,256]{2,1,0:T(8,128)}, f32[3,64,256]{2,1,0:T(8,128)}) custom-call(s32[3]{0:T(128)} %pad_add_fusion.meta, f32[2,6,96,256]{3,2,1,0:T(8,128)} %get-tuple-element.55.zn, f32[2,6,96,256]{3,2,1,0:T(8,128)} %get-tuple-element.54.ze, f32[2,3,64,256]{3,2,1,0:T(8,128)} %get-tuple-element.56.bx0, f32[2,2,64,256]{3,2,1,0:T(8,128)} %get-tuple-element.57.bx6, ...), custom_call_target="tpu_custom_call" | custom-call | bytes 6479884 | tf_op jit(solution)/shard_map/pallas_call | solution.py:19
  161.9 3.5 %collective-permute-start.17 = (f32[3,64,256]{2,1,0:T(8,128)}, f32[3,64,256]{2,1,0:T(8,128)S(1)}, u32[]{:S(2)}, u32[]{:S(2)}) collective-permute-start(f32[3,64,256]{2,1,0:T(8,128)} %get-tuple-element.60), channel_id=1, source_target_pairs={{0,256},{256,0},{1,257},{257,1},{2,258},{258,2},{3,259},{259,3},{4... | collective-permute-start | bytes 589832 | tf_op jit(solution)/shard_map/ppermute | solution.py:312
  165.3 5.9 %collective-permute-start.16 = (f32[3,64,256]{2,1,0:T(8,128)S(1)}, f32[3,64,256]{2,1,0:T(8,128)S(1)}, u32[]{:S(2)}, u32[]{:S(2)}) collective-permute-start(f32[3,64,256]{2,1,0:T(8,128)S(1)} %copy-done.20), channel_id=1, source_target_pairs={{256,1},{257,2},{258,3},{259,4},{260,5},{261,6},{262,7},{1,256},{2... | collective-permute-start | bytes 589832 | tf_op jit(solution)/shard_map/ppermute | solution.py:309
  171.3 0.7 copy-done.16
  172.0 2.0 shard_map.69.mid
  174.0 1.9 collective-permute-start.19
  175.9 15.0 %collective-permute-done.16.got = f32[3,64,256]{2,1,0:T(8,128)S(1)} collective-permute-done((f32[3,64,256]{2,1,0:T(8,128)S(1)}, f32[3,64,256]{2,1,0:T(8,128)S(1)}, u32[]{:S(2)}, u32[]{:S(2)}) %collective-permute-start.16) | collective-permute-done | bytes 196640 | tf_op jit(solution)/shard_map/ppermute | solution.py:309
  190.9 0.7 copy-done.15
  191.6 2.0 shard_map.68.far
  193.6 4.0 %collective-permute-start.18 = (f32[3,64,256]{2,1,0:T(8,128)}, f32[3,64,256]{2,1,0:T(8,128)S(1)}, u32[]{:S(2)}, u32[]{:S(2)}) collective-permute-start(f32[3,64,256]{2,1,0:T(8,128)} %shard_map.68.far), channel_id=1, source_target_pairs={{0,256},{256,0},{1,257},{257,1},{2,258},{258,2},{3,259},{259,3},{4... | collective-permute-start | bytes 589832 | tf_op jit(solution)/shard_map/ppermute | solution.py:312
  197.6 1.3 collective-permute-done.18.other_far
  198.9 0.7 copy-done.17
  199.5 0.7 copy-done.8
  200.3 2.4 %shard_map.70 = f32[64,16,256]{2,1,0:T(8,128)} custom-call(s32[3]{0:T(128)} %pad_add_fusion.meta, f32[3,64,256]{2,1,0:T(8,128)} %shard_map.68.far, f32[5,64,256]{2,1,0:T(8,128)} %shard_map.69.mid, f32[3,64,256]{2,1,0:T(8,128)} %copy-done.17, f32[5,64,256]{2,1,0:T(8,128)} %copy-done.8), custom_call_target="tpu_custom_call" | custom-call | bytes 2097164 | tf_op jit(solution)/shard_map/pallas_call | solution.py:19
  (35 shorter events, 0.1 us)
Async XLA Ops:
  3.1 28.6 %collective-permute-start.6 = (f32[520,256]{1,0:T(8,128)}, f32[520,256]{1,0:T(8,128)S(1)}, u32[]{:S(2)}, u32[]{:S(2)}) collective-permute-start(f32[520,256]{1,0:T(8,128)} %get-tuple-element.38.own), channel_id=1, source_target_pairs={{0,256},{256,0},{1,257},{257,1},{2,258},{258,2},{3,259},{259,3},{4... | collective-permute-start | bytes 1597448 | tf_op jit(solution)/shard_map/ppermute | solution.py:312
  8.0 59.3 %collective-permute-start.5 = (f32[11,32,256]{2,1,0:T(8,128)}, f32[11,32,256]{2,1,0:T(8,128)S(1)}, u32[]{:S(2)}, u32[]{:S(2)}) collective-permute-start(f32[11,32,256]{2,1,0:T(8,128)} %get-tuple-element.34.e_a.e), channel_id=1, source_target_pairs={{8,0},{16,8},{24,16},{32,24},{40,32},{48,40},{56,48},{64,56},{72,6... | collective-permute-start | bytes 1081352 | tf_op jit(solution)/shard_map/ppermute | solution.py:315
  12.2 62.0 %collective-permute-start.4 = (f32[11,32,256]{2,1,0:T(8,128)}, f32[11,32,256]{2,1,0:T(8,128)S(1)}, u32[]{:S(2)}, u32[]{:S(2)}) collective-permute-start(f32[11,32,256]{2,1,0:T(8,128)} %get-tuple-element.36.e_b.e), channel_id=1, source_target_pairs={{0,8},{8,16},{16,24},{24,32},{32,40},{40,48},{48,56},{56,64},{64,7... | collective-permute-start | bytes 1081352 | tf_op jit(solution)/shard_map/ppermute | solution.py:315
  16.1 26.9 %collective-permute-start = (f32[3,32,256]{2,1,0:T(8,128)}, f32[3,32,256]{2,1,0:T(8,128)S(1)}, u32[]{:S(2)}, u32[]{:S(2)}) collective-permute-start(f32[3,32,256]{2,1,0:T(8,128)} %get-tuple-element.33), channel_id=1, source_target_pairs={{256,1},{257,2},{258,3},{259,4},{260,5},{261,6},{262,7},{1,256},{2... | collective-permute-start | bytes 294920 | tf_op jit(solution)/shard_map/ppermute | solution.py:309
  31.7 0.8 copy-start
  34.5 39.7 %collective-permute-start.7 = (f32[16,16,256]{2,1,0:T(8,128)}, f32[16,16,256]{2,1,0:T(8,128)S(1)}, u32[]{:S(2)}, u32[]{:S(2)}) collective-permute-start(f32[16,16,256]{2,1,0:T(8,128)} %get-tuple-element.39), channel_id=1, source_target_pairs={{0,8},{8,16},{16,24},{24,32},{32,40},{40,48},{48,56},{56,64},{64,7... | collective-permute-start | bytes 786440 | tf_op jit(solution)/shard_map/ppermute | solution.py:315
  36.4 37.8 %collective-permute-start.8 = (f32[16,16,256]{2,1,0:T(8,128)}, f32[16,16,256]{2,1,0:T(8,128)S(1)}, u32[]{:S(2)}, u32[]{:S(2)}) collective-permute-start(f32[16,16,256]{2,1,0:T(8,128)} %get-tuple-element.40), channel_id=1, source_target_pairs={{8,0},{16,8},{24,16},{32,24},{40,32},{48,40},{56,48},{64,56},{72,6... | collective-permute-start | bytes 786440 | tf_op jit(solution)/shard_map/ppermute | solution.py:315
  43.0 38.9 %copy-start.4 = (f32[3,32,256]{2,1,0:T(8,128)}, f32[3,32,256]{2,1,0:T(8,128)S(1)}, u32[]{:S(2)}) copy-start(f32[3,32,256]{2,1,0:T(8,128)S(1)} %collective-permute-done.f_a.far) | copy-start | bytes 294916
  43.0 22.3 %collective-permute-start.1 = (f32[3,32,256]{2,1,0:T(8,128)}, f32[3,32,256]{2,1,0:T(8,128)S(1)}, u32[]{:S(2)}, u32[]{:S(2)}) collective-permute-start(f32[3,32,256]{2,1,0:T(8,128)} %get-tuple-element.35), channel_id=1, source_target_pairs={{256,1},{257,2},{258,3},{259,4},{260,5},{261,6},{262,7},{1,256},{2... | collective-permute-start | bytes 294920 | tf_op jit(solution)/shard_map/ppermute | solution.py:309
  65.3 16.6 %copy-start.5 = (f32[3,32,256]{2,1,0:T(8,128)}, f32[3,32,256]{2,1,0:T(8,128)S(1)}, u32[]{:S(2)}) copy-start(f32[3,32,256]{2,1,0:T(8,128)S(1)} %collective-permute-done.1.f_b.far) | copy-start | bytes 294916
  65.3 16.6 %collective-permute-start.3 = (f32[3,32,256]{2,1,0:T(8,128)S(1)}, f32[3,32,256]{2,1,0:T(8,128)S(1)}, u32[]{:S(2)}, u32[]{:S(2)}) collective-permute-start(f32[3,32,256]{2,1,0:T(8,128)S(1)} %collective-permute-done.f_a.far), channel_id=1, source_target_pairs={{8,0},{16,8},{24,16},{32,24},{40,32},{48,40},{56,48},{64,56},{72,6... | collective-permute-start | bytes 294920 | tf_op jit(solution)/shard_map/ppermute | solution.py:315
  67.3 7.0 %copy-start.6 = (f32[11,32,256]{2,1,0:T(8,128)}, f32[11,32,256]{2,1,0:T(8,128)S(1)}, u32[]{:S(2)}) copy-start(f32[11,32,256]{2,1,0:T(8,128)S(1)} %collective-permute-done.5.e_high) | copy-start | bytes 1081348
  67.3 14.7 %collective-permute-start.2 = (f32[3,32,256]{2,1,0:T(8,128)S(1)}, f32[3,32,256]{2,1,0:T(8,128)S(1)}, u32[]{:S(2)}, u32[]{:S(2)}) collective-permute-start(f32[3,32,256]{2,1,0:T(8,128)S(1)} %collective-permute-done.1.f_b.far), channel_id=1, source_target_pairs={{0,8},{8,16},{16,24},{24,32},{32,40},{40,48},{48,56},{56,64},{64,7... | collective-permute-start | bytes 294920 | tf_op jit(solution)/shard_map/ppermute | solution.py:315
  74.2 0.7 copy-start.7
  74.2 0.9 copy-start.1
  74.2 0.9 copy-start.2
  81.9 0.6 copy-start.18
  81.9 0.7 copy-start.19
  88.4 17.3 %collective-permute-start.13 = (f32[6,64,256]{2,1,0:T(8,128)}, f32[6,64,256]{2,1,0:T(8,128)S(1)}, u32[]{:S(2)}, u32[]{:S(2)}) collective-permute-start(f32[6,64,256]{2,1,0:T(8,128)} %get-tuple-element.51.c_part), channel_id=1, source_target_pairs={{0,256},{256,0},{1,257},{257,1},{2,258},{258,2},{3,259},{259,3},{4... | collective-permute-start | bytes 1179656 | tf_op jit(solution)/shard_map/ppermute | solution.py:312
  91.4 41.7 %collective-permute-start.9 = (f32[6,32,256]{2,1,0:T(8,128)}, f32[6,32,256]{2,1,0:T(8,128)S(1)}, u32[]{:S(2)}, u32[]{:S(2)}) collective-permute-start(f32[6,32,256]{2,1,0:T(8,128)} %get-tuple-element.48.c), channel_id=1, source_target_pairs={{256,1},{257,2},{258,3},{259,4},{260,5},{261,6},{262,7},{1,256},{2... | collective-permute-start | bytes 589832 | tf_op jit(solution)/shard_map/ppermute | solution.py:309
  98.6 39.0 %collective-permute-start.10 = (f32[6,32,256]{2,1,0:T(8,128)}, f32[6,32,256]{2,1,0:T(8,128)S(1)}, u32[]{:S(2)}, u32[]{:S(2)}) collective-permute-start(f32[6,32,256]{2,1,0:T(8,128)} %get-tuple-element.49.c), channel_id=1, source_target_pairs={{256,1},{257,2},{258,3},{259,4},{260,5},{261,6},{262,7},{1,256},{2... | collective-permute-start | bytes 589832 | tf_op jit(solution)/shard_map/ppermute | solution.py:309
  105.7 0.7 copy-start.3
  108.7 35.0 %collective-permute-start.15 = (f32[8,32,256]{2,1,0:T(8,128)}, f32[8,32,256]{2,1,0:T(8,128)S(1)}, u32[]{:S(2)}, u32[]{:S(2)}) collective-permute-start(f32[8,32,256]{2,1,0:T(8,128)} %get-tuple-element.52.e_a), channel_id=1, source_target_pairs={{8,0},{16,8},{24,16},{32,24},{40,32},{48,40},{56,48},{64,56},{72,6... | collective-permute-start | bytes 786440 | tf_op jit(solution)/shard_map/ppermute | solution.py:315
  112.5 31.3 %collective-permute-start.14 = (f32[8,32,256]{2,1,0:T(8,128)}, f32[8,32,256]{2,1,0:T(8,128)S(1)}, u32[]{:S(2)}, u32[]{:S(2)}) collective-permute-start(f32[8,32,256]{2,1,0:T(8,128)} %get-tuple-element.53.e_b), channel_id=1, source_target_pairs={{0,8},{8,16},{16,24},{24,32},{32,40},{40,48},{48,56},{56,64},{64,7... | collective-permute-start | bytes 786440 | tf_op jit(solution)/shard_map/ppermute | solution.py:315
  133.1 0.7 copy-start.14
  135.7 14.0 %collective-permute-start.12 = (f32[6,32,256]{2,1,0:T(8,128)}, f32[6,32,256]{2,1,0:T(8,128)S(1)}, u32[]{:S(2)}, u32[]{:S(2)}) collective-permute-start(f32[6,32,256]{2,1,0:T(8,128)} %shard_map.62.f_a), channel_id=1, source_target_pairs={{8,0},{16,8},{24,16},{32,24},{40,32},{48,40},{56,48},{64,56},{72,6... | collective-permute-start | bytes 589832 | tf_op jit(solution)/shard_map/ppermute | solution.py:359
  137.6 0.7 copy-start.13
  140.2 10.0 %collective-permute-start.11 = (f32[6,32,256]{2,1,0:T(8,128)}, f32[6,32,256]{2,1,0:T(8,128)S(1)}, u32[]{:S(2)}, u32[]{:S(2)}) collective-permute-start(f32[6,32,256]{2,1,0:T(8,128)} %shard_map.63.f_b), channel_id=1, source_target_pairs={{0,8},{8,16},{16,24},{24,32},{32,40},{40,48},{48,56},{56,64},{64,7... | collective-permute-start | bytes 589832 | tf_op jit(solution)/shard_map/ppermute | solution.py:361
  143.7 0.7 copy-start.9
  144.4 0.7 copy-start.10
  149.7 0.7 copy-start.11
  150.1 0.7 copy-start.12
  156.4 9.0 %copy-start.20 = (f32[3,64,256]{2,1,0:T(8,128)S(1)}, f32[3,64,256]{2,1,0:T(8,128)}, u32[]{:S(2)}) copy-start(f32[3,64,256]{2,1,0:T(8,128)} %get-tuple-element.59) | copy-start | bytes 589828
  161.9 9.4 %collective-permute-start.17 = (f32[3,64,256]{2,1,0:T(8,128)}, f32[3,64,256]{2,1,0:T(8,128)S(1)}, u32[]{:S(2)}, u32[]{:S(2)}) collective-permute-start(f32[3,64,256]{2,1,0:T(8,128)} %get-tuple-element.60), channel_id=1, source_target_pairs={{0,256},{256,0},{1,257},{257,1},{2,258},{258,2},{3,259},{259,3},{4... | collective-permute-start | bytes 589832 | tf_op jit(solution)/shard_map/ppermute | solution.py:312
  165.3 25.6 %collective-permute-start.16 = (f32[3,64,256]{2,1,0:T(8,128)S(1)}, f32[3,64,256]{2,1,0:T(8,128)S(1)}, u32[]{:S(2)}, u32[]{:S(2)}) collective-permute-start(f32[3,64,256]{2,1,0:T(8,128)S(1)} %copy-done.20), channel_id=1, source_target_pairs={{256,1},{257,2},{258,3},{259,4},{260,5},{261,6},{262,7},{1,256},{2... | collective-permute-start | bytes 589832 | tf_op jit(solution)/shard_map/ppermute | solution.py:309
  171.3 0.7 copy-start.16
  174.0 24.9 %collective-permute-start.19 = (f32[5,64,256]{2,1,0:T(8,128)}, f32[5,64,256]{2,1,0:T(8,128)S(1)}, u32[]{:S(2)}, u32[]{:S(2)}) collective-permute-start(f32[5,64,256]{2,1,0:T(8,128)} %shard_map.69.mid), channel_id=1, source_target_pairs={{0,256},{256,0},{1,257},{257,1},{2,258},{258,2},{3,259},{259,3},{4... | collective-permute-start | bytes 983048 | tf_op jit(solution)/shard_map/ppermute | solution.py:312
  190.9 0.7 copy-start.15
  193.6 5.3 %collective-permute-start.18 = (f32[3,64,256]{2,1,0:T(8,128)}, f32[3,64,256]{2,1,0:T(8,128)S(1)}, u32[]{:S(2)}, u32[]{:S(2)}) collective-permute-start(f32[3,64,256]{2,1,0:T(8,128)} %shard_map.68.far), channel_id=1, source_target_pairs={{0,256},{256,0},{1,257},{257,1},{2,258},{258,2},{3,259},{259,3},{4... | collective-permute-start | bytes 589832 | tf_op jit(solution)/shard_map/ppermute | solution.py:312
  198.8 0.7 copy-start.17
  199.5 0.7 copy-start.8

commit v2 on v1

v2 whole, which is shorter than its diff:
```python
import jax
import jax.numpy as jnp
from jax import lax
from jax.experimental import pallas as pl
from jax.experimental.pallas import tpu as pltpu
from jax.sharding import PartitionSpec as P

F32 = jnp.float32
BF16 = jnp.bfloat16
NX = 256
LIMIT = 20 * 1024 * 1024
VM = pl.BlockSpec(memory_space=pltpu.VMEM)
SM = pl.BlockSpec(memory_space=pltpu.SMEM)


def call(body, outs, *args, smem=1, flops=0, scratch=()):
    size = sum(a.size * a.dtype.itemsize for a in args)
    size += sum(4 * o.size for o in outs)
    return pl.pallas_call(
        body,
        out_shape=outs,
        in_specs=[SM] * smem + [VM] * (len(args) - smem),
        out_specs=[VM] * len(outs),
        scratch_shapes=list(scratch),
        compiler_params=pltpu.CompilerParams(vmem_limit_bytes=LIMIT),
        cost_estimate=pl.CostEstimate(flops=0, bytes_accessed=0, transcendentals=0),
    )(*args)


def f32(*shape):
    return jax.ShapeDtypeStruct(shape, F32)


def b16(*shape):
    return jax.ShapeDtypeStruct(shape, BF16)


def parts(x):
    high = x.astype(BF16)
    return high, (x - high.astype(F32)).astype(BF16)


def dot(a, b):
    return jnp.dot(a, b, preferred_element_type=F32)


def rows_of(ref, half):
    return jnp.swapaxes(ref[:, 8 * half : 8 * half + 8, :], 0, 1)


def by_core(meta, body):
    for core in range(2):
        pl.when(meta[0] == core)(lambda core=core: body(core, lambda r: r % 8 if core == 0 else 7 - r % 8))


def far_body(meta, start, out):
    def body(core, at):
        rows = rows_of(start, core)
        for j in range(3):
            out[j] = rows[at(j)]

    by_core(meta, body)


def start_body(meta, start, e_a, e_b):
    def body(core, at):
        rows = (rows_of(start, core), rows_of(start, 1 - core))
        for j in range(11):
            e_a[j] = rows[j // 8][at(j), :32]
            e_b[j] = rows[j // 8][at(j), 32:]

    by_core(meta, body)


def observed_body(meta, e_a, e_b, observed, mine, send_a, send_b, low, high):
    def body(core, at):
        rows, others = rows_of(observed, core), rows_of(observed, 1 - core)
        for j in range(8):
            row, other = rows[at(j)], others[at(15 - j)]
            mine[j] = row
            if j < 4:
                send_a[j] = other
            else:
                send_b[j - 4] = other
            for k, x in ((j, row), (8 + j, other)):
                low[352 + 16 * k : 368 + 16 * k] = x[0:16]
                high[352 + 16 * k : 368 + 16 * k] = x[48:64]

    by_core(meta, body)
    for j in range(11):
        low[32 * j : 32 * j + 32] = e_a[j]
        high[32 * j : 32 * j + 32] = e_b[j]


def collect_body(meta, mine, got_a, got_b, obs):
    other = 1 - meta[0]
    obs[meta[0]] = mine[...]
    obs[other, 0:4] = got_a[other]
    obs[other, 4:8] = got_b[other]


def margins_body(g_low, g_high, send):
    for j in range(8):
        send[j, 0:16] = g_low[480 + 16 * j : 496 + 16 * j]
        send[j, 16:32] = g_high[480 + 16 * j : 496 + 16 * j]


def halves_body(far, _, a, b):
    for j in range(3):
        a[j] = far[j, :32]
        b[j] = far[j, 32:]


def profiles_body(sz, sy, sx, out):
    out[...] = jnp.zeros((8, NX), F32)
    out[0:1, 0:31] = sz[...]
    out[1:2, 0:7] = sy[...]
    out[2:3, 0:7] = sx[...]


def weights_body(meta, both, zf, zb, xf, xb, yw):
    def band(shape, row, taps, place, shift=lambda j: j):
        d = shift(lax.broadcasted_iota(jnp.int32, shape, 1)) - lax.broadcasted_iota(jnp.int32, shape, 0)
        total = jnp.zeros(shape, F32)
        for t in range(taps):
            total = jnp.where(d == place(t), row[:, t : t + 1], total)
        return total

    for v in range(2):
        w = both[v]
        sums = jnp.sum(w, axis=1, keepdims=True)
        w = w / sums_or_one(sums)
        wz, wy, wx = w[0:1], w[1:2], w[2:3]
        high, low = parts(band((96, 128), wz, 31, lambda t: t + 1))
        zf[192 * v : 192 * v + 96, 0:128] = high
        zf[192 * v : 192 * v + 96, 128:256] = high
        zf[192 * v + 96 : 192 * v + 192, 0:128] = low
        zf[192 * v + 96 : 192 * v + 192, 128:256] = jnp.zeros((96, 128), BF16)
        for first, width, shift in ((0, 64, lambda j: j), (128, 32, lambda j: jnp.where(j < 16, j - 16, j + 48))):
            high, low = parts(band((64, width), wz, 31, lambda t: 15 - t, shift))
            zb[v, 0:64, first : first + width] = high
            zb[v, 0:64, first + width : first + 2 * width] = high
            zb[v, 64:128, first : first + width] = low
            zb[v, 64:128, first + width : first + 2 * width] = jnp.zeros((64, width), BF16)
        high, low = parts(band((256, 256), wx, 7, lambda t: 3 - t))
        xf[v, 0] = high
        xf[v, 1] = low
        high, low = parts(band((256, 256), wx, 7, lambda t: t - 3))
        xb[v, 0] = high
        xb[v, 1] = low
        for core in range(2):

            @pl.when(meta[0] == core)
            def _(core=core, v=v, wy=wy):
                for t in range(7):
                    s = t if core == 0 else 6 - t
                    yw[8 * v + t : 8 * v + t + 1, :] = jnp.broadcast_to(wy[:, s : s + 1], (1, NX))

        yw[8 * v + 7 : 8 * v + 8, :] = jnp.zeros((1, NX), F32)


def sums_or_one(sums):
    rows = lax.broadcasted_iota(jnp.int32, sums.shape, 0)
    return jnp.where(rows < 3, sums, 1.0)


def blur_z(zf, low, a, b, high):
    highs, lows = zip(*[parts(x) for x in (low, a, b, high)])
    both = dot(zf[...], jnp.concatenate(highs + lows, axis=0))
    return [both[192 * v : 192 * v + 96] + both[192 * v + 96 : 192 * v + 192] for v in range(2)]


def blur_x(x, weight, v):
    high, low = parts(x)
    return dot(high, weight[v, 0]) + dot(low, weight[v, 0]) + dot(high, weight[v, 1])


def quotient(rows, recorded, yw, xf, v, inside=None):
    total = yw[8 * v : 8 * v + 1] * rows[0]
    for t in range(1, 7):
        total = total + yw[8 * v + t : 8 * v + t + 1] * rows[t]
    blurred = blur_x(total, xf, v)
    return recorded / (blurred if inside is None else jnp.where(inside(blurred.shape), blurred, 1.0))


def margin_inside(meta):
    def inside(shape):
        at = lax.broadcasted_iota(jnp.int32, shape, 0)
        return (at >= meta[1]) & (at < meta[2])

    return inside


def margins(rows):
    return jnp.concatenate([rows[0:16], rows[80:96]], axis=0)


def back_own(q, zb, xb, v):
    both = dot(zb[v, :, 0:128], jnp.concatenate(parts(q), axis=0))
    return blur_x(both[0:64] + both[64:128], xb, v)


def back_margins(q, zb, xb, v):
    both = dot(zb[v, :, 128:192], jnp.concatenate(parts(q), axis=0))
    both = both[0:64] + both[64:128]
    return blur_x(jnp.concatenate([both[0:16], both[48:64]], axis=0), xb, v)


def row_result(meta, rows, obs, margin, yw, xf, xb, zb, j, v):
    own = quotient([r[16:80] for r in rows], obs[v, j], yw, xf, v)
    out = quotient([margins(r) for r in rows], margin[v, j], yw, xf, v, margin_inside(meta))
    both = dot(zb[v], jnp.concatenate(parts(own) + parts(out), axis=0))
    return blur_x(both[0:64] + both[64:128], xb, v)


def spread_back(yw, terms, row, planes=slice(0, 64)):
    total = None
    for v in range(2):
        for t in range(7):
            j = row + t - 3
            if 0 <= j <= 7:
                term = yw[8 * v + 6 - t : 8 * v + 7 - t] * terms(v, j)[planes]
                total = term if total is None else total + term
    return total


def early1_body(e_a, e_b, obs, g_low, g_high, zf, zb, xf, xb, yw, ze, bx):
    for r in range(11):
        low, high = g_low[32 * r : 32 * r + 32], g_high[32 * r : 32 * r + 32]
        for v, x in enumerate(blur_z(zf, low, e_a[r], e_b[r], high)):
            ze[v, r] = x
    for j in range(3, 6):
        for v in range(2):
            q = quotient([ze[v, j - 3 + t, 16:80] for t in range(7)], obs[v, j], yw, xf, v)
            bx[v, j - 3] = back_own(q, zb, xb, v)


def late1_body(f, f_low, f_high, ze, bx, obs, zf, zb, xf, xb, yw, c_far, zn, new):
    for j in range(3):
        for v, x in enumerate(blur_z(zf, f_low[j], f[j, :32], f[j, 32:], f_high[j])):
            zn[v, 2 - j] = x
    for j in range(3):
        for v in range(2):
            rows = [zn[v, j + t, 16:80] if j + t < 3 else ze[v, j + t - 3, 16:80] for t in range(7)]
            new[v, j] = back_own(quotient(rows, obs[v, j], yw, xf, v), zb, xb, v)
    for row in range(-3, 3):
        c_far[row + 3] = spread_back(yw, lambda v, j: new[v, j] if j < 3 else bx[v, j - 3], row, slice(16, 48))


def rest1_body(meta, ze, zn, bx0, bx3, obs, g_low, g_high, got, zb, xf, xb, yw, c_far, c_mid, c_part, margin, new):
    other = 1 - meta[0]
    margin[other] = got[other]
    for j in range(8):
        margin[meta[0], j, 0:16] = g_low[352 + 16 * j : 368 + 16 * j]
        margin[meta[0], j, 16:32] = g_high[352 + 16 * j : 368 + 16 * j]
    for j in range(8):
        for v in range(2):
            rows = [zn[v, j + t] if j + t < 3 else ze[v, j + t - 3] for t in range(7)]
            if j < 6:
                own = bx0[v, j] if j < 3 else bx3[v, j - 3]
                q = quotient([margins(r) for r in rows], margin[v, j], yw, xf, v, margin_inside(meta))
                edge = back_margins(q, zb, xb, v)
                new[v, j, 0:16] = own[0:16] + edge[0:16]
                new[v, j, 16:48] = own[16:48]
                new[v, j, 48:64] = own[48:64] + edge[16:32]
            else:
                new[v, j] = row_result(meta, rows, obs, margin, yw, xf, xb, zb, j, v)
    for row in range(-3, 11):
        total = spread_back(yw, lambda v, j: new[v, j], row)
        if row < 3:
            c_far[row + 3, 0:16] = total[0:16]
            c_far[row + 3, 16:32] = total[48:64]
        elif row < 5:
            c_mid[row - 3] = total
        else:
            c_part[row - 5] = total


def update_mid_body(meta, e_a, e_b, c_mid, c_part, got, _, out_a, out_b):
    for r in range(3, 11):
        c = c_mid[r - 3] if r < 5 else c_part[r - 5] + got[1 - meta[0], 10 - r]
        out_a[r - 3] = e_a[r] * (0.5 * c[:32])
        out_b[r - 3] = e_b[r] * (0.5 * c[32:])


def update_far_body(far, e_a, e_b, c_mid, c_edge, got_mid, got_edge, out_a, out_b):
    for r in range(-3, 3):
        mid = 0.5 * (c_mid[r + 3] + got_mid[2 - r])
        edge = 0.5 * (c_edge[r + 3] + got_edge[2 - r])
        old_a = far[-1 - r, 0:32] if r < 0 else e_a[r]
        old_b = far[-1 - r, 32:64] if r < 0 else e_b[r]
        out_a[r + 3] = old_a * jnp.concatenate([edge[0:16], mid[0:16]], axis=0)
        out_b[r + 3] = old_b * jnp.concatenate([mid[16:32], edge[16:32]], axis=0)


def early2_body(meta, e_a, e_b, e_low, e_high, obs, margin, zf, zb, xf, xb, yw, ze, bx, buf):
    for r in range(8):
        for v, x in enumerate(blur_z(zf, e_low[r], e_a[r], e_b[r], e_high[r])):
            buf[v, r] = x
            if r < 6:
                ze[v, r] = x
    for j in (6, 7):
        for v in range(2):
            rows = [buf[v, j - 6 + t] for t in range(7)]
            bx[v, j - 6] = row_result(meta, rows, obs, margin, yw, xf, xb, zb, j, v)


def late2_body(meta, f_a, f_b, f_low, f_high, ze, obs, margin, zf, zb, xf, xb, yw, c_far, zn, bx):
    for r in range(6):
        for v, x in enumerate(blur_z(zf, f_low[r], f_a[r], f_b[r], f_high[r])):
            zn[v, r] = x
    for j in range(3):
        for v in range(2):
            rows = [zn[v, j + t] if j + t < 6 else ze[v, j + t - 6] for t in range(7)]
            bx[v, j] = row_result(meta, rows, obs, margin, yw, xf, xb, zb, j, v)
    for k in range(3):
        c_far[k] = spread_back(yw, lambda v, j: bx[v, j] if j < 3 else None, -1 - k)


def rest2_body(meta, zn, ze, bx0, bx6, obs, margin, zb, xf, xb, yw, c_own, c_part, new):
    for j in range(3, 6):
        for v in range(2):
            rows = [zn[v, j + t] if j + t < 6 else ze[v, j + t - 6] for t in range(7)]
            new[v, j - 3] = row_result(meta, rows, obs, margin, yw, xf, xb, zb, j, v)

    def terms(v, j):
        return bx0[v, j] if j < 3 else new[v, j - 3] if j < 6 else bx6[v, j - 6]

    for row in range(11):
        total = spread_back(yw, terms, row)
        if row < 8:
            c_own[row] = total
        else:
            c_part[row - 8] = total


def final_mid_body(meta, e_a, e_b, c_own, got, out):
    for r in range(3, 8):
        c = c_own[r] if r < 5 else c_own[r] + got[1 - meta[0], 7 - r]
        out[r - 3, :32] = e_a[r - 3] * (0.5 * c[:32])
        out[r - 3, 32:] = e_b[r - 3] * (0.5 * c[32:])


def final_far_body(f_a, f_b, c_own, got, out):
    for r in range(3):
        c = c_own[r] + got[r]
        out[r, :32] = f_a[r + 3] * (0.5 * c[:32])
        out[r, 32:] = f_b[r + 3] * (0.5 * c[32:])


def output_body(meta, far, mid, out):
    def body(core, at):
        for c in range(2):
            block = [far[c, r] if r < 3 else mid[c, r - 3] for r in range(8)]
            block = block if c == 0 else block[::-1]
            out[:, 8 * c : 8 * c + 8, :] = jnp.swapaxes(jnp.stack(block), 0, 1)

    body(0, None)


def on_device(observed, start, spread_z, spread_y, spread_x):
    gy, gz = lax.axis_size("gy"), lax.axis_size("gz")
    across = [(gy + g, g + 1) for g in range(gy - 1)]
    across += [(b, a) for a, b in across]
    up = [(i, i + 1) for i in range(gz - 1)]
    down = [(j, i) for i, j in up]

    def far(x):
        return lax.ppermute(x, ("view", "gy"), across)

    def both(x):
        return lax.all_gather(x, "view")

    def along_z(first, last):
        return lax.ppermute(last, "gz", up), lax.ppermute(first, "gz", down)

    def place():
        at = lax.axis_index("gz")
        limits = [jnp.where(at == 0, 16, 0), jnp.where(at == gz - 1, 16, 32)]
        return jnp.stack([lax.axis_index("view"), *limits]).astype(jnp.int32)

    meta = place()
    recorded = observed[0]

    (send_far,) = call(far_body, [f32(3, 64, NX)], meta, start)
    f = far(send_far)

    def beside(start, recorded, spread_z, spread_y, spread_x):
        meta = place()
        e_a, e_b = call(start_body, [f32(11, 32, NX)] * 2, meta, start)
        mine, send_a, send_b, first, last = call(
            observed_body,
            [f32(8, 64, NX), f32(4, 64, NX), f32(4, 64, NX), f32(608, NX), f32(608, NX)],
            meta, e_a, e_b, recorded,
        )
        g_low, g_high = along_z(first, last)
        (obs,) = call(collect_body, [f32(2, 8, 64, NX)], meta, mine, both(send_a), both(send_b))
        (profiles,) = call(profiles_body, [f32(8, NX)], spread_z, spread_y, spread_x, smem=0)
        weights = call(
            weights_body,
            [b16(384, 256), b16(2, 128, 192), b16(2, 2, 256, 256), b16(2, 2, 256, 256), f32(16, NX)],
            meta, both(profiles),
        )
        return e_a, e_b, obs, g_low, g_high, *weights

    args = (start, recorded, spread_z, spread_y, spread_x)
    shapes = jax.eval_shape(beside, *args)
    e_a, e_b, obs, g_low, g_high, zf, zb, xf, xb, yw = lax.cond(
        lax.axis_index("gz") < gz, beside, lambda *a: tuple(jnp.zeros(x.shape, x.dtype) for x in shapes), *args
    )
    f_low, f_high = along_z(*call(halves_body, [f32(3, 32, NX)] * 2, f, yw, smem=0))
    ze, bx3 = call(
        early1_body, [f32(2, 11, 96, NX), f32(2, 3, 64, NX)],
        e_a, e_b, obs, g_low, g_high, zf, zb, xf, xb, yw, smem=0,
    )
    c_far_mid, zn, bx0 = call(
        late1_body, [f32(6, 32, NX), f32(2, 3, 96, NX), f32(2, 3, 64, NX)],
        f, f_low, f_high, ze, bx3, obs, zf, zb, xf, xb, yw, smem=0,
    )
    got_mid = far(c_far_mid)
    (send,) = call(margins_body, [f32(8, 32, NX)], g_low, g_high, smem=0)
    c_far_edge, c_mid, c_part, margin = call(
        rest1_body, [f32(6, 32, NX), f32(2, 64, NX), f32(6, 64, NX), f32(2, 8, 32, NX)],
        meta, ze, zn, bx0, bx3, obs, g_low, g_high, both(send), zb, xf, xb, yw,
        scratch=[pltpu.VMEM((2, 8, 64, NX), F32)],
    )
    got_edge = far(c_far_edge)
    obs = (obs, margin)
    got = both(c_part)
    m_a, m_b = call(update_mid_body, [f32(8, 32, NX)] * 2, meta, e_a, e_b, c_mid, c_part, got, got_mid)
    m_low, m_high = along_z(m_a, m_b)
    ze, bx6 = call(
        early2_body, [f32(2, 6, 96, NX), f32(2, 2, 64, NX)],
        meta, m_a, m_b, m_low, m_high, *obs, zf, zb, xf, xb, yw,
        scratch=[pltpu.VMEM((2, 8, 96, NX), F32)],
    )
    n_a, n_b = call(
        update_far_body, [f32(6, 32, NX)] * 2, f, e_a, e_b, c_far_mid, c_far_edge, got_mid, got_edge, smem=0
    )
    n_low, n_high = along_z(n_a, n_b)
    c_far, zn, bx0 = call(
        late2_body, [f32(3, 64, NX), f32(2, 6, 96, NX), f32(2, 3, 64, NX)],
        meta, n_a, n_b, n_low, n_high, ze, *obs, zf, zb, xf, xb, yw,
    )
    got_far = far(c_far)
    c_own, c_part = call(
        rest2_body, [f32(8, 64, NX), f32(3, 64, NX)],
        meta, zn, ze, bx0, bx6, *obs, zb, xf, xb, yw,
        scratch=[pltpu.VMEM((2, 3, 64, NX), F32)],
    )
    got_part = both(c_part)
    (mid,) = call(final_mid_body, [f32(5, 64, NX)], meta, m_a, m_b, c_own, got_part)
    other_mid = both(mid)
    (last,) = call(final_far_body, [f32(3, 64, NX)], n_a, n_b, c_own, got_far, smem=0)
    other_last = both(last)
    (out,) = call(output_body, [f32(64, 16, NX)], meta, other_last, other_mid)
    return out


def solution(mesh):
    return jax.shard_map(
        on_device,
        mesh=mesh,
        in_specs=(
            P("view", "gz", "gy", None),
            P("gz", "gy", None),
            P("view", None),
            P("view", None),
            P("view", None),
        ),
        out_specs=P("gz", "gy", None),
        check_vma=False,
    )
```

time: 204 us -> 178 us (0.87)
  the two profiles are of different devices: /device:TPU:37 before, /device:TPU:101 now
where the time goes in v2:
time: 178 us; the launch traced here: 177 us
  starting transfers between devices  62.4 us (35%)
  blocking collectives  40.7 us (23%)
  waiting for transfers between devices  37.9 us (21%)
  Pallas kernels  35.7 us (20%)
    all_gather x8, blocking collectives, both(): return lax.all_gather(x, 'view')  40.7 us
    ppermute x4, starting transfers between devices, far(): return lax.ppermute(x, ('view', 'gy'), across)  35.9 us
    pallas_call x19, Pallas kernels, call(): pl.pallas_call(body, out_shape=outs, in_specs=[SM] * smem + [VM] * (len(a...  35.7 us
    ppermute x8, starting transfers between devices, along_z(): return (lax.ppermute(last, 'gz', up), lax.ppermute(first, 'gz', down))  26.5 us
    ppermute x4, waiting for transfers between devices, far(): return lax.ppermute(x, ('view', 'gy'), across)  19.8 us
    ppermute x8, waiting for transfers between devices, along_z(): return (lax.ppermute(last, 'gz', up), lax.ppermute(first, 'gz', down))  18.1 us
  transfers between devices with their start and end apart: 12, of which 3 were waited for; matrix products, arithmetic and copies ran while one was open for 0% of the time, Pallas kernels for 11%

profile of v2, /device:TPU:101, one launch (start us, length us, event | category | flops | bytes accessed | tf_op | source)
XLA Modules:
  0.0 177.2 jit_solution(4438404987876690197)
XLA Ops:
  0.0 0.0 copy-start.7
  0.0 0.1 pad_add_fusion.1.meta
  0.1 1.3 shard_map.59
  1.4 13.3 %collective-permute-start.2 = (f32[3,64,256]{2,1,0:T(8,128)S(1)}, f32[3,64,256]{2,1,0:T(8,128)S(1)}, u32[]{:S(2)}, u32[]{:S(2)}) collective-permute-start(f32[3,64,256]{2,1,0:T(8,128)S(1)} %shard_map.59), channel_id=1, source_target_pairs={{256,1},{257,2},{258,3},{259,4},{260,5},{261,6},{262,7},{1,256},{2... | collective-permute-start | bytes 589832 | tf_op jit(solution)/shard_map/ppermute | solution.py:369
  14.7 0.0 copy-done.7
  14.7 0.0 copy-done.6
  14.7 0.0 copy-done.5
  14.8 34.5 %conditional.1 = (f32[11,32,256]{2,1,0:T(8,128)S(1)}, f32[11,32,256]{2,1,0:T(8,128)S(1)}, f32[2,8,64,256]{3,2,1,0:T(8,128)S(1)}, f32[608,256]{1,0:T(8,128)}, f32...) conditional(s32[]{:T(128)} %convert_element_type.3, () %tuple.13, ...), branch_computations={%region_0.1_spmd, %region_1.2_spmd} | conditional | flops 16 | bytes 16540080 | solution.py:408
  14.8 0.0 copy-start.4
  14.8 0.1 pad_add_fusion.meta
  14.9 1.5 branch_1_fun.5
  16.3 0.0 copy-start
  16.4 0.0 copy-start.2
  16.4 0.0 copy-done.4
  16.4 0.9 branch_1_fun.6
  17.2 3.2 %collective-permute-start = (f32[608,256]{1,0:T(8,128)S(1)}, f32[608,256]{1,0:T(8,128)}, u32[]{:S(2)}, u32[]{:S(2)}) collective-permute-start(f32[608,256]{1,0:T(8,128)S(1)} %get-tuple-element.22), channel_id=1, source_target_pairs={{0,8},{8,16},{16,24},{24,32},{32,40},{40,48},{48,56},{56,64},{64,7... | collective-permute-start | bytes 1867784 | tf_op jit(solution)/shard_map/cond/branch_1_fun/ppermute | solution.py:375
  20.4 4.2 %collective-permute-start.1 = (f32[608,256]{1,0:T(8,128)S(1)}, f32[608,256]{1,0:T(8,128)}, u32[]{:S(2)}, u32[]{:S(2)}) collective-permute-start(f32[608,256]{1,0:T(8,128)S(1)} %get-tuple-element.23), channel_id=1, source_target_pairs={{8,0},{16,8},{24,16},{32,24},{40,32},{48,40},{56,48},{64,56},{72,6... | collective-permute-start | bytes 1867784 | tf_op jit(solution)/shard_map/cond/branch_1_fun/ppermute | solution.py:375
  24.7 1.8 %all-gather.2 = f32[16,256]{1,0:T(8,128)S(1)} all-gather(f32[8,256]{1,0:T(8,128)S(1)} %branch_1_fun.8), channel_id=4, replica_groups=mesh['view'=2,'gz'=32,'gy'=8] {'view'}, dimensions={0}, use_global_device_ids=true | all-gather | bytes 24576 | tf_op jit(solution)/shard_map/cond/branch_1_fun/all_gather | solution.py:372
  26.5 2.5 %branch_1_fun.9 = (bf16[384,256]{1,0:T(8,128)(2,1)S(1)}, bf16[2,128,192]{2,1,0:T(8,128)(2,1)S(1)}, bf16[2,2,256,256]{3,2,1,0:T(8,128)(2,1)S(1)}, bf16[2,2,256,256]{3,2,1,0:T(8,128)(2,1)S(1)}, f32[16,256]{1,0:T(8,128)}) custom-call(s32[3]{0:T(128)S(1)} %pad_add_fusion.meta, f32[2,8,256]{2,1,0:T(8,128)S(1)} %bitcast.22), custom_call_target="tpu_custom_call" | custom-call | tf_op jit(solution)/shard_map/cond/branch_1_fun/pallas_call | solution.py:19
  29.0 2.2 %all-gather = f32[8,64,256]{2,1,0:T(8,128)S(1)} all-gather(f32[4,64,256]{2,1,0:T(8,128)S(1)} %get-tuple-element.20), channel_id=2, replica_groups=mesh['view'=2,'gz'=32,'gy'=8] {'view'}, dimensions={0}, use_global_device_ids=true | all-gather | bytes 786432 | tf_op jit(solution)/shard_map/cond/branch_1_fun/all_gather | solution.py:372
  31.2 0.0 copy-done
  31.2 0.0 copy-done.2
  31.2 2.2 %all-gather.1 = f32[8,64,256]{2,1,0:T(8,128)S(1)} all-gather(f32[4,64,256]{2,1,0:T(8,128)S(1)} %get-tuple-element.21), channel_id=3, replica_groups=mesh['view'=2,'gz'=32,'gy'=8] {'view'}, dimensions={0}, use_global_device_ids=true | all-gather | bytes 786432 | tf_op jit(solution)/shard_map/cond/branch_1_fun/all_gather | solution.py:372
  33.4 0.6 branch_1_fun.7
  34.0 15.3 %collective-permute-done = f32[608,256]{1,0:T(8,128)} collective-permute-done((f32[608,256]{1,0:T(8,128)S(1)}, f32[608,256]{1,0:T(8,128)}, u32[]{:S(2)}, u32[]{:S(2)}) %collective-permute-start) | collective-permute-done | bytes 622624 | tf_op jit(solution)/shard_map/cond/branch_1_fun/ppermute | solution.py:375
  49.3 0.0 collective-permute-done.1
  49.3 0.0 copy-done.1
  49.3 0.0 copy-done.3
  49.3 1.3 shard_map.63
  50.6 3.8 %shard_map.61 = (f32[2,11,96,256]{3,2,1,0:T(8,128)S(1)}, f32[2,3,64,256]{3,2,1,0:T(8,128)S(1)}) custom-call(f32[11,32,256]{2,1,0:T(8,128)S(1)} %get-tuple-element.64.e_a, f32[11,32,256]{2,1,0:T(8,128)S(1)} %get-tuple-element.65.e_b, f32[2,8,64,256]{3,2,1,0:T(8,128)S(1)} %get-tuple-element.69.obs, f32[608,256]{1,0:T(8,128)} %get-tuple-element.70.g_low, ...), custom_call_target="tpu_custom_call" | custom-call | tf_op jit(solution)/shard_map/pallas_call | solution.py:19
  54.4 0.0 collective-permute-done.2.far.f
  54.4 0.7 shard_map.60
  55.1 1.9 %collective-permute-start.3 = (f32[3,32,256]{2,1,0:T(8,128)S(1)}, f32[3,32,256]{2,1,0:T(8,128)S(1)}, u32[]{:S(2)}, u32[]{:S(2)}) collective-permute-start(f32[3,32,256]{2,1,0:T(8,128)S(1)} %get-tuple-element.67), channel_id=1, source_target_pairs={{0,8},{8,16},{16,24},{24,32},{32,40},{40,48},{48,56},{56,64},{64,7... | collective-permute-start | bytes 294920 | tf_op jit(solution)/shard_map/ppermute | solution.py:375
  57.1 5.5 %collective-permute-start.4 = (f32[3,32,256]{2,1,0:T(8,128)S(1)}, f32[3,32,256]{2,1,0:T(8,128)S(1)}, u32[]{:S(2)}, u32[]{:S(2)}) collective-permute-start(f32[3,32,256]{2,1,0:T(8,128)S(1)} %get-tuple-element.68), channel_id=1, source_target_pairs={{8,0},{16,8},{24,16},{32,24},{40,32},{48,40},{56,48},{64,56},{72,6... | collective-permute-start | bytes 294920 | tf_op jit(solution)/shard_map/ppermute | solution.py:375
  62.6 2.8 %all-gather.3 = f32[16,32,256]{2,1,0:T(8,128)S(1)} all-gather(f32[8,32,256]{2,1,0:T(8,128)S(1)} %shard_map.63), channel_id=5, replica_groups=mesh['view'=2,'gz'=32,'gy'=8] {'view'}, dimensions={0}, use_global_device_ids=true | all-gather | bytes 786432 | tf_op jit(solution)/shard_map/all_gather | solution.py:372
  65.3 0.0 collective-permute-done.3.f_low
  65.3 0.0 collective-permute-done.4.f_high
  65.3 2.9 %shard_map.62 = (f32[6,32,256]{2,1,0:T(8,128)S(1)}, f32[2,3,96,256]{3,2,1,0:T(8,128)S(1)}, f32[2,3,64,256]{3,2,1,0:T(8,128)S(1)}) custom-call(f32[3,64,256]{2,1,0:T(8,128)S(1)} %collective-permute-done.2.far.f, f32[3,32,256]{2,1,0:T(8,128)S(1)} %collective-permute-done.3.f_low, f32[3,32,256]{2,1,0:T(8,128)S(1)} %collective-permute-done.4.f_high, ...), custom_call_target="tpu_custom_call" | custom-call | tf_op jit(solution)/shard_map/pallas_call | solution.py:19
  68.2 6.2 %shard_map.64 = (f32[6,32,256]{2,1,0:T(8,128)S(1)}, f32[2,64,256]{2,1,0:T(8,128)S(1)}, f32[6,64,256]{2,1,0:T(8,128)S(1)}, f32[2,8,32,256]{3,2,1,0:T(8,128)S(1)}) custom-call(s32[3]{0:T(128)S(1)} %pad_add_fusion.1.meta, f32[2,11,96,256]{3,2,1,0:T(8,128)S(1)} %get-tuple-element.76.ze, f32[2,3,96,256]{3,2,1,0:T(8,128)S(1)} %get-tuple-element.79.zn, ...), custom_call_target="tpu_custom_call" | custom-call | tf_op jit(solution)/shard_map/pallas_call | solution.py:19
  74.4 1.9 %collective-permute-start.6 = (f32[6,32,256]{2,1,0:T(8,128)S(1)}, f32[6,32,256]{2,1,0:T(8,128)S(1)}, u32[]{:S(2)}, u32[]{:S(2)}) collective-permute-start(f32[6,32,256]{2,1,0:T(8,128)S(1)} %get-tuple-element.81.c_edge), channel_id=1, source_target_pairs={{256,1},{257,2},{258,3},{259,4},{260,5},{261,6},{262,7},{1,256},{2... | collective-permute-start | bytes 589832 | tf_op jit(solution)/shard_map/ppermute | solution.py:369
  76.3 12.4 %collective-permute-start.5 = (f32[6,32,256]{2,1,0:T(8,128)S(1)}, f32[6,32,256]{2,1,0:T(8,128)S(1)}, u32[]{:S(2)}, u32[]{:S(2)}) collective-permute-start(f32[6,32,256]{2,1,0:T(8,128)S(1)} %get-tuple-element.78.c_mid), channel_id=1, source_target_pairs={{256,1},{257,2},{258,3},{259,4},{260,5},{261,6},{262,7},{1,256},{2... | collective-permute-start | bytes 589832 | tf_op jit(solution)/shard_map/ppermute | solution.py:369
  88.7 3.3 %all-gather.4 = f32[12,64,256]{2,1,0:T(8,128)S(1)} all-gather(f32[6,64,256]{2,1,0:T(8,128)S(1)} %get-tuple-element.85.c_part), channel_id=6, replica_groups=mesh['view'=2,'gz'=32,'gy'=8] {'view'}, dimensions={0}, use_global_device_ids=true | all-gather | bytes 1179648 | tf_op jit(solution)/shard_map/all_gather | solution.py:372
  92.0 19.7 %collective-permute-done.5.got_mid._ = f32[6,32,256]{2,1,0:T(8,128)S(1)} collective-permute-done((f32[6,32,256]{2,1,0:T(8,128)S(1)}, f32[6,32,256]{2,1,0:T(8,128)S(1)}, u32[]{:S(2)}, u32[]{:S(2)}) %collective-permute-start.5) | collective-permute-done | bytes 196640 | tf_op jit(solution)/shard_map/ppermute | solution.py:369
  111.7 0.6 shard_map.66
  112.3 1.9 %collective-permute-start.10 = (f32[8,32,256]{2,1,0:T(8,128)S(1)}, f32[8,32,256]{2,1,0:T(8,128)S(1)}, u32[]{:S(2)}, u32[]{:S(2)}) collective-permute-start(f32[8,32,256]{2,1,0:T(8,128)S(1)} %get-tuple-element.86.e_a), channel_id=1, source_target_pairs={{8,0},{16,8},{24,16},{32,24},{40,32},{48,40},{56,48},{64,56},{72,6... | collective-permute-start | bytes 786440 | tf_op jit(solution)/shard_map/ppermute | solution.py:375
  114.3 3.4 %collective-permute-start.9 = (f32[8,32,256]{2,1,0:T(8,128)S(1)}, f32[8,32,256]{2,1,0:T(8,128)S(1)}, u32[]{:S(2)}, u32[]{:S(2)}) collective-permute-start(f32[8,32,256]{2,1,0:T(8,128)S(1)} %get-tuple-element.87.e_b), channel_id=1, source_target_pairs={{0,8},{8,16},{16,24},{24,32},{32,40},{40,48},{48,56},{56,64},{64,7... | collective-permute-start | bytes 786440 | tf_op jit(solution)/shard_map/ppermute | solution.py:375
  117.6 0.0 collective-permute-done.6.got_edge
  117.6 0.1 shard_map.65
  117.7 4.0 %collective-permute-start.8 = (f32[6,32,256]{2,1,0:T(8,128)S(1)}, f32[6,32,256]{2,1,0:T(8,128)S(1)}, u32[]{:S(2)}, u32[]{:S(2)}) collective-permute-start(f32[6,32,256]{2,1,0:T(8,128)S(1)} %get-tuple-element.82.f_a), channel_id=1, source_target_pairs={{8,0},{16,8},{24,16},{32,24},{40,32},{48,40},{56,48},{64,56},{72,6... | collective-permute-start | bytes 589832 | tf_op jit(solution)/shard_map/ppermute | solution.py:375
  121.8 2.4 %collective-permute-start.7 = (f32[6,32,256]{2,1,0:T(8,128)S(1)}, f32[6,32,256]{2,1,0:T(8,128)S(1)}, u32[]{:S(2)}, u32[]{:S(2)}) collective-permute-start(f32[6,32,256]{2,1,0:T(8,128)S(1)} %get-tuple-element.83.f_b), channel_id=1, source_target_pairs={{0,8},{8,16},{16,24},{24,32},{32,40},{40,48},{48,56},{56,64},{64,7... | collective-permute-start | bytes 589832 | tf_op jit(solution)/shard_map/ppermute | solution.py:375
  124.2 0.0 collective-permute-done.10.e_high
  124.2 0.0 collective-permute-done.9.e_low
  124.2 3.2 %shard_map.67 = (f32[2,6,96,256]{3,2,1,0:T(8,128)S(1)}, f32[2,2,64,256]{3,2,1,0:T(8,128)S(1)}) custom-call(s32[3]{0:T(128)S(1)} %pad_add_fusion.1.meta, f32[8,32,256]{2,1,0:T(8,128)S(1)} %get-tuple-element.86.e_a, f32[8,32,256]{2,1,0:T(8,128)S(1)} %get-tuple-element.87.e_b, f32[8,32,256]{2,1,0:T(8,128)S(1)} %collective-permute-done.9.e_low, ...), custom_call_target="tpu_custom_call" | custom-call | tf_op jit(solution)/shard_map/pallas_call | solution.py:19
  127.4 0.0 collective-permute-done.8.f_high
  127.5 2.8 %collective-permute-done.7.f_low = f32[6,32,256]{2,1,0:T(8,128)S(1)} collective-permute-done((f32[6,32,256]{2,1,0:T(8,128)S(1)}, f32[6,32,256]{2,1,0:T(8,128)S(1)}, u32[]{:S(2)}, u32[]{:S(2)}) %collective-permute-start.7) | collective-permute-done | bytes 196640 | tf_op jit(solution)/shard_map/ppermute | solution.py:375
  130.3 4.1 %shard_map.68 = (f32[3,64,256]{2,1,0:T(8,128)S(1)}, f32[2,6,96,256]{3,2,1,0:T(8,128)S(1)}, f32[2,3,64,256]{3,2,1,0:T(8,128)S(1)}) custom-call(s32[3]{0:T(128)S(1)} %pad_add_fusion.1.meta, f32[6,32,256]{2,1,0:T(8,128)S(1)} %get-tuple-element.82.f_a, f32[6,32,256]{2,1,0:T(8,128)S(1)} %get-tuple-element.83.f_b, f32[6,32,256]{2,1,0:T(8,128)S(1)} %collective-permute-done.7.f_low, ...), custom_call_target="tpu_custom_call" | custom-call | tf_op jit(solution)/shard_map/pallas_call | solution.py:19
  134.4 8.3 %collective-permute-start.11 = (f32[3,64,256]{2,1,0:T(8,128)S(1)}, f32[3,64,256]{2,1,0:T(8,128)S(1)}, u32[]{:S(2)}, u32[]{:S(2)}) collective-permute-start(f32[3,64,256]{2,1,0:T(8,128)S(1)} %get-tuple-element.94), channel_id=1, source_target_pairs={{256,1},{257,2},{258,3},{259,4},{260,5},{261,6},{262,7},{1,256},{2... | collective-permute-start | bytes 589832 | tf_op jit(solution)/shard_map/ppermute | solution.py:369
  142.6 3.8 %shard_map.69 = (f32[8,64,256]{2,1,0:T(8,128)S(1)}, f32[3,64,256]{2,1,0:T(8,128)S(1)}) custom-call(s32[3]{0:T(128)S(1)} %pad_add_fusion.1.meta, f32[2,6,96,256]{3,2,1,0:T(8,128)S(1)} %get-tuple-element.90.zn, f32[2,6,96,256]{3,2,1,0:T(8,128)S(1)} %get-tuple-element.89.ze, f32[2,3,64,256]{3,2,1,0:T(8,128)S(1)} %get-tuple-element.91.bx0, ...), custom_call_target="tpu_custom_call" | custom-call | tf_op jit(solution)/shard_map/pallas_call | solution.py:19
  146.4 6.5 %all-gather.6 = f32[6,64,256]{2,1,0:T(8,128)S(1)} all-gather(f32[3,64,256]{2,1,0:T(8,128)S(1)} %get-tuple-element.95), channel_id=8, replica_groups=mesh['view'=2,'gz'=32,'gy'=8] {'view'}, dimensions={0}, use_global_device_ids=true | all-gather | bytes 589824 | tf_op jit(solution)/shard_map/all_gather | solution.py:372
  153.0 0.6 shard_map.71
  153.6 2.3 %all-gather.7 = f32[10,64,256]{2,1,0:T(8,128)S(1)} all-gather(f32[5,64,256]{2,1,0:T(8,128)S(1)} %shard_map.71), channel_id=9, replica_groups=mesh['view'=2,'gz'=32,'gy'=8] {'view'}, dimensions={0}, use_global_device_ids=true | all-gather | bytes 983040 | tf_op jit(solution)/shard_map/all_gather | solution.py:372
  155.8 0.0 collective-permute-done.11.got
  155.9 19.7 %all-gather.5 = f32[6,64,256]{2,1,0:T(8,128)S(1)} all-gather(f32[3,64,256]{2,1,0:T(8,128)S(1)} %shard_map.70), channel_id=7, replica_groups=mesh['view'=2,'gz'=32,'gy'=8] {'view'}, dimensions={0}, use_global_device_ids=true | all-gather | bytes 589824 | tf_op jit(solution)/shard_map/all_gather | solution.py:372
  175.5 1.7 shard_map.72
  (6 shorter events, 0.0 us)
Async XLA Ops:
  0.0 14.7 %copy-start.7 = (f32[1,7]{1,0:T(1,128)S(1)}, f32[1,7]{1,0:T(1,128)}, u32[]{:S(2)}) copy-start(f32[1,7]{1,0:T(1,128)} %param.11) | copy-start | bytes 88
  0.0 14.7 %copy-start.6 = (f32[1,7]{1,0:T(1,128)S(1)}, f32[1,7]{1,0:T(1,128)}, u32[]{:S(2)}) copy-start(f32[1,7]{1,0:T(1,128)} %param.10) | copy-start | bytes 88
  0.0 14.7 %copy-start.5 = (f32[1,31]{1,0:T(1,128)S(1)}, f32[1,31]{1,0:T(1,128)}, u32[]{:S(2)}) copy-start(f32[1,31]{1,0:T(1,128)} %param.9) | copy-start | bytes 376
  1.4 53.0 %collective-permute-start.2 = (f32[3,64,256]{2,1,0:T(8,128)S(1)}, f32[3,64,256]{2,1,0:T(8,128)S(1)}, u32[]{:S(2)}, u32[]{:S(2)}) collective-permute-start(f32[3,64,256]{2,1,0:T(8,128)S(1)} %shard_map.59), channel_id=1, source_target_pairs={{256,1},{257,2},{258,3},{259,4},{260,5},{261,6},{262,7},{1,256},{2... | collective-permute-start | bytes 589832 | tf_op jit(solution)/shard_map/ppermute | solution.py:369
  14.8 1.6 copy-start.4
  16.3 14.9 %copy-start = (f32[11,32,256]{2,1,0:T(8,128)}, f32[11,32,256]{2,1,0:T(8,128)S(1)}, u32[]{:S(2)}) copy-start(f32[11,32,256]{2,1,0:T(8,128)S(1)} %get-tuple-element.116.e_b) | copy-start | bytes 1081348 | tf_op jit(solution)/shard_map/cond
  16.4 14.9 %copy-start.2 = (f32[11,32,256]{2,1,0:T(8,128)}, f32[11,32,256]{2,1,0:T(8,128)S(1)}, u32[]{:S(2)}) copy-start(f32[11,32,256]{2,1,0:T(8,128)S(1)} %get-tuple-element.115.e_a) | copy-start | bytes 1081348 | tf_op jit(solution)/shard_map/cond
  17.2 32.1 %collective-permute-start = (f32[608,256]{1,0:T(8,128)S(1)}, f32[608,256]{1,0:T(8,128)}, u32[]{:S(2)}, u32[]{:S(2)}) collective-permute-start(f32[608,256]{1,0:T(8,128)S(1)} %get-tuple-element.22), channel_id=1, source_target_pairs={{0,8},{8,16},{16,24},{24,32},{32,40},{40,48},{48,56},{56,64},{64,7... | collective-permute-start | bytes 1867784 | tf_op jit(solution)/shard_map/cond/branch_1_fun/ppermute | solution.py:375
  20.4 28.8 %collective-permute-start.1 = (f32[608,256]{1,0:T(8,128)S(1)}, f32[608,256]{1,0:T(8,128)}, u32[]{:S(2)}, u32[]{:S(2)}) collective-permute-start(f32[608,256]{1,0:T(8,128)S(1)} %get-tuple-element.23), channel_id=1, source_target_pairs={{8,0},{16,8},{24,16},{32,24},{40,32},{48,40},{56,48},{64,56},{72,6... | collective-permute-start | bytes 1867784 | tf_op jit(solution)/shard_map/cond/branch_1_fun/ppermute | solution.py:375
  33.4 15.9 %copy-start.1 = (f32[11,32,256]{2,1,0:T(8,128)S(1)}, f32[11,32,256]{2,1,0:T(8,128)}, u32[]{:S(2)}) copy-start(f32[11,32,256]{2,1,0:T(8,128)} %copy-done) | copy-start | bytes 1081348 | tf_op jit(solution)/shard_map/cond
  33.4 15.9 %copy-start.3 = (f32[11,32,256]{2,1,0:T(8,128)S(1)}, f32[11,32,256]{2,1,0:T(8,128)}, u32[]{:S(2)}) copy-start(f32[11,32,256]{2,1,0:T(8,128)} %copy-done.2) | copy-start | bytes 1081348 | tf_op jit(solution)/shard_map/cond
  55.1 10.2 %collective-permute-start.3 = (f32[3,32,256]{2,1,0:T(8,128)S(1)}, f32[3,32,256]{2,1,0:T(8,128)S(1)}, u32[]{:S(2)}, u32[]{:S(2)}) collective-permute-start(f32[3,32,256]{2,1,0:T(8,128)S(1)} %get-tuple-element.67), channel_id=1, source_target_pairs={{0,8},{8,16},{16,24},{24,32},{32,40},{40,48},{48,56},{56,64},{64,7... | collective-permute-start | bytes 294920 | tf_op jit(solution)/shard_map/ppermute | solution.py:375
  57.1 8.2 %collective-permute-start.4 = (f32[3,32,256]{2,1,0:T(8,128)S(1)}, f32[3,32,256]{2,1,0:T(8,128)S(1)}, u32[]{:S(2)}, u32[]{:S(2)}) collective-permute-start(f32[3,32,256]{2,1,0:T(8,128)S(1)} %get-tuple-element.68), channel_id=1, source_target_pairs={{8,0},{16,8},{24,16},{32,24},{40,32},{48,40},{56,48},{64,56},{72,6... | collective-permute-start | bytes 294920 | tf_op jit(solution)/shard_map/ppermute | solution.py:375
  74.4 43.2 %collective-permute-start.6 = (f32[6,32,256]{2,1,0:T(8,128)S(1)}, f32[6,32,256]{2,1,0:T(8,128)S(1)}, u32[]{:S(2)}, u32[]{:S(2)}) collective-permute-start(f32[6,32,256]{2,1,0:T(8,128)S(1)} %get-tuple-element.81.c_edge), channel_id=1, source_target_pairs={{256,1},{257,2},{258,3},{259,4},{260,5},{261,6},{262,7},{1,256},{2... | collective-permute-start | bytes 589832 | tf_op jit(solution)/shard_map/ppermute | solution.py:369
  76.3 35.4 %collective-permute-start.5 = (f32[6,32,256]{2,1,0:T(8,128)S(1)}, f32[6,32,256]{2,1,0:T(8,128)S(1)}, u32[]{:S(2)}, u32[]{:S(2)}) collective-permute-start(f32[6,32,256]{2,1,0:T(8,128)S(1)} %get-tuple-element.78.c_mid), channel_id=1, source_target_pairs={{256,1},{257,2},{258,3},{259,4},{260,5},{261,6},{262,7},{1,256},{2... | collective-permute-start | bytes 589832 | tf_op jit(solution)/shard_map/ppermute | solution.py:369
  112.3 11.9 %collective-permute-start.10 = (f32[8,32,256]{2,1,0:T(8,128)S(1)}, f32[8,32,256]{2,1,0:T(8,128)S(1)}, u32[]{:S(2)}, u32[]{:S(2)}) collective-permute-start(f32[8,32,256]{2,1,0:T(8,128)S(1)} %get-tuple-element.86.e_a), channel_id=1, source_target_pairs={{8,0},{16,8},{24,16},{32,24},{40,32},{48,40},{56,48},{64,56},{72,6... | collective-permute-start | bytes 786440 | tf_op jit(solution)/shard_map/ppermute | solution.py:375
  114.3 9.9 %collective-permute-start.9 = (f32[8,32,256]{2,1,0:T(8,128)S(1)}, f32[8,32,256]{2,1,0:T(8,128)S(1)}, u32[]{:S(2)}, u32[]{:S(2)}) collective-permute-start(f32[8,32,256]{2,1,0:T(8,128)S(1)} %get-tuple-element.87.e_b), channel_id=1, source_target_pairs={{0,8},{8,16},{16,24},{24,32},{32,40},{40,48},{48,56},{56,64},{64,7... | collective-permute-start | bytes 786440 | tf_op jit(solution)/shard_map/ppermute | solution.py:375
  117.7 9.7 %collective-permute-start.8 = (f32[6,32,256]{2,1,0:T(8,128)S(1)}, f32[6,32,256]{2,1,0:T(8,128)S(1)}, u32[]{:S(2)}, u32[]{:S(2)}) collective-permute-start(f32[6,32,256]{2,1,0:T(8,128)S(1)} %get-tuple-element.82.f_a), channel_id=1, source_target_pairs={{8,0},{16,8},{24,16},{32,24},{40,32},{48,40},{56,48},{64,56},{72,6... | collective-permute-start | bytes 589832 | tf_op jit(solution)/shard_map/ppermute | solution.py:375
  121.8 8.5 %collective-permute-start.7 = (f32[6,32,256]{2,1,0:T(8,128)S(1)}, f32[6,32,256]{2,1,0:T(8,128)S(1)}, u32[]{:S(2)}, u32[]{:S(2)}) collective-permute-start(f32[6,32,256]{2,1,0:T(8,128)S(1)} %get-tuple-element.83.f_b), channel_id=1, source_target_pairs={{0,8},{8,16},{16,24},{24,32},{32,40},{40,48},{48,56},{56,64},{64,7... | collective-permute-start | bytes 589832 | tf_op jit(solution)/shard_map/ppermute | solution.py:375
  134.4 21.5 %collective-permute-start.11 = (f32[3,64,256]{2,1,0:T(8,128)S(1)}, f32[3,64,256]{2,1,0:T(8,128)S(1)}, u32[]{:S(2)}, u32[]{:S(2)}) collective-permute-start(f32[3,64,256]{2,1,0:T(8,128)S(1)} %get-tuple-element.94), channel_id=1, source_target_pairs={{256,1},{257,2},{258,3},{259,4},{260,5},{261,6},{262,7},{1,256},{2... | collective-permute-start | bytes 589832 | tf_op jit(solution)/shard_map/ppermute | solution.py:369

commit v3 on v1

v3 whole, which is shorter than its diff:
```python
import jax
import jax.numpy as jnp
from jax import lax
from jax.experimental import pallas as pl
from jax.experimental.pallas import tpu as pltpu
from jax.sharding import PartitionSpec as P

F32 = jnp.float32
BF16 = jnp.bfloat16
NX = 256
LIMIT = 20 * 1024 * 1024
VM = pl.BlockSpec(memory_space=pltpu.VMEM)
SM = pl.BlockSpec(memory_space=pltpu.SMEM)


def call(body, outs, *args, smem=1, flops=0, scratch=()):
    size = sum(a.size * a.dtype.itemsize for a in args)
    size += sum(4 * o.size for o in outs)
    return pl.pallas_call(
        body,
        out_shape=outs,
        in_specs=[SM] * smem + [VM] * (len(args) - smem),
        out_specs=[VM] * len(outs),
        scratch_shapes=list(scratch),
        compiler_params=pltpu.CompilerParams(vmem_limit_bytes=LIMIT),
        cost_estimate=pl.CostEstimate(flops=0, bytes_accessed=0, transcendentals=0),
    )(*args)


def f32(*shape):
    return jax.ShapeDtypeStruct(shape, F32)


def b16(*shape):
    return jax.ShapeDtypeStruct(shape, BF16)


def parts(x):
    high = x.astype(BF16)
    return high, (x - high.astype(F32)).astype(BF16)


def dot(a, b):
    return jnp.dot(a, b, preferred_element_type=F32)


def rows_of(ref, half):
    return jnp.swapaxes(ref[:, 8 * half : 8 * half + 8, :], 0, 1)


def by_core(meta, body):
    for core in range(2):
        pl.when(meta[0] == core)(lambda core=core: body(core, lambda r: r % 8 if core == 0 else 7 - r % 8))


def far_body(meta, start, out):
    def body(core, at):
        rows = rows_of(start, core)
        for j in range(3):
            out[j] = rows[at(j)]

    by_core(meta, body)


def start_body(meta, start, e_a, e_b):
    def body(core, at):
        rows = (rows_of(start, core), rows_of(start, 1 - core))
        for j in range(11):
            e_a[j] = rows[j // 8][at(j), :32]
            e_b[j] = rows[j // 8][at(j), 32:]

    by_core(meta, body)


def observed_body(meta, observed, mine, send_a, send_b):
    def body(core, at):
        rows, others = rows_of(observed, core), rows_of(observed, 1 - core)
        for j in range(8):
            mine[j] = rows[at(j)]
            if j < 4:
                send_a[j] = others[at(15 - j)]
            else:
                send_b[j - 4] = others[at(15 - j)]

    by_core(meta, body)


def profiles_body(sz, sy, sx, out):
    out[...] = jnp.zeros((8, NX), F32)
    out[0:1, 0:31] = sz[...]
    out[1:2, 0:7] = sy[...]
    out[2:3, 0:7] = sx[...]


def edges_body(meta, mine, got_a, got_b, obs, low, high):
    other = 1 - meta[0]
    for j in range(8):
        for v, row in ((meta[0], mine[j]), (other, got_a[other, j] if j < 4 else got_b[other, j - 4])):
            obs[v, j] = row
            low[v, j] = row[0:16]
            high[v, j] = row[48:64]


def faces_body(far, _, first, last):
    for j in range(3):
        first[j] = far[j, 0:32]
        last[j] = far[j, 32:64]


def weights_body(meta, both, zf, zb, xf, xb, yw):
    def band(shape, row, taps, place):
        d = lax.broadcasted_iota(jnp.int32, shape, 1) - lax.broadcasted_iota(jnp.int32, shape, 0)
        total = jnp.zeros(shape, F32)
        for t in range(taps):
            total = jnp.where(d == place(t), row[:, t : t + 1], total)
        return total

    for v in range(2):
        w = both[v]
        sums = jnp.sum(w, axis=1, keepdims=True)
        w = w / sums_or_one(sums)
        wz, wy, wx = w[0:1], w[1:2], w[2:3]
        high, low = parts(band((96, 128), wz, 31, lambda t: t + 1))
        zf[192 * v : 192 * v + 96, 0:128] = high
        zf[192 * v : 192 * v + 96, 128:256] = high
        zf[192 * v + 96 : 192 * v + 192, 0:128] = low
        zf[192 * v + 96 : 192 * v + 192, 128:256] = jnp.zeros((96, 128), BF16)
        high, low = parts(band((64, 96), wz, 31, lambda t: 31 - t))
        zb[v, 0:64] = jnp.concatenate([high, high], axis=1)
        zb[v, 64:128] = jnp.concatenate([low, jnp.zeros((64, 96), BF16)], axis=1)
        high, low = parts(band((256, 256), wx, 7, lambda t: 3 - t))
        xf[v, 0] = high
        xf[v, 1] = low
        high, low = parts(band((256, 256), wx, 7, lambda t: t - 3))
        xb[v, 0] = high
        xb[v, 1] = low
        for core in range(2):

            @pl.when(meta[0] == core)
            def _(core=core, v=v, wy=wy):
                for t in range(7):
                    s = t if core == 0 else 6 - t
                    yw[8 * v + t : 8 * v + t + 1, :] = jnp.broadcast_to(wy[:, s : s + 1], (1, NX))

        yw[8 * v + 7 : 8 * v + 8, :] = jnp.zeros((1, NX), F32)


def sums_or_one(sums):
    rows = lax.broadcasted_iota(jnp.int32, sums.shape, 0)
    return jnp.where(rows < 3, sums, 1.0)


def blur_z(zf, low, a, b, high):
    highs, lows = zip(*[parts(x) for x in (low, a, b, high)])
    both = dot(zf[...], jnp.concatenate(highs + lows, axis=0))
    return [both[192 * v : 192 * v + 96] + both[192 * v + 96 : 192 * v + 192] for v in range(2)]


def blur_x(x, weight, v):
    high, low = parts(x)
    return dot(high, weight[v, 0]) + dot(low, weight[v, 0]) + dot(high, weight[v, 1])


def row_result(meta, rows, recorded, yw, xf, xb, zb, v):
    total = yw[8 * v : 8 * v + 1] * rows[0]
    for t in range(1, 7):
        total = total + yw[8 * v + t : 8 * v + t + 1] * rows[t]
    blurred = blur_x(total, xf, v)
    at = lax.broadcasted_iota(jnp.int32, blurred.shape, 0)
    inside = (at >= meta[1]) & (at < meta[2])
    quotient = recorded / jnp.where(inside, blurred, 1.0)
    high, low = parts(quotient)
    both = dot(zb[v], jnp.concatenate([high, low], axis=0))
    return blur_x(both[0:64] + both[64:128], xb, v)


def recorded_row(obs, o_low, o_high, j, v):
    return jnp.concatenate([o_low[v, j], obs[v, j], o_high[v, j]], axis=0)


def spread_back(yw, terms, row, planes=slice(0, 64)):
    total = None
    for v in range(2):
        for t in range(7):
            j = row + t - 3
            if 0 <= j <= 7:
                term = yw[8 * v + 6 - t : 8 * v + 7 - t] * terms(v, j)[planes]
                total = term if total is None else total + term
    return total


def early1_body(e_a, e_b, e_low, e_high, zf, ze):
    for r in range(11):
        for v, x in enumerate(blur_z(zf, e_low[r], e_a[r], e_b[r], e_high[r])):
            ze[v, r] = x


def middle1_body(meta, ze, obs, o_low, o_high, zb, xf, xb, yw, bx):
    for j in range(3, 8):
        for v in range(2):
            rec = recorded_row(obs, o_low, o_high, j, v)
            bx[v, j - 3] = row_result(meta, [ze[v, j - 3 + t] for t in range(7)], rec, yw, xf, xb, zb, v)


def late1_body(meta, f, f_low, f_high, ze, bx, obs, o_low, o_high, zf, zb, xf, xb, yw,
               c_far, c_mid, c_part, buf, new):
    for j in range(3):
        for v, x in enumerate(blur_z(zf, f_low[j], f[j, :32], f[j, 32:], f_high[j])):
            buf[v, 2 - j] = x
    for j in range(3):
        for v in range(2):
            rows = [buf[v, j + t] if j + t < 3 else ze[v, j + t - 3] for t in range(7)]
            rec = recorded_row(obs, o_low, o_high, j, v)
            new[v, j] = row_result(meta, rows, rec, yw, xf, xb, zb, v)

    def terms(v, j):
        return new[v, j] if j < 3 else bx[v, j - 3]

    for row in range(-3, 11):
        total = spread_back(yw, terms, row)
        if row < 3:
            c_far[row + 3] = total
        elif row < 5:
            c_mid[row - 3] = total
        else:
            c_part[row - 5] = total


def update_mid_body(meta, e_a, e_b, c_mid, c_part, got, out_a, out_b):
    for r in range(3, 11):
        c = c_mid[r - 3] if r < 5 else c_part[r - 5] + got[1 - meta[0], 10 - r]
        out_a[r - 3] = e_a[r] * (0.5 * c[:32])
        out_b[r - 3] = e_b[r] * (0.5 * c[32:])


def update_far_body(far, e_a, e_b, c, got, out_a, out_b):
    for r in range(-3, 3):
        factor = 0.5 * (c[r + 3] + got[2 - r])
        out_a[r + 3] = (far[-1 - r, :32] if r < 0 else e_a[r]) * factor[:32]
        out_b[r + 3] = (far[-1 - r, 32:] if r < 0 else e_b[r]) * factor[32:]


def early2_body(meta, e_a, e_b, e_low, e_high, obs, o_low, o_high, zf, zb, xf, xb, yw, ze, bx, buf):
    for r in range(8):
        for v, x in enumerate(blur_z(zf, e_low[r], e_a[r], e_b[r], e_high[r])):
            buf[v, r] = x
            if r < 6:
                ze[v, r] = x
    for j in (6, 7):
        for v in range(2):
            rec = recorded_row(obs, o_low, o_high, j, v)
            bx[v, j - 6] = row_result(meta, [buf[v, j - 6 + t] for t in range(7)], rec, yw, xf, xb, zb, v)


def late2_body(meta, f_a, f_b, f_low, f_high, ze, obs, o_low, o_high, zf, zb, xf, xb, yw,
               c_far, zn, bx):
    for r in range(6):
        for v, x in enumerate(blur_z(zf, f_low[r], f_a[r], f_b[r], f_high[r])):
            zn[v, r] = x
    for j in range(3):
        for v in range(2):
            rows = [zn[v, j + t] if j + t < 6 else ze[v, j + t - 6] for t in range(7)]
            rec = recorded_row(obs, o_low, o_high, j, v)
            bx[v, j] = row_result(meta, rows, rec, yw, xf, xb, zb, v)
    for k in range(3):
        c_far[k] = spread_back(yw, lambda v, j: bx[v, j] if j < 3 else None, -1 - k)


def rest2_body(meta, zn, ze, bx0, bx6, obs, o_low, o_high, zb, xf, xb, yw, c_own, c_part, new):
    for j in range(3, 6):
        for v in range(2):
            rows = [zn[v, j + t] if j + t < 6 else ze[v, j + t - 6] for t in range(7)]
            rec = recorded_row(obs, o_low, o_high, j, v)
            new[v, j - 3] = row_result(meta, rows, rec, yw, xf, xb, zb, v)

    def terms(v, j):
        return bx0[v, j] if j < 3 else new[v, j - 3] if j < 6 else bx6[v, j - 6]

    for row in range(11):
        total = spread_back(yw, terms, row)
        if row < 8:
            c_own[row] = total
        else:
            c_part[row - 8] = total


def final_mid_body(meta, e_a, e_b, c_own, got, out):
    for r in range(3, 8):
        c = c_own[r] if r < 5 else c_own[r] + got[1 - meta[0], 7 - r]
        out[r - 3, :32] = e_a[r - 3] * (0.5 * c[:32])
        out[r - 3, 32:] = e_b[r - 3] * (0.5 * c[32:])


def final_far_body(f_a, f_b, c_own, got, out):
    for r in range(3):
        c = c_own[r] + got[r]
        out[r, :32] = f_a[r + 3] * (0.5 * c[:32])
        out[r, 32:] = f_b[r + 3] * (0.5 * c[32:])


def output_body(meta, far, mid, out):
    def body(core, at):
        for c in range(2):
            block = [far[c, r] if r < 3 else mid[c, r - 3] for r in range(8)]
            block = block if c == 0 else block[::-1]
            out[:, 8 * c : 8 * c + 8, :] = jnp.swapaxes(jnp.stack(block), 0, 1)

    body(0, None)


def on_device(observed, start, spread_z, spread_y, spread_x):
    gy, gz = lax.axis_size("gy"), lax.axis_size("gz")
    across = [(gy + g, g + 1) for g in range(gy - 1)]
    across += [(b, a) for a, b in across]
    up = [(i, i + 1) for i in range(gz - 1)]
    down = [(j, i) for i, j in up]

    def far(x):
        return lax.ppermute(x, ("view", "gy"), across)

    def both(x):
        return lax.all_gather(x, "view")

    def along_z(first, last):
        return lax.ppermute(last, "gz", up), lax.ppermute(first, "gz", down)

    at = lax.axis_index("gz")
    meta = jnp.stack(
        [lax.axis_index("view"), jnp.where(at == 0, 16, 0), jnp.where(at == gz - 1, 80, 96)]
    ).astype(jnp.int32)
    recorded = observed[0]

    (send_far,) = call(far_body, [f32(3, 64, NX)], meta, start)
    f = far(send_far)
    e_a, e_b = call(start_body, [f32(11, 32, NX)] * 2, meta, start)
    e_low, e_high = along_z(e_a, e_b)
    mine, send_a, send_b = call(
        observed_body, [f32(8, 64, NX), f32(4, 64, NX), f32(4, 64, NX)], meta, recorded
    )
    obs, o_first, o_last = call(
        edges_body, [f32(2, 8, 64, NX), f32(2, 8, 16, NX), f32(2, 8, 16, NX)],
        meta, mine, both(send_a), both(send_b),
    )
    o_low, o_high = along_z(o_first, o_last)
    (profiles,) = call(profiles_body, [f32(8, NX)], spread_z, spread_y, spread_x, smem=0)
    zf, zb, xf, xb, yw = call(
        weights_body,
        [b16(384, 256), b16(2, 128, 192), b16(2, 2, 256, 256), b16(2, 2, 256, 256), f32(16, NX)],
        meta, both(profiles),
    )
    obs = (obs, o_low, o_high)
    (ze,) = call(early1_body, [f32(2, 11, 96, NX)], e_a, e_b, e_low, e_high, zf, smem=0)
    f_low, f_high = along_z(*call(faces_body, [f32(3, 32, NX)] * 2, f, ze, smem=0))
    (bx,) = call(middle1_body, [f32(2, 5, 64, NX)], meta, ze, *obs, zb, xf, xb, yw)
    c_far, c_mid, c_part = call(
        late1_body, [f32(6, 64, NX), f32(2, 64, NX), f32(6, 64, NX)],
        meta, f, f_low, f_high, ze, bx, *obs, zf, zb, xf, xb, yw,
        scratch=[pltpu.VMEM((2, 3, 96, NX), F32), pltpu.VMEM((2, 3, 64, NX), F32)],
    )
    got_far = far(c_far)
    got = both(c_part)
    m_a, m_b = call(update_mid_body, [f32(8, 32, NX)] * 2, meta, e_a, e_b, c_mid, c_part, got)
    m_low, m_high = along_z(m_a, m_b)
    ze, bx6 = call(
        early2_body, [f32(2, 6, 96, NX), f32(2, 2, 64, NX)],
        meta, m_a, m_b, m_low, m_high, *obs, zf, zb, xf, xb, yw,
        scratch=[pltpu.VMEM((2, 8, 96, NX), F32)],
    )
    n_a, n_b = call(update_far_body, [f32(6, 32, NX)] * 2, f, e_a, e_b, c_far, got_far, smem=0)
    n_low, n_high = along_z(n_a, n_b)
    c_far, zn, bx0 = call(
        late2_body, [f32(3, 64, NX), f32(2, 6, 96, NX), f32(2, 3, 64, NX)],
        meta, n_a, n_b, n_low, n_high, ze, *obs, zf, zb, xf, xb, yw,
    )
    got_far = far(c_far)
    c_own, c_part = call(
        rest2_body, [f32(8, 64, NX), f32(3, 64, NX)],
        meta, zn, ze, bx0, bx6, *obs, zb, xf, xb, yw,
        scratch=[pltpu.VMEM((2, 3, 64, NX), F32)],
    )
    got_part = both(c_part)
    (mid,) = call(final_mid_body, [f32(5, 64, NX)], meta, m_a, m_b, c_own, got_part)
    other_mid = both(mid)
    (last,) = call(final_far_body, [f32(3, 64, NX)], n_a, n_b, c_own, got_far, smem=0)
    other_last = both(last)
    (out,) = call(output_body, [f32(64, 16, NX)], meta, other_last, other_mid)
    return out


def solution(mesh):
    return jax.shard_map(
        on_device,
        mesh=mesh,
        in_specs=(
            P("view", "gz", "gy", None),
            P("gz", "gy", None),
            P("view", None),
            P("view", None),
            P("view", None),
        ),
        out_specs=P("gz", "gy", None),
        check_vma=False,
    )
```

time: 204 us -> 153 us (0.75)
  the two profiles are of different devices: /device:TPU:37 before, /device:TPU:29 now
where the time goes in v3:
time: 153 us; the launch traced here: 152 us
  starting transfers between devices  57.9 us (38%)
  waiting for transfers between devices  41.7 us (27%)
  blocking collectives  28.4 us (19%)
  Pallas kernels  22.7 us (15%)
    ppermute x3, waiting for transfers between devices, far(): return lax.ppermute(x, ('view', 'gy'), across)  36 us
    ppermute x10, starting transfers between devices, along_z(): return (lax.ppermute(last, 'gz', up), lax.ppermute(first, 'gz', down))  33.3 us
    all_gather x7, blocking collectives, both(): return lax.all_gather(x, 'view')  28.4 us
    ppermute x3, starting transfers between devices, far(): return lax.ppermute(x, ('view', 'gy'), across)  24.6 us
    pallas_call x18, Pallas kernels, call(): pl.pallas_call(body, out_shape=outs, in_specs=[SM] * smem + [VM] * (len(a...  22.7 us
    ppermute x10, waiting for transfers between devices, along_z(): return (lax.ppermute(last, 'gz', up), lax.ppermute(first, 'gz', down))  5.7 us
  transfers between devices with their start and end apart: 13, of which 6 were waited for; matrix products, arithmetic and copies ran while one was open for 0% of the time, Pallas kernels for 9%

profile of v3, /device:TPU:29, one launch (start us, length us, event | category | flops | bytes accessed | tf_op | source)
XLA Modules:
  0.0 152.2 jit_solution(6075876203703477277)
XLA Ops:
  0.0 0.1 pad_add_fusion.meta
  0.1 0.0 copy-start
  0.1 1.2 copy-done
  1.3 0.0 copy-start.1
  1.3 0.6 shard_map.55
  1.9 16.0 %collective-permute-start = (f32[3,64,256]{2,1,0:T(8,128)S(1)}, f32[3,64,256]{2,1,0:T(8,128)S(1)}, u32[]{:S(2)}, u32[]{:S(2)}) collective-permute-start(f32[3,64,256]{2,1,0:T(8,128)S(1)} %shard_map.55), channel_id=1, source_target_pairs={{256,1},{257,2},{258,3},{259,4},{260,5},{261,6},{262,7},{1,256},{2... | collective-permute-start | bytes 589832 | tf_op jit(solution)/shard_map/ppermute | solution.py:319
  17.9 0.7 shard_map.56
  18.7 2.4 %collective-permute-start.2 = (f32[11,32,256]{2,1,0:T(8,128)S(1)}, f32[11,32,256]{2,1,0:T(8,128)S(1)}, u32[]{:S(2)}, u32[]{:S(2)}) collective-permute-start(f32[11,32,256]{2,1,0:T(8,128)S(1)} %get-tuple-element.34.e_a), channel_id=1, source_target_pairs={{8,0},{16,8},{24,16},{32,24},{40,32},{48,40},{56,48},{64,56},{72,6... | collective-permute-start | bytes 1081352 | tf_op jit(solution)/shard_map/ppermute | solution.py:325
  21.0 5.0 %collective-permute-start.1 = (f32[11,32,256]{2,1,0:T(8,128)S(1)}, f32[11,32,256]{2,1,0:T(8,128)S(1)}, u32[]{:S(2)}, u32[]{:S(2)}) collective-permute-start(f32[11,32,256]{2,1,0:T(8,128)S(1)} %get-tuple-element.35.e_b), channel_id=1, source_target_pairs={{0,8},{8,16},{16,24},{24,32},{32,40},{40,48},{48,56},{56,64},{64,7... | collective-permute-start | bytes 1081352 | tf_op jit(solution)/shard_map/ppermute | solution.py:325
  26.1 0.0 copy-done.1
  26.1 0.8 shard_map.61
  26.9 2.2 %all-gather.1 = f32[8,64,256]{2,1,0:T(8,128)S(1)} all-gather(f32[4,64,256]{2,1,0:T(8,128)S(1)} %get-tuple-element.40), channel_id=3, replica_groups=mesh['view'=2,'gz'=32,'gy'=8] {'view'}, dimensions={0}, use_global_device_ids=true | all-gather | bytes 786432 | tf_op jit(solution)/shard_map/all_gather | solution.py:322
  29.1 0.0 copy-start.2
  29.1 0.0 copy-start.3
  29.1 0.0 copy-start.4
  29.1 2.3 %all-gather.2 = f32[8,64,256]{2,1,0:T(8,128)S(1)} all-gather(f32[4,64,256]{2,1,0:T(8,128)S(1)} %get-tuple-element.41), channel_id=4, replica_groups=mesh['view'=2,'gz'=32,'gy'=8] {'view'}, dimensions={0}, use_global_device_ids=true | all-gather | bytes 786432 | tf_op jit(solution)/shard_map/all_gather | solution.py:322
  31.4 0.6 shard_map.62
  32.0 1.9 %collective-permute-start.5 = (f32[2,8,16,256]{3,2,1,0:T(8,128)S(1)}, f32[2,8,16,256]{3,2,1,0:T(8,128)S(1)}, u32[]{:S(2)}, u32[]{:S(2)}) collective-permute-start(f32[2,8,16,256]{3,2,1,0:T(8,128)S(1)} %get-tuple-element.43), channel_id=1, source_target_pairs={{0,8},{8,16},{16,24},{24,32},{32,40},{40,48},{48,56},{56,64},{64,7... | collective-permute-start | bytes 786440 | tf_op jit(solution)/shard_map/ppermute | solution.py:325
  34.0 3.4 %collective-permute-start.6 = (f32[2,8,16,256]{3,2,1,0:T(8,128)S(1)}, f32[2,8,16,256]{3,2,1,0:T(8,128)S(1)}, u32[]{:S(2)}, u32[]{:S(2)}) collective-permute-start(f32[2,8,16,256]{3,2,1,0:T(8,128)S(1)} %get-tuple-element.44), channel_id=1, source_target_pairs={{8,0},{16,8},{24,16},{32,24},{40,32},{48,40},{56,48},{64,56},{72,6... | collective-permute-start | bytes 786440 | tf_op jit(solution)/shard_map/ppermute | solution.py:325
  37.3 0.0 copy-done.2
  37.3 0.0 copy-done.3
  37.3 0.0 copy-done.4
  37.4 2.4 %all-gather = f32[16,256]{1,0:T(8,128)S(1)} all-gather(f32[8,256]{1,0:T(8,128)S(1)} %shard_map.57), channel_id=2, replica_groups=mesh['view'=2,'gz'=32,'gy'=8] {'view'}, dimensions={0}, use_global_device_ids=true | all-gather | bytes 24576 | tf_op jit(solution)/shard_map/all_gather | solution.py:322
  39.8 1.8 %shard_map.58 = (bf16[384,256]{1,0:T(8,128)(2,1)S(1)}, bf16[2,128,192]{2,1,0:T(8,128)(2,1)S(1)}, bf16[2,2,256,256]{3,2,1,0:T(8,128)(2,1)S(1)}, bf16[2,2,256,256]{3,2,1,0:T(8,128)(2,1)S(1)}, f32[16,256]{1,0:T(8,128)S(1)}) custom-call(s32[3]{0:T(128)S(1)} %pad_add_fusion.meta, f32[2,8,256]{2,1,0:T(8,128)S(1)} %bitcast.18), custom_call_target="tpu_custom_call" | custom-call | tf_op jit(solution)/shard_map/pallas_call | solution.py:19
  41.6 2.6 %collective-permute-done.2.e_high = f32[11,32,256]{2,1,0:T(8,128)S(1)} collective-permute-done((f32[11,32,256]{2,1,0:T(8,128)S(1)}, f32[11,32,256]{2,1,0:T(8,128)S(1)}, u32[]{:S(2)}, u32[]{:S(2)}) %collective-permute-start.2) | collective-permute-done | bytes 360480 | tf_op jit(solution)/shard_map/ppermute | solution.py:325
  44.2 0.0 collective-permute-done.1.e_low
  44.2 0.7 shard_map.59._.ze
  44.9 0.0 collective-permute-done.far.f
  45.0 3.9 %collective-permute-start.3 = (f32[3,32,256]{2,1,0:T(8,128)S(1)}, f32[3,32,256]{2,1,0:T(8,128)S(1)}, u32[]{:S(2)}, u32[]{:S(2)}) collective-permute-start(f32[3,32,256]{2,1,0:T(8,128)S(1)} %get-tuple-element.37), channel_id=1, source_target_pairs={{0,8},{8,16},{16,24},{24,32},{32,40},{40,48},{48,56},{56,64},{64,7... | collective-permute-start | bytes 294920 | tf_op jit(solution)/shard_map/ppermute | solution.py:325
  48.9 1.9 %collective-permute-start.4 = (f32[3,32,256]{2,1,0:T(8,128)S(1)}, f32[3,32,256]{2,1,0:T(8,128)S(1)}, u32[]{:S(2)}, u32[]{:S(2)}) collective-permute-start(f32[3,32,256]{2,1,0:T(8,128)S(1)} %get-tuple-element.38), channel_id=1, source_target_pairs={{8,0},{16,8},{24,16},{32,24},{40,32},{48,40},{56,48},{64,56},{72,6... | collective-permute-start | bytes 294920 | tf_op jit(solution)/shard_map/ppermute | solution.py:325
  50.8 0.0 collective-permute-done.5.o_low
  50.8 0.0 collective-permute-done.6.o_high
  50.8 3.4 %shard_map.63.bx = f32[2,5,64,256]{3,2,1,0:T(8,128)S(1)} custom-call(s32[3]{0:T(128)S(1)} %pad_add_fusion.meta, f32[2,11,96,256]{3,2,1,0:T(8,128)S(1)} %shard_map.59._.ze, f32[2,8,64,256]{3,2,1,0:T(8,128)S(1)} %get-tuple-element.42.obs, f32[2,8,16,256]{3,2,1,0:T(8,128)S(1)} %collective-permute-done.5.o_low, ...), custom_call_target="tpu_custom_call" | custom-call | tf_op jit(solution)/shard_map/pallas_call | solution.py:19
  54.3 0.0 collective-permute-done.3.f_low
  54.3 2.1 %collective-permute-done.4.f_high = f32[3,32,256]{2,1,0:T(8,128)S(1)} collective-permute-done((f32[3,32,256]{2,1,0:T(8,128)S(1)}, f32[3,32,256]{2,1,0:T(8,128)S(1)}, u32[]{:S(2)}, u32[]{:S(2)}) %collective-permute-start.4) | collective-permute-done | bytes 98336 | tf_op jit(solution)/shard_map/ppermute | solution.py:325
  56.3 3.1 %shard_map.64 = (f32[6,64,256]{2,1,0:T(8,128)S(1)}, f32[2,64,256]{2,1,0:T(8,128)S(1)}, f32[6,64,256]{2,1,0:T(8,128)S(1)}) custom-call(s32[3]{0:T(128)S(1)} %pad_add_fusion.meta, f32[3,64,256]{2,1,0:T(8,128)S(1)} %collective-permute-done.far.f, f32[3,32,256]{2,1,0:T(8,128)S(1)} %collective-permute-done.3.f_low, ...), custom_call_target="tpu_custom_call" | custom-call | tf_op jit(solution)/shard_map/pallas_call | solution.py:19
  59.5 6.6 %collective-permute-start.7 = (f32[6,64,256]{2,1,0:T(8,128)S(1)}, f32[6,64,256]{2,1,0:T(8,128)S(1)}, u32[]{:S(2)}, u32[]{:S(2)}) collective-permute-start(f32[6,64,256]{2,1,0:T(8,128)S(1)} %get-tuple-element.49.c), channel_id=1, source_target_pairs={{256,1},{257,2},{258,3},{259,4},{260,5},{261,6},{262,7},{1,256},{2... | collective-permute-start | bytes 1179656 | tf_op jit(solution)/shard_map/ppermute | solution.py:319
  66.1 2.4 %all-gather.3 = f32[12,64,256]{2,1,0:T(8,128)S(1)} all-gather(f32[6,64,256]{2,1,0:T(8,128)S(1)} %get-tuple-element.53.c_part), channel_id=5, replica_groups=mesh['view'=2,'gz'=32,'gy'=8] {'view'}, dimensions={0}, use_global_device_ids=true | all-gather | bytes 1179648 | tf_op jit(solution)/shard_map/all_gather | solution.py:322
  68.5 0.6 shard_map.66
  69.1 1.9 %collective-permute-start.11 = (f32[8,32,256]{2,1,0:T(8,128)S(1)}, f32[8,32,256]{2,1,0:T(8,128)S(1)}, u32[]{:S(2)}, u32[]{:S(2)}) collective-permute-start(f32[8,32,256]{2,1,0:T(8,128)S(1)} %get-tuple-element.54.e_a), channel_id=1, source_target_pairs={{8,0},{16,8},{24,16},{32,24},{40,32},{48,40},{56,48},{64,56},{72,6... | collective-permute-start | bytes 786440 | tf_op jit(solution)/shard_map/ppermute | solution.py:325
  71.1 5.5 %collective-permute-start.10 = (f32[8,32,256]{2,1,0:T(8,128)S(1)}, f32[8,32,256]{2,1,0:T(8,128)S(1)}, u32[]{:S(2)}, u32[]{:S(2)}) collective-permute-start(f32[8,32,256]{2,1,0:T(8,128)S(1)} %get-tuple-element.55.e_b), channel_id=1, source_target_pairs={{0,8},{8,16},{16,24},{24,32},{32,40},{40,48},{48,56},{56,64},{64,7... | collective-permute-start | bytes 786440 | tf_op jit(solution)/shard_map/ppermute | solution.py:325
  76.5 30.6 %collective-permute-done.7.got = f32[6,64,256]{2,1,0:T(8,128)S(1)} collective-permute-done((f32[6,64,256]{2,1,0:T(8,128)S(1)}, f32[6,64,256]{2,1,0:T(8,128)S(1)}, u32[]{:S(2)}, u32[]{:S(2)}) %collective-permute-start.7) | collective-permute-done | bytes 393248 | tf_op jit(solution)/shard_map/ppermute | solution.py:319
  107.1 0.1 shard_map.65
  107.2 1.9 %collective-permute-start.9 = (f32[6,32,256]{2,1,0:T(8,128)S(1)}, f32[6,32,256]{2,1,0:T(8,128)S(1)}, u32[]{:S(2)}, u32[]{:S(2)}) collective-permute-start(f32[6,32,256]{2,1,0:T(8,128)S(1)} %get-tuple-element.50.f_a), channel_id=1, source_target_pairs={{8,0},{16,8},{24,16},{32,24},{40,32},{48,40},{56,48},{64,56},{72,6... | collective-permute-start | bytes 589832 | tf_op jit(solution)/shard_map/ppermute | solution.py:325
  109.1 5.5 %collective-permute-start.8 = (f32[6,32,256]{2,1,0:T(8,128)S(1)}, f32[6,32,256]{2,1,0:T(8,128)S(1)}, u32[]{:S(2)}, u32[]{:S(2)}) collective-permute-start(f32[6,32,256]{2,1,0:T(8,128)S(1)} %get-tuple-element.51.f_b), channel_id=1, source_target_pairs={{0,8},{8,16},{16,24},{24,32},{32,40},{40,48},{48,56},{56,64},{64,7... | collective-permute-start | bytes 589832 | tf_op jit(solution)/shard_map/ppermute | solution.py:325
  114.6 0.0 collective-permute-done.11.e_high
  114.6 0.0 collective-permute-done.10.e_low
  114.6 2.3 %shard_map.67 = (f32[2,6,96,256]{3,2,1,0:T(8,128)S(1)}, f32[2,2,64,256]{3,2,1,0:T(8,128)S(1)}) custom-call(s32[3]{0:T(128)S(1)} %pad_add_fusion.meta, f32[8,32,256]{2,1,0:T(8,128)S(1)} %get-tuple-element.54.e_a, f32[8,32,256]{2,1,0:T(8,128)S(1)} %get-tuple-element.55.e_b, f32[8,32,256]{2,1,0:T(8,128)S(1)} %collective-permute-done.10.e_low, ...), custom_call_target="tpu_custom_call" | custom-call | tf_op jit(solution)/shard_map/pallas_call | solution.py:19
  117.0 0.2 collective-permute-done.9.f_high
  117.1 0.9 collective-permute-done.8.f_low
  118.0 2.9 %shard_map.68 = (f32[3,64,256]{2,1,0:T(8,128)S(1)}, f32[2,6,96,256]{3,2,1,0:T(8,128)S(1)}, f32[2,3,64,256]{3,2,1,0:T(8,128)S(1)}) custom-call(s32[3]{0:T(128)S(1)} %pad_add_fusion.meta, f32[6,32,256]{2,1,0:T(8,128)S(1)} %get-tuple-element.50.f_a, f32[6,32,256]{2,1,0:T(8,128)S(1)} %get-tuple-element.51.f_b, f32[6,32,256]{2,1,0:T(8,128)S(1)} %collective-permute-done.8.f_low, ...), custom_call_target="tpu_custom_call" | custom-call | tf_op jit(solution)/shard_map/pallas_call | solution.py:19
  120.9 1.9 %collective-permute-start.12 = (f32[3,64,256]{2,1,0:T(8,128)S(1)}, f32[3,64,256]{2,1,0:T(8,128)S(1)}, u32[]{:S(2)}, u32[]{:S(2)}) collective-permute-start(f32[3,64,256]{2,1,0:T(8,128)S(1)} %get-tuple-element.61), channel_id=1, source_target_pairs={{256,1},{257,2},{258,3},{259,4},{260,5},{261,6},{262,7},{1,256},{2... | collective-permute-start | bytes 589832 | tf_op jit(solution)/shard_map/ppermute | solution.py:319
  122.8 2.6 %shard_map.69 = (f32[8,64,256]{2,1,0:T(8,128)S(1)}, f32[3,64,256]{2,1,0:T(8,128)S(1)}) custom-call(s32[3]{0:T(128)S(1)} %pad_add_fusion.meta, f32[2,6,96,256]{3,2,1,0:T(8,128)S(1)} %get-tuple-element.57.zn, f32[2,6,96,256]{3,2,1,0:T(8,128)S(1)} %get-tuple-element.56.ze, f32[2,3,64,256]{3,2,1,0:T(8,128)S(1)} %get-tuple-element.58.bx0, ...), custom_call_target="tpu_custom_call" | custom-call | tf_op jit(solution)/shard_map/pallas_call | solution.py:19
  125.4 3.4 %all-gather.5 = f32[6,64,256]{2,1,0:T(8,128)S(1)} all-gather(f32[3,64,256]{2,1,0:T(8,128)S(1)} %get-tuple-element.62), channel_id=7, replica_groups=mesh['view'=2,'gz'=32,'gy'=8] {'view'}, dimensions={0}, use_global_device_ids=true | all-gather | bytes 589824 | tf_op jit(solution)/shard_map/all_gather | solution.py:322
  128.8 0.6 shard_map.71
  129.4 2.3 %all-gather.6 = f32[10,64,256]{2,1,0:T(8,128)S(1)} all-gather(f32[5,64,256]{2,1,0:T(8,128)S(1)} %shard_map.71), channel_id=8, replica_groups=mesh['view'=2,'gz'=32,'gy'=8] {'view'}, dimensions={0}, use_global_device_ids=true | all-gather | bytes 983040 | tf_op jit(solution)/shard_map/all_gather | solution.py:322
  131.7 5.4 %collective-permute-done.12.got = f32[3,64,256]{2,1,0:T(8,128)S(1)} collective-permute-done((f32[3,64,256]{2,1,0:T(8,128)S(1)}, f32[3,64,256]{2,1,0:T(8,128)S(1)}, u32[]{:S(2)}, u32[]{:S(2)}) %collective-permute-start.12) | collective-permute-done | bytes 196640 | tf_op jit(solution)/shard_map/ppermute | solution.py:319
  137.1 13.5 %all-gather.4 = f32[6,64,256]{2,1,0:T(8,128)S(1)} all-gather(f32[3,64,256]{2,1,0:T(8,128)S(1)} %shard_map.70), channel_id=6, replica_groups=mesh['view'=2,'gz'=32,'gy'=8] {'view'}, dimensions={0}, use_global_device_ids=true | all-gather | bytes 589824 | tf_op jit(solution)/shard_map/all_gather | solution.py:322
  150.5 1.7 %shard_map.72 = f32[64,16,256]{2,1,0:T(8,128)} custom-call(s32[3]{0:T(128)S(1)} %pad_add_fusion.meta, f32[2,3,64,256]{3,2,1,0:T(8,128)S(1)} %bitcast.15, f32[2,5,64,256]{3,2,1,0:T(8,128)S(1)} %bitcast.12), custom_call_target="tpu_custom_call" | custom-call | tf_op jit(solution)/shard_map/pallas_call | solution.py:19
  (3 shorter events, 0.1 us)
Async XLA Ops:
  0.1 1.2 copy-start
  1.3 24.8 %copy-start.1 = (f32[1,64,16,256]{3,2,1,0:T(8,128)S(1)}, f32[1,64,16,256]{3,2,1,0:T(8,128)}, u32[]{:S(2)}) copy-start(f32[1,64,16,256]{3,2,1,0:T(8,128)} %param.5) | copy-start | bytes 3145732
  1.9 43.0 %collective-permute-start = (f32[3,64,256]{2,1,0:T(8,128)S(1)}, f32[3,64,256]{2,1,0:T(8,128)S(1)}, u32[]{:S(2)}, u32[]{:S(2)}) collective-permute-start(f32[3,64,256]{2,1,0:T(8,128)S(1)} %shard_map.55), channel_id=1, source_target_pairs={{256,1},{257,2},{258,3},{259,4},{260,5},{261,6},{262,7},{1,256},{2... | collective-permute-start | bytes 589832 | tf_op jit(solution)/shard_map/ppermute | solution.py:319
  18.7 25.5 %collective-permute-start.2 = (f32[11,32,256]{2,1,0:T(8,128)S(1)}, f32[11,32,256]{2,1,0:T(8,128)S(1)}, u32[]{:S(2)}, u32[]{:S(2)}) collective-permute-start(f32[11,32,256]{2,1,0:T(8,128)S(1)} %get-tuple-element.34.e_a), channel_id=1, source_target_pairs={{8,0},{16,8},{24,16},{32,24},{40,32},{48,40},{56,48},{64,56},{72,6... | collective-permute-start | bytes 1081352 | tf_op jit(solution)/shard_map/ppermute | solution.py:325
  21.0 23.1 %collective-permute-start.1 = (f32[11,32,256]{2,1,0:T(8,128)S(1)}, f32[11,32,256]{2,1,0:T(8,128)S(1)}, u32[]{:S(2)}, u32[]{:S(2)}) collective-permute-start(f32[11,32,256]{2,1,0:T(8,128)S(1)} %get-tuple-element.35.e_b), channel_id=1, source_target_pairs={{0,8},{8,16},{16,24},{24,32},{32,40},{40,48},{48,56},{56,64},{64,7... | collective-permute-start | bytes 1081352 | tf_op jit(solution)/shard_map/ppermute | solution.py:325
  29.1 8.3 %copy-start.2 = (f32[1,31]{1,0:T(1,128)S(1)}, f32[1,31]{1,0:T(1,128)}, u32[]{:S(2)}) copy-start(f32[1,31]{1,0:T(1,128)} %sz.1) | copy-start | bytes 376
  29.1 8.3 %copy-start.3 = (f32[1,7]{1,0:T(1,128)S(1)}, f32[1,7]{1,0:T(1,128)}, u32[]{:S(2)}) copy-start(f32[1,7]{1,0:T(1,128)} %sy.1) | copy-start | bytes 88
  29.1 8.3 %copy-start.4 = (f32[1,7]{1,0:T(1,128)S(1)}, f32[1,7]{1,0:T(1,128)}, u32[]{:S(2)}) copy-start(f32[1,7]{1,0:T(1,128)} %sx.1) | copy-start | bytes 88
  32.0 18.8 %collective-permute-start.5 = (f32[2,8,16,256]{3,2,1,0:T(8,128)S(1)}, f32[2,8,16,256]{3,2,1,0:T(8,128)S(1)}, u32[]{:S(2)}, u32[]{:S(2)}) collective-permute-start(f32[2,8,16,256]{3,2,1,0:T(8,128)S(1)} %get-tuple-element.43), channel_id=1, source_target_pairs={{0,8},{8,16},{16,24},{24,32},{32,40},{40,48},{48,56},{56,64},{64,7... | collective-permute-start | bytes 786440 | tf_op jit(solution)/shard_map/ppermute | solution.py:325
  34.0 16.8 %collective-permute-start.6 = (f32[2,8,16,256]{3,2,1,0:T(8,128)S(1)}, f32[2,8,16,256]{3,2,1,0:T(8,128)S(1)}, u32[]{:S(2)}, u32[]{:S(2)}) collective-permute-start(f32[2,8,16,256]{3,2,1,0:T(8,128)S(1)} %get-tuple-element.44), channel_id=1, source_target_pairs={{8,0},{16,8},{24,16},{32,24},{40,32},{48,40},{56,48},{64,56},{72,6... | collective-permute-start | bytes 786440 | tf_op jit(solution)/shard_map/ppermute | solution.py:325
  45.0 9.3 %collective-permute-start.3 = (f32[3,32,256]{2,1,0:T(8,128)S(1)}, f32[3,32,256]{2,1,0:T(8,128)S(1)}, u32[]{:S(2)}, u32[]{:S(2)}) collective-permute-start(f32[3,32,256]{2,1,0:T(8,128)S(1)} %get-tuple-element.37), channel_id=1, source_target_pairs={{0,8},{8,16},{16,24},{24,32},{32,40},{40,48},{48,56},{56,64},{64,7... | collective-permute-start | bytes 294920 | tf_op jit(solution)/shard_map/ppermute | solution.py:325
  48.9 7.5 %collective-permute-start.4 = (f32[3,32,256]{2,1,0:T(8,128)S(1)}, f32[3,32,256]{2,1,0:T(8,128)S(1)}, u32[]{:S(2)}, u32[]{:S(2)}) collective-permute-start(f32[3,32,256]{2,1,0:T(8,128)S(1)} %get-tuple-element.38), channel_id=1, source_target_pairs={{8,0},{16,8},{24,16},{32,24},{40,32},{48,40},{56,48},{64,56},{72,6... | collective-permute-start | bytes 294920 | tf_op jit(solution)/shard_map/ppermute | solution.py:325
  59.5 47.6 %collective-permute-start.7 = (f32[6,64,256]{2,1,0:T(8,128)S(1)}, f32[6,64,256]{2,1,0:T(8,128)S(1)}, u32[]{:S(2)}, u32[]{:S(2)}) collective-permute-start(f32[6,64,256]{2,1,0:T(8,128)S(1)} %get-tuple-element.49.c), channel_id=1, source_target_pairs={{256,1},{257,2},{258,3},{259,4},{260,5},{261,6},{262,7},{1,256},{2... | collective-permute-start | bytes 1179656 | tf_op jit(solution)/shard_map/ppermute | solution.py:319
  69.1 45.5 %collective-permute-start.11 = (f32[8,32,256]{2,1,0:T(8,128)S(1)}, f32[8,32,256]{2,1,0:T(8,128)S(1)}, u32[]{:S(2)}, u32[]{:S(2)}) collective-permute-start(f32[8,32,256]{2,1,0:T(8,128)S(1)} %get-tuple-element.54.e_a), channel_id=1, source_target_pairs={{8,0},{16,8},{24,16},{32,24},{40,32},{48,40},{56,48},{64,56},{72,6... | collective-permute-start | bytes 786440 | tf_op jit(solution)/shard_map/ppermute | solution.py:325
  71.1 43.6 %collective-permute-start.10 = (f32[8,32,256]{2,1,0:T(8,128)S(1)}, f32[8,32,256]{2,1,0:T(8,128)S(1)}, u32[]{:S(2)}, u32[]{:S(2)}) collective-permute-start(f32[8,32,256]{2,1,0:T(8,128)S(1)} %get-tuple-element.55.e_b), channel_id=1, source_target_pairs={{0,8},{8,16},{16,24},{24,32},{32,40},{40,48},{48,56},{56,64},{64,7... | collective-permute-start | bytes 786440 | tf_op jit(solution)/shard_map/ppermute | solution.py:325
  107.2 9.9 %collective-permute-start.9 = (f32[6,32,256]{2,1,0:T(8,128)S(1)}, f32[6,32,256]{2,1,0:T(8,128)S(1)}, u32[]{:S(2)}, u32[]{:S(2)}) collective-permute-start(f32[6,32,256]{2,1,0:T(8,128)S(1)} %get-tuple-element.50.f_a), channel_id=1, source_target_pairs={{8,0},{16,8},{24,16},{32,24},{40,32},{48,40},{56,48},{64,56},{72,6... | collective-permute-start | bytes 589832 | tf_op jit(solution)/shard_map/ppermute | solution.py:325
  109.1 8.9 %collective-permute-start.8 = (f32[6,32,256]{2,1,0:T(8,128)S(1)}, f32[6,32,256]{2,1,0:T(8,128)S(1)}, u32[]{:S(2)}, u32[]{:S(2)}) collective-permute-start(f32[6,32,256]{2,1,0:T(8,128)S(1)} %get-tuple-element.51.f_b), channel_id=1, source_target_pairs={{0,8},{8,16},{16,24},{24,32},{32,40},{40,48},{48,56},{56,64},{64,7... | collective-permute-start | bytes 589832 | tf_op jit(solution)/shard_map/ppermute | solution.py:325
  120.9 16.2 %collective-permute-start.12 = (f32[3,64,256]{2,1,0:T(8,128)S(1)}, f32[3,64,256]{2,1,0:T(8,128)S(1)}, u32[]{:S(2)}, u32[]{:S(2)}) collective-permute-start(f32[3,64,256]{2,1,0:T(8,128)S(1)} %get-tuple-element.61), channel_id=1, source_target_pairs={{256,1},{257,2},{258,3},{259,4},{260,5},{261,6},{262,7},{1,256},{2... | collective-permute-start | bytes 589832 | tf_op jit(solution)/shard_map/ppermute | solution.py:319

commit v4 on v3

--- a/solution.py
+++ b/solution.py
@@ -161,17 +161,23 @@
     return dot(high, weight[v, 0]) + dot(low, weight[v, 0]) + dot(high, weight[v, 1])
 
 
-def row_result(meta, rows, recorded, yw, xf, xb, zb, v):
-    total = yw[8 * v : 8 * v + 1] * rows[0]
-    for t in range(1, 7):
-        total = total + yw[8 * v + t : 8 * v + t + 1] * rows[t]
-    blurred = blur_x(total, xf, v)
-    at = lax.broadcasted_iota(jnp.int32, blurred.shape, 0)
+def row_results(meta, rows, recorded, yw, xf, xb, zb, v):
+    totals = []
+    for about in rows:
+        total = yw[8 * v : 8 * v + 1] * about[0]
+        for t in range(1, 7):
+            total = total + yw[8 * v + t : 8 * v + t + 1] * about[t]
+        totals.append(total)
+    blurred = blur_x(jnp.concatenate(totals, axis=0), xf, v)
+    at = lax.broadcasted_iota(jnp.int32, (96, NX), 0)
     inside = (at >= meta[1]) & (at < meta[2])
-    quotient = recorded / jnp.where(inside, blurred, 1.0)
-    high, low = parts(quotient)
-    both = dot(zb[v], jnp.concatenate([high, low], axis=0))
-    return blur_x(both[0:64] + both[64:128], xb, v)
+    back = []
+    for k, rec in enumerate(recorded):
+        quotient = rec / jnp.where(inside, blurred[96 * k : 96 * k + 96], 1.0)
+        both = dot(zb[v], jnp.concatenate(parts(quotient), axis=0))
+        back.append(both[0:64] + both[64:128])
+    back = blur_x(jnp.concatenate(back, axis=0), xb, v)
+    return [back[64 * k : 64 * k + 64] for k in range(len(rows))]
 
 
 def recorded_row(obs, o_low, o_high, j, v):
@@ -196,10 +202,11 @@
 
 
 def middle1_body(meta, ze, obs, o_low, o_high, zb, xf, xb, yw, bx):
-    for j in range(3, 8):
-        for v in range(2):
-            rec = recorded_row(obs, o_low, o_high, j, v)
-            bx[v, j - 3] = row_result(meta, [ze[v, j - 3 + t] for t in range(7)], rec, yw, xf, xb, zb, v)
+    for v in range(2):
+        rows = [[ze[v, k + t] for t in range(7)] for k in range(5)]
+        recs = [recorded_row(obs, o_low, o_high, j, v) for j in range(3, 8)]
+        for k, x in enumerate(row_results(meta, rows, recs, yw, xf, xb, zb, v)):
+            bx[v, k] = x
 
 
 def late1_body(meta, f, f_low, f_high, ze, bx, obs, o_low, o_high, zf, zb, xf, xb, yw,
@@ -207,11 +214,11 @@
     for j in range(3):
         for v, x in enumerate(blur_z(zf, f_low[j], f[j, :32], f[j, 32:], f_high[j])):
             buf[v, 2 - j] = x
-    for j in range(3):
-        for v in range(2):
-            rows = [buf[v, j + t] if j + t < 3 else ze[v, j + t - 3] for t in range(7)]
-            rec = recorded_row(obs, o_low, o_high, j, v)
-            new[v, j] = row_result(meta, rows, rec, yw, xf, xb, zb, v)
+    for v in range(2):
+        rows = [[buf[v, j + t] if j + t < 3 else ze[v, j + t - 3] for t in range(7)] for j in range(3)]
+        recs = [recorded_row(obs, o_low, o_high, j, v) for j in range(3)]
+        for j, x in enumerate(row_results(meta, rows, recs, yw, xf, xb, zb, v)):
+            new[v, j] = x
 
     def terms(v, j):
         return new[v, j] if j < 3 else bx[v, j - 3]
@@ -246,10 +253,11 @@
             buf[v, r] = x
             if r < 6:
                 ze[v, r] = x
-    for j in (6, 7):
-        for v in range(2):
-            rec = recorded_row(obs, o_low, o_high, j, v)
-            bx[v, j - 6] = row_result(meta, [buf[v, j - 6 + t] for t in range(7)], rec, yw, xf, xb, zb, v)
+    for v in range(2):
+        rows = [[buf[v, k + t] for t in range(7)] for k in range(2)]
+        recs = [recorded_row(obs, o_low, o_high, j, v) for j in (6, 7)]
+        for k, x in enumerate(row_results(meta, rows, recs, yw, xf, xb, zb, v)):
+            bx[v, k] = x
 
 
 def late2_body(meta, f_a, f_b, f_low, f_high, ze, obs, o_low, o_high, zf, zb, xf, xb, yw,
@@ -257,21 +265,21 @@
     for r in range(6):
         for v, x in enumerate(blur_z(zf, f_low[r], f_a[r], f_b[r], f_high[r])):
             zn[v, r] = x
-    for j in range(3):
-        for v in range(2):
-            rows = [zn[v, j + t] if j + t < 6 else ze[v, j + t - 6] for t in range(7)]
-            rec = recorded_row(obs, o_low, o_high, j, v)
-            bx[v, j] = row_result(meta, rows, rec, yw, xf, xb, zb, v)
+    for v in range(2):
+        rows = [[zn[v, j + t] if j + t < 6 else ze[v, j + t - 6] for t in range(7)] for j in range(3)]
+        recs = [recorded_row(obs, o_low, o_high, j, v) for j in range(3)]
+        for j, x in enumerate(row_results(meta, rows, recs, yw, xf, xb, zb, v)):
+            bx[v, j] = x
     for k in range(3):
         c_far[k] = spread_back(yw, lambda v, j: bx[v, j] if j < 3 else None, -1 - k)
 
 
 def rest2_body(meta, zn, ze, bx0, bx6, obs, o_low, o_high, zb, xf, xb, yw, c_own, c_part, new):
-    for j in range(3, 6):
-        for v in range(2):
-            rows = [zn[v, j + t] if j + t < 6 else ze[v, j + t - 6] for t in range(7)]
-            rec = recorded_row(obs, o_low, o_high, j, v)
-            new[v, j - 3] = row_result(meta, rows, rec, yw, xf, xb, zb, v)
+    for v in range(2):
+        rows = [[zn[v, j + t] if j + t < 6 else ze[v, j + t - 6] for t in range(7)] for j in range(3, 6)]
+        recs = [recorded_row(obs, o_low, o_high, j, v) for j in range(3, 6)]
+        for k, x in enumerate(row_results(meta, rows, recs, yw, xf, xb, zb, v)):
+            new[v, k] = x
 
     def terms(v, j):
         return bx0[v, j] if j < 3 else new[v, j - 3] if j < 6 else bx6[v, j - 6]

time: 153 us -> 150 us (0.980)
  waiting for transfers between devices: 41.7 us -> 51.8 us
  blocking collectives: 28.4 us -> 19.2 us
  Pallas kernels: 22.7 us -> 19.2 us
    all_gather x7, blocking collectives: 28.4 us -> 19.2 us  [both(): return lax.all_gather(x, 'view')]
    ppermute x3, waiting for transfers between devices: 36 us -> 44.7 us  [far(): return lax.ppermute(x, ('view', 'gy'), across)]
    pallas_call x18, Pallas kernels: 22.7 us -> 19.2 us  [call(): pl.pallas_call(body, out_shape=outs, in_specs=[SM] * smem + [VM] * (len(a...]
  transfers between devices with their start and end apart: 13 -> 13, of which waited for: 6 -> 6; matrix products, arithmetic and copies ran while one was open for 0% -> 0% of each run, Pallas kernels for 9% -> 8%
where the time goes in v4:
time: 150 us
  starting transfers between devices  57.9 us (39%)
  waiting for transfers between devices  51.8 us (35%)
  Pallas kernels  19.2 us (13%)
  blocking collectives  19.2 us (13%)
    ppermute x3, waiting for transfers between devices, far(): return lax.ppermute(x, ('view', 'gy'), across)  44.7 us
    ppermute x10, starting transfers between devices, along_z(): return (lax.ppermute(last, 'gz', up), lax.ppermute(first, 'gz', down))  33.3 us
    ppermute x3, starting transfers between devices, far(): return lax.ppermute(x, ('view', 'gy'), across)  24.6 us
    pallas_call x18, Pallas kernels, call(): pl.pallas_call(body, out_shape=outs, in_specs=[SM] * smem + [VM] * (len(a...  19.2 us
    all_gather x7, blocking collectives, both(): return lax.all_gather(x, 'view')  19.2 us
    ppermute x10, waiting for transfers between devices, along_z(): return (lax.ppermute(last, 'gz', up), lax.ppermute(first, 'gz', down))  7.1 us
  transfers between devices with their start and end apart: 13, of which 6 were waited for; matrix products, arithmetic and copies ran while one was open for 0% of the time, Pallas kernels for 8%

profile of v4, /device:TPU:29, one launch (start us, length us, event | category | flops | bytes accessed | tf_op | source)
XLA Modules:
  0.0 149.7 jit_solution(12241185591087059900)
XLA Ops:
  0.0 0.1 pad_add_fusion.meta
  0.1 0.0 copy-start
  0.1 1.2 copy-done
  1.3 0.0 copy-start.1
  1.3 0.6 shard_map.55
  1.9 16.0 %collective-permute-start = (f32[3,64,256]{2,1,0:T(8,128)S(1)}, f32[3,64,256]{2,1,0:T(8,128)S(1)}, u32[]{:S(2)}, u32[]{:S(2)}) collective-permute-start(f32[3,64,256]{2,1,0:T(8,128)S(1)} %shard_map.55), channel_id=1, source_target_pairs={{256,1},{257,2},{258,3},{259,4},{260,5},{261,6},{262,7},{1,256},{2... | collective-permute-start | bytes 589832 | tf_op jit(solution)/shard_map/ppermute | solution.py:327
  17.9 0.7 shard_map.56
  18.7 2.4 %collective-permute-start.2 = (f32[11,32,256]{2,1,0:T(8,128)S(1)}, f32[11,32,256]{2,1,0:T(8,128)S(1)}, u32[]{:S(2)}, u32[]{:S(2)}) collective-permute-start(f32[11,32,256]{2,1,0:T(8,128)S(1)} %get-tuple-element.34.e_a), channel_id=1, source_target_pairs={{8,0},{16,8},{24,16},{32,24},{40,32},{48,40},{56,48},{64,56},{72,6... | collective-permute-start | bytes 1081352 | tf_op jit(solution)/shard_map/ppermute | solution.py:333
  21.0 5.0 %collective-permute-start.1 = (f32[11,32,256]{2,1,0:T(8,128)S(1)}, f32[11,32,256]{2,1,0:T(8,128)S(1)}, u32[]{:S(2)}, u32[]{:S(2)}) collective-permute-start(f32[11,32,256]{2,1,0:T(8,128)S(1)} %get-tuple-element.35.e_b), channel_id=1, source_target_pairs={{0,8},{8,16},{16,24},{24,32},{32,40},{40,48},{48,56},{56,64},{64,7... | collective-permute-start | bytes 1081352 | tf_op jit(solution)/shard_map/ppermute | solution.py:333
  26.1 0.0 copy-done.1
  26.1 0.8 shard_map.61
  26.9 2.2 %all-gather.1 = f32[8,64,256]{2,1,0:T(8,128)S(1)} all-gather(f32[4,64,256]{2,1,0:T(8,128)S(1)} %get-tuple-element.40), channel_id=3, replica_groups=mesh['view'=2,'gz'=32,'gy'=8] {'view'}, dimensions={0}, use_global_device_ids=true | all-gather | bytes 786432 | tf_op jit(solution)/shard_map/all_gather | solution.py:330
  29.1 0.0 copy-start.2
  29.1 0.0 copy-start.3
  29.1 0.0 copy-start.4
  29.1 2.3 %all-gather.2 = f32[8,64,256]{2,1,0:T(8,128)S(1)} all-gather(f32[4,64,256]{2,1,0:T(8,128)S(1)} %get-tuple-element.41), channel_id=4, replica_groups=mesh['view'=2,'gz'=32,'gy'=8] {'view'}, dimensions={0}, use_global_device_ids=true | all-gather | bytes 786432 | tf_op jit(solution)/shard_map/all_gather | solution.py:330
  31.4 0.6 shard_map.62
  32.0 1.9 %collective-permute-start.5 = (f32[2,8,16,256]{3,2,1,0:T(8,128)S(1)}, f32[2,8,16,256]{3,2,1,0:T(8,128)S(1)}, u32[]{:S(2)}, u32[]{:S(2)}) collective-permute-start(f32[2,8,16,256]{3,2,1,0:T(8,128)S(1)} %get-tuple-element.43), channel_id=1, source_target_pairs={{0,8},{8,16},{16,24},{24,32},{32,40},{40,48},{48,56},{56,64},{64,7... | collective-permute-start | bytes 786440 | tf_op jit(solution)/shard_map/ppermute | solution.py:333
  34.0 3.4 %collective-permute-start.6 = (f32[2,8,16,256]{3,2,1,0:T(8,128)S(1)}, f32[2,8,16,256]{3,2,1,0:T(8,128)S(1)}, u32[]{:S(2)}, u32[]{:S(2)}) collective-permute-start(f32[2,8,16,256]{3,2,1,0:T(8,128)S(1)} %get-tuple-element.44), channel_id=1, source_target_pairs={{8,0},{16,8},{24,16},{32,24},{40,32},{48,40},{56,48},{64,56},{72,6... | collective-permute-start | bytes 786440 | tf_op jit(solution)/shard_map/ppermute | solution.py:333
  37.3 0.0 copy-done.2
  37.3 0.0 copy-done.3
  37.3 0.0 copy-done.4
  37.4 2.4 %all-gather = f32[16,256]{1,0:T(8,128)S(1)} all-gather(f32[8,256]{1,0:T(8,128)S(1)} %shard_map.57), channel_id=2, replica_groups=mesh['view'=2,'gz'=32,'gy'=8] {'view'}, dimensions={0}, use_global_device_ids=true | all-gather | bytes 24576 | tf_op jit(solution)/shard_map/all_gather | solution.py:330
  39.8 1.8 %shard_map.58 = (bf16[384,256]{1,0:T(8,128)(2,1)S(1)}, bf16[2,128,192]{2,1,0:T(8,128)(2,1)S(1)}, bf16[2,2,256,256]{3,2,1,0:T(8,128)(2,1)S(1)}, bf16[2,2,256,256]{3,2,1,0:T(8,128)(2,1)S(1)}, f32[16,256]{1,0:T(8,128)S(1)}) custom-call(s32[3]{0:T(128)S(1)} %pad_add_fusion.meta, f32[2,8,256]{2,1,0:T(8,128)S(1)} %bitcast.18), custom_call_target="tpu_custom_call" | custom-call | tf_op jit(solution)/shard_map/pallas_call | solution.py:19
  41.6 2.6 %collective-permute-done.2.e_high = f32[11,32,256]{2,1,0:T(8,128)S(1)} collective-permute-done((f32[11,32,256]{2,1,0:T(8,128)S(1)}, f32[11,32,256]{2,1,0:T(8,128)S(1)}, u32[]{:S(2)}, u32[]{:S(2)}) %collective-permute-start.2) | collective-permute-done | bytes 360480 | tf_op jit(solution)/shard_map/ppermute | solution.py:333
  44.2 0.0 collective-permute-done.1.e_low
  44.2 0.7 shard_map.59._.ze
  44.9 0.0 collective-permute-done.far.f
  45.0 3.9 %collective-permute-start.3 = (f32[3,32,256]{2,1,0:T(8,128)S(1)}, f32[3,32,256]{2,1,0:T(8,128)S(1)}, u32[]{:S(2)}, u32[]{:S(2)}) collective-permute-start(f32[3,32,256]{2,1,0:T(8,128)S(1)} %get-tuple-element.37), channel_id=1, source_target_pairs={{0,8},{8,16},{16,24},{24,32},{32,40},{40,48},{48,56},{56,64},{64,7... | collective-permute-start | bytes 294920 | tf_op jit(solution)/shard_map/ppermute | solution.py:333
  48.9 1.9 %collective-permute-start.4 = (f32[3,32,256]{2,1,0:T(8,128)S(1)}, f32[3,32,256]{2,1,0:T(8,128)S(1)}, u32[]{:S(2)}, u32[]{:S(2)}) collective-permute-start(f32[3,32,256]{2,1,0:T(8,128)S(1)} %get-tuple-element.38), channel_id=1, source_target_pairs={{8,0},{16,8},{24,16},{32,24},{40,32},{48,40},{56,48},{64,56},{72,6... | collective-permute-start | bytes 294920 | tf_op jit(solution)/shard_map/ppermute | solution.py:333
  50.8 0.0 collective-permute-done.5.o_low
  50.8 0.0 collective-permute-done.6.o_high
  50.8 2.5 %shard_map.63.bx = f32[2,5,64,256]{3,2,1,0:T(8,128)S(1)} custom-call(s32[3]{0:T(128)S(1)} %pad_add_fusion.meta, f32[2,11,96,256]{3,2,1,0:T(8,128)S(1)} %shard_map.59._.ze, f32[2,8,64,256]{3,2,1,0:T(8,128)S(1)} %get-tuple-element.42.obs, f32[2,8,16,256]{3,2,1,0:T(8,128)S(1)} %collective-permute-done.5.o_low, ...), custom_call_target="tpu_custom_call" | custom-call | tf_op jit(solution)/shard_map/pallas_call | solution.py:19
  53.3 0.0 collective-permute-done.3.f_low
  53.3 3.0 %collective-permute-done.4.f_high = f32[3,32,256]{2,1,0:T(8,128)S(1)} collective-permute-done((f32[3,32,256]{2,1,0:T(8,128)S(1)}, f32[3,32,256]{2,1,0:T(8,128)S(1)}, u32[]{:S(2)}, u32[]{:S(2)}) %collective-permute-start.4) | collective-permute-done | bytes 98336 | tf_op jit(solution)/shard_map/ppermute | solution.py:333
  56.3 2.4 %shard_map.64 = (f32[6,64,256]{2,1,0:T(8,128)S(1)}, f32[2,64,256]{2,1,0:T(8,128)S(1)}, f32[6,64,256]{2,1,0:T(8,128)S(1)}) custom-call(s32[3]{0:T(128)S(1)} %pad_add_fusion.meta, f32[3,64,256]{2,1,0:T(8,128)S(1)} %collective-permute-done.far.f, f32[3,32,256]{2,1,0:T(8,128)S(1)} %collective-permute-done.3.f_low, ...), custom_call_target="tpu_custom_call" | custom-call | tf_op jit(solution)/shard_map/pallas_call | solution.py:19
  58.7 6.6 %collective-permute-start.7 = (f32[6,64,256]{2,1,0:T(8,128)S(1)}, f32[6,64,256]{2,1,0:T(8,128)S(1)}, u32[]{:S(2)}, u32[]{:S(2)}) collective-permute-start(f32[6,64,256]{2,1,0:T(8,128)S(1)} %get-tuple-element.49.c), channel_id=1, source_target_pairs={{256,1},{257,2},{258,3},{259,4},{260,5},{261,6},{262,7},{1,256},{2... | collective-permute-start | bytes 1179656 | tf_op jit(solution)/shard_map/ppermute | solution.py:327
  65.4 2.4 %all-gather.3 = f32[12,64,256]{2,1,0:T(8,128)S(1)} all-gather(f32[6,64,256]{2,1,0:T(8,128)S(1)} %get-tuple-element.53.c_part), channel_id=5, replica_groups=mesh['view'=2,'gz'=32,'gy'=8] {'view'}, dimensions={0}, use_global_device_ids=true | all-gather | bytes 1179648 | tf_op jit(solution)/shard_map/all_gather | solution.py:330
  67.7 0.6 shard_map.66
  68.3 1.9 %collective-permute-start.11 = (f32[8,32,256]{2,1,0:T(8,128)S(1)}, f32[8,32,256]{2,1,0:T(8,128)S(1)}, u32[]{:S(2)}, u32[]{:S(2)}) collective-permute-start(f32[8,32,256]{2,1,0:T(8,128)S(1)} %get-tuple-element.54.e_a), channel_id=1, source_target_pairs={{8,0},{16,8},{24,16},{32,24},{40,32},{48,40},{56,48},{64,56},{72,6... | collective-permute-start | bytes 786440 | tf_op jit(solution)/shard_map/ppermute | solution.py:333
  70.3 5.5 %collective-permute-start.10 = (f32[8,32,256]{2,1,0:T(8,128)S(1)}, f32[8,32,256]{2,1,0:T(8,128)S(1)}, u32[]{:S(2)}, u32[]{:S(2)}) collective-permute-start(f32[8,32,256]{2,1,0:T(8,128)S(1)} %get-tuple-element.55.e_b), channel_id=1, source_target_pairs={{0,8},{8,16},{16,24},{24,32},{32,40},{40,48},{48,56},{56,64},{64,7... | collective-permute-start | bytes 786440 | tf_op jit(solution)/shard_map/ppermute | solution.py:333
  75.8 30.6 %collective-permute-done.7.got = f32[6,64,256]{2,1,0:T(8,128)S(1)} collective-permute-done((f32[6,64,256]{2,1,0:T(8,128)S(1)}, f32[6,64,256]{2,1,0:T(8,128)S(1)}, u32[]{:S(2)}, u32[]{:S(2)}) %collective-permute-start.7) | collective-permute-done | bytes 393248 | tf_op jit(solution)/shard_map/ppermute | solution.py:327
  106.3 0.1 shard_map.65
  106.4 1.9 %collective-permute-start.9 = (f32[6,32,256]{2,1,0:T(8,128)S(1)}, f32[6,32,256]{2,1,0:T(8,128)S(1)}, u32[]{:S(2)}, u32[]{:S(2)}) collective-permute-start(f32[6,32,256]{2,1,0:T(8,128)S(1)} %get-tuple-element.50.f_a), channel_id=1, source_target_pairs={{8,0},{16,8},{24,16},{32,24},{40,32},{48,40},{56,48},{64,56},{72,6... | collective-permute-start | bytes 589832 | tf_op jit(solution)/shard_map/ppermute | solution.py:333
  108.3 5.5 %collective-permute-start.8 = (f32[6,32,256]{2,1,0:T(8,128)S(1)}, f32[6,32,256]{2,1,0:T(8,128)S(1)}, u32[]{:S(2)}, u32[]{:S(2)}) collective-permute-start(f32[6,32,256]{2,1,0:T(8,128)S(1)} %get-tuple-element.51.f_b), channel_id=1, source_target_pairs={{0,8},{8,16},{16,24},{24,32},{32,40},{40,48},{48,56},{56,64},{64,7... | collective-permute-start | bytes 589832 | tf_op jit(solution)/shard_map/ppermute | solution.py:333
  113.8 0.0 collective-permute-done.11.e_high
  113.8 0.0 collective-permute-done.10.e_low
  113.8 2.0 %shard_map.67 = (f32[2,6,96,256]{3,2,1,0:T(8,128)S(1)}, f32[2,2,64,256]{3,2,1,0:T(8,128)S(1)}) custom-call(s32[3]{0:T(128)S(1)} %pad_add_fusion.meta, f32[8,32,256]{2,1,0:T(8,128)S(1)} %get-tuple-element.54.e_a, f32[8,32,256]{2,1,0:T(8,128)S(1)} %get-tuple-element.55.e_b, f32[8,32,256]{2,1,0:T(8,128)S(1)} %collective-permute-done.10.e_low, ...), custom_call_target="tpu_custom_call" | custom-call | tf_op jit(solution)/shard_map/pallas_call | solution.py:19
  115.8 0.6 collective-permute-done.9.f_high
  116.4 0.9 collective-permute-done.8.f_low
  117.2 2.1 %shard_map.68 = (f32[3,64,256]{2,1,0:T(8,128)S(1)}, f32[2,6,96,256]{3,2,1,0:T(8,128)S(1)}, f32[2,3,64,256]{3,2,1,0:T(8,128)S(1)}) custom-call(s32[3]{0:T(128)S(1)} %pad_add_fusion.meta, f32[6,32,256]{2,1,0:T(8,128)S(1)} %get-tuple-element.50.f_a, f32[6,32,256]{2,1,0:T(8,128)S(1)} %get-tuple-element.51.f_b, f32[6,32,256]{2,1,0:T(8,128)S(1)} %collective-permute-done.8.f_low, ...), custom_call_target="tpu_custom_call" | custom-call | tf_op jit(solution)/shard_map/pallas_call | solution.py:19
  119.4 1.9 %collective-permute-start.12 = (f32[3,64,256]{2,1,0:T(8,128)S(1)}, f32[3,64,256]{2,1,0:T(8,128)S(1)}, u32[]{:S(2)}, u32[]{:S(2)}) collective-permute-start(f32[3,64,256]{2,1,0:T(8,128)S(1)} %get-tuple-element.61), channel_id=1, source_target_pairs={{256,1},{257,2},{258,3},{259,4},{260,5},{261,6},{262,7},{1,256},{2... | collective-permute-start | bytes 589832 | tf_op jit(solution)/shard_map/ppermute | solution.py:327
  121.3 2.0 %shard_map.69 = (f32[8,64,256]{2,1,0:T(8,128)S(1)}, f32[3,64,256]{2,1,0:T(8,128)S(1)}) custom-call(s32[3]{0:T(128)S(1)} %pad_add_fusion.meta, f32[2,6,96,256]{3,2,1,0:T(8,128)S(1)} %get-tuple-element.57.zn, f32[2,6,96,256]{3,2,1,0:T(8,128)S(1)} %get-tuple-element.56.ze, f32[2,3,64,256]{3,2,1,0:T(8,128)S(1)} %get-tuple-element.58.bx0, ...), custom_call_target="tpu_custom_call" | custom-call | tf_op jit(solution)/shard_map/pallas_call | solution.py:19
  123.3 3.4 %all-gather.5 = f32[6,64,256]{2,1,0:T(8,128)S(1)} all-gather(f32[3,64,256]{2,1,0:T(8,128)S(1)} %get-tuple-element.62), channel_id=7, replica_groups=mesh['view'=2,'gz'=32,'gy'=8] {'view'}, dimensions={0}, use_global_device_ids=true | all-gather | bytes 589824 | tf_op jit(solution)/shard_map/all_gather | solution.py:330
  126.7 0.6 shard_map.71
  127.3 2.3 %all-gather.6 = f32[10,64,256]{2,1,0:T(8,128)S(1)} all-gather(f32[5,64,256]{2,1,0:T(8,128)S(1)} %shard_map.71), channel_id=8, replica_groups=mesh['view'=2,'gz'=32,'gy'=8] {'view'}, dimensions={0}, use_global_device_ids=true | all-gather | bytes 983040 | tf_op jit(solution)/shard_map/all_gather | solution.py:330
  129.5 14.1 %collective-permute-done.12.got = f32[3,64,256]{2,1,0:T(8,128)S(1)} collective-permute-done((f32[3,64,256]{2,1,0:T(8,128)S(1)}, f32[3,64,256]{2,1,0:T(8,128)S(1)}, u32[]{:S(2)}, u32[]{:S(2)}) %collective-permute-start.12) | collective-permute-done | bytes 196640 | tf_op jit(solution)/shard_map/ppermute | solution.py:327
  143.7 4.3 %all-gather.4 = f32[6,64,256]{2,1,0:T(8,128)S(1)} all-gather(f32[3,64,256]{2,1,0:T(8,128)S(1)} %shard_map.70), channel_id=6, replica_groups=mesh['view'=2,'gz'=32,'gy'=8] {'view'}, dimensions={0}, use_global_device_ids=true | all-gather | bytes 589824 | tf_op jit(solution)/shard_map/all_gather | solution.py:330
  148.0 1.7 %shard_map.72 = f32[64,16,256]{2,1,0:T(8,128)} custom-call(s32[3]{0:T(128)S(1)} %pad_add_fusion.meta, f32[2,3,64,256]{3,2,1,0:T(8,128)S(1)} %bitcast.15, f32[2,5,64,256]{3,2,1,0:T(8,128)S(1)} %bitcast.12), custom_call_target="tpu_custom_call" | custom-call | tf_op jit(solution)/shard_map/pallas_call | solution.py:19
  (3 shorter events, 0.1 us)
Async XLA Ops:
  0.1 1.2 copy-start
  1.3 24.8 %copy-start.1 = (f32[1,64,16,256]{3,2,1,0:T(8,128)S(1)}, f32[1,64,16,256]{3,2,1,0:T(8,128)}, u32[]{:S(2)}) copy-start(f32[1,64,16,256]{3,2,1,0:T(8,128)} %param.5) | copy-start | bytes 3145732
  1.9 43.0 %collective-permute-start = (f32[3,64,256]{2,1,0:T(8,128)S(1)}, f32[3,64,256]{2,1,0:T(8,128)S(1)}, u32[]{:S(2)}, u32[]{:S(2)}) collective-permute-start(f32[3,64,256]{2,1,0:T(8,128)S(1)} %shard_map.55), channel_id=1, source_target_pairs={{256,1},{257,2},{258,3},{259,4},{260,5},{261,6},{262,7},{1,256},{2... | collective-permute-start | bytes 589832 | tf_op jit(solution)/shard_map/ppermute | solution.py:327
  18.7 25.5 %collective-permute-start.2 = (f32[11,32,256]{2,1,0:T(8,128)S(1)}, f32[11,32,256]{2,1,0:T(8,128)S(1)}, u32[]{:S(2)}, u32[]{:S(2)}) collective-permute-start(f32[11,32,256]{2,1,0:T(8,128)S(1)} %get-tuple-element.34.e_a), channel_id=1, source_target_pairs={{8,0},{16,8},{24,16},{32,24},{40,32},{48,40},{56,48},{64,56},{72,6... | collective-permute-start | bytes 1081352 | tf_op jit(solution)/shard_map/ppermute | solution.py:333
  21.0 23.1 %collective-permute-start.1 = (f32[11,32,256]{2,1,0:T(8,128)S(1)}, f32[11,32,256]{2,1,0:T(8,128)S(1)}, u32[]{:S(2)}, u32[]{:S(2)}) collective-permute-start(f32[11,32,256]{2,1,0:T(8,128)S(1)} %get-tuple-element.35.e_b), channel_id=1, source_target_pairs={{0,8},{8,16},{16,24},{24,32},{32,40},{40,48},{48,56},{56,64},{64,7... | collective-permute-start | bytes 1081352 | tf_op jit(solution)/shard_map/ppermute | solution.py:333
  29.1 8.3 %copy-start.2 = (f32[1,31]{1,0:T(1,128)S(1)}, f32[1,31]{1,0:T(1,128)}, u32[]{:S(2)}) copy-start(f32[1,31]{1,0:T(1,128)} %sz.1) | copy-start | bytes 376
  29.1 8.3 %copy-start.3 = (f32[1,7]{1,0:T(1,128)S(1)}, f32[1,7]{1,0:T(1,128)}, u32[]{:S(2)}) copy-start(f32[1,7]{1,0:T(1,128)} %sy.1) | copy-start | bytes 88
  29.1 8.3 %copy-start.4 = (f32[1,7]{1,0:T(1,128)S(1)}, f32[1,7]{1,0:T(1,128)}, u32[]{:S(2)}) copy-start(f32[1,7]{1,0:T(1,128)} %sx.1) | copy-start | bytes 88
  32.0 18.8 %collective-permute-start.5 = (f32[2,8,16,256]{3,2,1,0:T(8,128)S(1)}, f32[2,8,16,256]{3,2,1,0:T(8,128)S(1)}, u32[]{:S(2)}, u32[]{:S(2)}) collective-permute-start(f32[2,8,16,256]{3,2,1,0:T(8,128)S(1)} %get-tuple-element.43), channel_id=1, source_target_pairs={{0,8},{8,16},{16,24},{24,32},{32,40},{40,48},{48,56},{56,64},{64,7... | collective-permute-start | bytes 786440 | tf_op jit(solution)/shard_map/ppermute | solution.py:333
  34.0 16.8 %collective-permute-start.6 = (f32[2,8,16,256]{3,2,1,0:T(8,128)S(1)}, f32[2,8,16,256]{3,2,1,0:T(8,128)S(1)}, u32[]{:S(2)}, u32[]{:S(2)}) collective-permute-start(f32[2,8,16,256]{3,2,1,0:T(8,128)S(1)} %get-tuple-element.44), channel_id=1, source_target_pairs={{8,0},{16,8},{24,16},{32,24},{40,32},{48,40},{56,48},{64,56},{72,6... | collective-permute-start | bytes 786440 | tf_op jit(solution)/shard_map/ppermute | solution.py:333
  45.0 8.3 %collective-permute-start.3 = (f32[3,32,256]{2,1,0:T(8,128)S(1)}, f32[3,32,256]{2,1,0:T(8,128)S(1)}, u32[]{:S(2)}, u32[]{:S(2)}) collective-permute-start(f32[3,32,256]{2,1,0:T(8,128)S(1)} %get-tuple-element.37), channel_id=1, source_target_pairs={{0,8},{8,16},{16,24},{24,32},{32,40},{40,48},{48,56},{56,64},{64,7... | collective-permute-start | bytes 294920 | tf_op jit(solution)/shard_map/ppermute | solution.py:333
  48.9 7.5 %collective-permute-start.4 = (f32[3,32,256]{2,1,0:T(8,128)S(1)}, f32[3,32,256]{2,1,0:T(8,128)S(1)}, u32[]{:S(2)}, u32[]{:S(2)}) collective-permute-start(f32[3,32,256]{2,1,0:T(8,128)S(1)} %get-tuple-element.38), channel_id=1, source_target_pairs={{8,0},{16,8},{24,16},{32,24},{40,32},{48,40},{56,48},{64,56},{72,6... | collective-permute-start | bytes 294920 | tf_op jit(solution)/shard_map/ppermute | solution.py:333
  58.7 47.6 %collective-permute-start.7 = (f32[6,64,256]{2,1,0:T(8,128)S(1)}, f32[6,64,256]{2,1,0:T(8,128)S(1)}, u32[]{:S(2)}, u32[]{:S(2)}) collective-permute-start(f32[6,64,256]{2,1,0:T(8,128)S(1)} %get-tuple-element.49.c), channel_id=1, source_target_pairs={{256,1},{257,2},{258,3},{259,4},{260,5},{261,6},{262,7},{1,256},{2... | collective-permute-start | bytes 1179656 | tf_op jit(solution)/shard_map/ppermute | solution.py:327
  68.3 45.4 %collective-permute-start.11 = (f32[8,32,256]{2,1,0:T(8,128)S(1)}, f32[8,32,256]{2,1,0:T(8,128)S(1)}, u32[]{:S(2)}, u32[]{:S(2)}) collective-permute-start(f32[8,32,256]{2,1,0:T(8,128)S(1)} %get-tuple-element.54.e_a), channel_id=1, source_target_pairs={{8,0},{16,8},{24,16},{32,24},{40,32},{48,40},{56,48},{64,56},{72,6... | collective-permute-start | bytes 786440 | tf_op jit(solution)/shard_map/ppermute | solution.py:333
  70.3 43.5 %collective-permute-start.10 = (f32[8,32,256]{2,1,0:T(8,128)S(1)}, f32[8,32,256]{2,1,0:T(8,128)S(1)}, u32[]{:S(2)}, u32[]{:S(2)}) collective-permute-start(f32[8,32,256]{2,1,0:T(8,128)S(1)} %get-tuple-element.55.e_b), channel_id=1, source_target_pairs={{0,8},{8,16},{16,24},{24,32},{32,40},{40,48},{48,56},{56,64},{64,7... | collective-permute-start | bytes 786440 | tf_op jit(solution)/shard_map/ppermute | solution.py:333
  106.4 10.0 %collective-permute-start.9 = (f32[6,32,256]{2,1,0:T(8,128)S(1)}, f32[6,32,256]{2,1,0:T(8,128)S(1)}, u32[]{:S(2)}, u32[]{:S(2)}) collective-permute-start(f32[6,32,256]{2,1,0:T(8,128)S(1)} %get-tuple-element.50.f_a), channel_id=1, source_target_pairs={{8,0},{16,8},{24,16},{32,24},{40,32},{48,40},{56,48},{64,56},{72,6... | collective-permute-start | bytes 589832 | tf_op jit(solution)/shard_map/ppermute | solution.py:333
  108.3 8.9 %collective-permute-start.8 = (f32[6,32,256]{2,1,0:T(8,128)S(1)}, f32[6,32,256]{2,1,0:T(8,128)S(1)}, u32[]{:S(2)}, u32[]{:S(2)}) collective-permute-start(f32[6,32,256]{2,1,0:T(8,128)S(1)} %get-tuple-element.51.f_b), channel_id=1, source_target_pairs={{0,8},{8,16},{16,24},{24,32},{32,40},{40,48},{48,56},{56,64},{64,7... | collective-permute-start | bytes 589832 | tf_op jit(solution)/shard_map/ppermute | solution.py:333
  119.4 24.3 %collective-permute-start.12 = (f32[3,64,256]{2,1,0:T(8,128)S(1)}, f32[3,64,256]{2,1,0:T(8,128)S(1)}, u32[]{:S(2)}, u32[]{:S(2)}) collective-permute-start(f32[3,64,256]{2,1,0:T(8,128)S(1)} %get-tuple-element.61), channel_id=1, source_target_pairs={{256,1},{257,2},{258,3},{259,4},{260,5},{261,6},{262,7},{1,256},{2... | collective-permute-start | bytes 589832 | tf_op jit(solution)/shard_map/ppermute | solution.py:327

commit v5 on v4

--- a/solution.py
+++ b/solution.py
@@ -53,9 +53,12 @@
         pl.when(meta[0] == core)(lambda core=core: body(core, lambda r: r % 8 if core == 0 else 7 - r % 8))
 
 
-def far_body(meta, start, out):
+def far_body(meta, start, out, half, sem):
     def body(core, at):
-        rows = rows_of(start, core)
+        copy = pltpu.make_async_copy(start.at[:, 8 * core : 8 * core + 8, :], half, sem)
+        copy.start()
+        copy.wait()
+        rows = jnp.swapaxes(half[...], 0, 1)
         for j in range(3):
             out[j] = rows[at(j)]
 
@@ -203,14 +206,14 @@
 
 def middle1_body(meta, ze, obs, o_low, o_high, zb, xf, xb, yw, bx):
     for v in range(2):
-        rows = [[ze[v, k + t] for t in range(7)] for k in range(5)]
-        recs = [recorded_row(obs, o_low, o_high, j, v) for j in range(3, 8)]
+        rows = [[ze[v, k + t] for t in range(7)] for k in range(3)]
+        recs = [recorded_row(obs, o_low, o_high, j, v) for j in range(3, 6)]
         for k, x in enumerate(row_results(meta, rows, recs, yw, xf, xb, zb, v)):
             bx[v, k] = x
 
 
 def late1_body(meta, f, f_low, f_high, ze, bx, obs, o_low, o_high, zf, zb, xf, xb, yw,
-               c_far, c_mid, c_part, buf, new):
+               c_far, new, buf):
     for j in range(3):
         for v, x in enumerate(blur_z(zf, f_low[j], f[j, :32], f[j, 32:], f_high[j])):
             buf[v, 2 - j] = x
@@ -220,24 +223,43 @@
         for j, x in enumerate(row_results(meta, rows, recs, yw, xf, xb, zb, v)):
             new[v, j] = x
 
+    for row in range(-3, 3):
+        c_far[row + 3] = spread_back(yw, lambda v, j: new[v, j] if j < 3 else bx[v, j - 3], row)
+
+
+def rest1_body(meta, ze, bx0, bx3, obs, o_low, o_high, zb, xf, xb, yw, c_mid, c_part, new):
+    for v in range(2):
+        rows = [[ze[v, k + t] for t in range(7)] for k in (3, 4)]
+        recs = [recorded_row(obs, o_low, o_high, j, v) for j in (6, 7)]
+        for k, x in enumerate(row_results(meta, rows, recs, yw, xf, xb, zb, v)):
+            new[v, k] = x
+
     def terms(v, j):
-        return new[v, j] if j < 3 else bx[v, j - 3]
-
-    for row in range(-3, 11):
+        return bx0[v, j] if j < 3 else bx3[v, j - 3] if j < 6 else new[v, j - 6]
+
+    for row in range(3, 11):
         total = spread_back(yw, terms, row)
-        if row < 3:
-            c_far[row + 3] = total
-        elif row < 5:
+        if row < 5:
             c_mid[row - 3] = total
         else:
             c_part[row - 5] = total
 
 
-def update_mid_body(meta, e_a, e_b, c_mid, c_part, got, out_a, out_b):
+def update_mid_body(meta, e_a, e_b, c_mid, c_part, got, out_a, out_b, first, last):
     for r in range(3, 11):
         c = c_mid[r - 3] if r < 5 else c_part[r - 5] + got[1 - meta[0], 10 - r]
-        out_a[r - 3] = e_a[r] * (0.5 * c[:32])
-        out_b[r - 3] = e_b[r] * (0.5 * c[32:])
+        new_a, new_b = e_a[r] * (0.5 * c[:32]), e_b[r] * (0.5 * c[32:])
+        out_a[r - 3] = new_a
+        out_b[r - 3] = new_b
+        if r < 8:
+            first[r - 3] = new_a
+            last[r - 3] = new_b
+
+
+def halo_body(low, high, out):
+    for j in range(3):
+        out[j, 0:32] = low[j + 2]
+        out[j, 32:64] = high[j + 2]
 
 
 def update_far_body(far, e_a, e_b, c, got, out_a, out_b):
@@ -247,9 +269,13 @@
         out_b[r + 3] = (far[-1 - r, 32:] if r < 0 else e_b[r]) * factor[32:]
 
 
-def early2_body(meta, e_a, e_b, e_low, e_high, obs, o_low, o_high, zf, zb, xf, xb, yw, ze, bx, buf):
+def early2_body(meta, e_a, e_b, e_low, e_high, got, obs, o_low, o_high, zf, zb, xf, xb, yw, ze, bx, buf):
     for r in range(8):
-        for v, x in enumerate(blur_z(zf, e_low[r], e_a[r], e_b[r], e_high[r])):
+        if r < 5:
+            low, high = e_low[r], e_high[r]
+        else:
+            low, high = got[1 - meta[0], 7 - r, 0:32], got[1 - meta[0], 7 - r, 32:64]
+        for v, x in enumerate(blur_z(zf, low, e_a[r], e_b[r], high)):
             buf[v, r] = x
             if r < 6:
                 ze[v, r] = x
@@ -306,14 +332,12 @@
         out[r, 32:] = f_b[r + 3] * (0.5 * c[32:])
 
 
-def output_body(meta, far, mid, out):
-    def body(core, at):
-        for c in range(2):
-            block = [far[c, r] if r < 3 else mid[c, r - 3] for r in range(8)]
-            block = block if c == 0 else block[::-1]
-            out[:, 8 * c : 8 * c + 8, :] = jnp.swapaxes(jnp.stack(block), 0, 1)
-
-    body(0, None)
+def output_body(far, mid, out):
+    planes = pl.ds(pl.multiple_of(16 * pl.program_id(0), 16), 16)
+    for c in range(2):
+        block = [far[c, r, planes] if r < 3 else mid[c, r - 3, planes] for r in range(8)]
+        block = block if c == 0 else block[::-1]
+        out[:, 8 * c : 8 * c + 8, :] = jnp.swapaxes(jnp.stack(block), 0, 1)
 
 
 def on_device(observed, start, spread_z, spread_y, spread_x):
@@ -338,7 +362,14 @@
     ).astype(jnp.int32)
     recorded = observed[0]
 
-    (send_far,) = call(far_body, [f32(3, 64, NX)], meta, start)
+    send_far = pl.pallas_call(
+        far_body,
+        out_shape=f32(3, 64, NX),
+        in_specs=[SM, pl.BlockSpec(memory_space=pltpu.HBM)],
+        out_specs=VM,
+        scratch_shapes=[pltpu.VMEM((64, 8, NX), F32), pltpu.SemaphoreType.DMA(())],
+        compiler_params=pltpu.CompilerParams(vmem_limit_bytes=60 * 1024 * 1024),
+    )(meta, start)
     f = far(send_far)
     e_a, e_b = call(start_body, [f32(11, 32, NX)] * 2, meta, start)
     e_low, e_high = along_z(e_a, e_b)
@@ -359,19 +390,26 @@
     obs = (obs, o_low, o_high)
     (ze,) = call(early1_body, [f32(2, 11, 96, NX)], e_a, e_b, e_low, e_high, zf, smem=0)
     f_low, f_high = along_z(*call(faces_body, [f32(3, 32, NX)] * 2, f, ze, smem=0))
-    (bx,) = call(middle1_body, [f32(2, 5, 64, NX)], meta, ze, *obs, zb, xf, xb, yw)
-    c_far, c_mid, c_part = call(
-        late1_body, [f32(6, 64, NX), f32(2, 64, NX), f32(6, 64, NX)],
+    (bx,) = call(middle1_body, [f32(2, 3, 64, NX)], meta, ze, *obs, zb, xf, xb, yw)
+    c_far, bx0 = call(
+        late1_body, [f32(6, 64, NX), f32(2, 3, 64, NX)],
         meta, f, f_low, f_high, ze, bx, *obs, zf, zb, xf, xb, yw,
-        scratch=[pltpu.VMEM((2, 3, 96, NX), F32), pltpu.VMEM((2, 3, 64, NX), F32)],
+        scratch=[pltpu.VMEM((2, 3, 96, NX), F32)],
     )
     got_far = far(c_far)
+    c_mid, c_part = call(
+        rest1_body, [f32(2, 64, NX), f32(6, 64, NX)],
+        meta, ze, bx0, bx, *obs, zb, xf, xb, yw,
+        scratch=[pltpu.VMEM((2, 2, 64, NX), F32)],
+    )
     got = both(c_part)
-    m_a, m_b = call(update_mid_body, [f32(8, 32, NX)] * 2, meta, e_a, e_b, c_mid, c_part, got)
-    m_low, m_high = along_z(m_a, m_b)
+    m_a, m_b, first, last = call(
+        update_mid_body, [f32(8, 32, NX)] * 2 + [f32(5, 32, NX)] * 2, meta, e_a, e_b, c_mid, c_part, got)
+    m_low, m_high = along_z(first, last)
+    (halo,) = call(halo_body, [f32(3, 64, NX)], m_low, m_high, smem=0)
     ze, bx6 = call(
         early2_body, [f32(2, 6, 96, NX), f32(2, 2, 64, NX)],
-        meta, m_a, m_b, m_low, m_high, *obs, zf, zb, xf, xb, yw,
+        meta, m_a, m_b, m_low, m_high, both(halo), *obs, zf, zb, xf, xb, yw,
         scratch=[pltpu.VMEM((2, 8, 96, NX), F32)],
     )
     n_a, n_b = call(update_far_body, [f32(6, 32, NX)] * 2, f, e_a, e_b, c_far, got_far, smem=0)
@@ -391,8 +429,14 @@
     other_mid = both(mid)
     (last,) = call(final_far_body, [f32(3, 64, NX)], n_a, n_b, c_own, got_far, smem=0)
     other_last = both(last)
-    (out,) = call(output_body, [f32(64, 16, NX)], meta, other_last, other_mid)
-    return out
+    return pl.pallas_call(
+        output_body,
+        out_shape=f32(64, 16, NX),
+        grid=(4,),
+        in_specs=[VM, VM],
+        out_specs=pl.BlockSpec((16, 16, NX), lambda i: (i, 0, 0)),
+        compiler_params=pltpu.CompilerParams(vmem_limit_bytes=LIMIT),
+    )(other_last, other_mid)
 
 
 def solution(mesh):

time: 150 us -> 152 us (1.013)
  blocking collectives: 19.2 us -> 25.9 us
  waiting for transfers between devices: 51.8 us -> 46.1 us
  Pallas kernels: 19.2 us -> 21.7 us
  starting transfers between devices: 57.9 us -> 55.8 us
    all_gather x7 -> x8, blocking collectives: 19.2 us -> 25.9 us  [both(): return lax.all_gather(x, 'view')]
    ppermute x3, waiting for transfers between devices: 44.7 us -> 40.2 us  [far(): return lax.ppermute(x, ('view', 'gy'), across)]
    pallas_call x0 -> x2, Pallas kernels: none -> 4.04 us  [the longest x1 2.45 us: on_device(): pl.pallas_call(far_body, out_shape=f32(3, 64, NX), in_specs=[SM, pl.Block...]
    ppermute x10, starting transfers between devices: 33.3 us -> 31.2 us  [along_z(): return (lax.ppermute(last, 'gz', up), lax.ppermute(first, 'gz', down))]
    pallas_call x18, Pallas kernels: 19.2 us -> 17.7 us  [call(): pl.pallas_call(body, out_shape=outs, in_specs=[SM] * smem + [VM] * (len(a...]
  transfers between devices with their start and end apart: 13 -> 13, of which waited for: 6 -> 4; matrix products, arithmetic and copies ran while one was open for 0% -> 0% of each run, Pallas kernels for 8% -> 9%
where the time goes in v5:
time: 152 us; the launch traced here: 151 us
  starting transfers between devices  55.8 us (37%)
  waiting for transfers between devices  46.1 us (30%)
  blocking collectives  25.9 us (17%)
  Pallas kernels  21.7 us (14%)
    ppermute x3, waiting for transfers between devices, far(): return lax.ppermute(x, ('view', 'gy'), across)  40.2 us
    ppermute x10, starting transfers between devices, along_z(): return (lax.ppermute(last, 'gz', up), lax.ppermute(first, 'gz', down))  31.2 us
    all_gather x8, blocking collectives, both(): return lax.all_gather(x, 'view')  25.9 us
    ppermute x3, starting transfers between devices, far(): return lax.ppermute(x, ('view', 'gy'), across)  24.6 us
    pallas_call x18, Pallas kernels, call(): pl.pallas_call(body, out_shape=outs, in_specs=[SM] * smem + [VM] * (len(a...  17.7 us
    ppermute x10, waiting for transfers between devices, along_z(): return (lax.ppermute(last, 'gz', up), lax.ppermute(first, 'gz', down))  5.84 us
  transfers between devices with their start and end apart: 13, of which 4 were waited for; matrix products, arithmetic and copies ran while one was open for 0% of the time, Pallas kernels for 9%

profile of v5, /device:TPU:29, one launch (start us, length us, event | category | flops | bytes accessed | tf_op | source)
XLA Modules:
  0.0 151.2 jit_solution(12196352442904550464)
XLA Ops:
  0.0 0.0 copy-start
  0.0 0.0 copy-start.1
  0.0 0.7 pad_add_fusion.meta
  0.7 2.4 %shard_map.55 = f32[3,64,256]{2,1,0:T(8,128)} custom-call(s32[3]{0:T(128)} %pad_add_fusion.meta, f32[64,16,256]{2,1,0:T(8,128)} %start.3), custom_call_target="tpu_custom_call" | custom-call | tf_op jit(solution)/shard_map/pallas_call | solution.py:365
  3.1 16.0 %collective-permute-start = (f32[3,64,256]{2,1,0:T(8,128)}, f32[3,64,256]{2,1,0:T(8,128)S(1)}, u32[]{:S(2)}, u32[]{:S(2)}) collective-permute-start(f32[3,64,256]{2,1,0:T(8,128)} %shard_map.55), channel_id=1, source_target_pairs={{256,1},{257,2},{258,3},{259,4},{260,5},{261,6},{262,7},{1,256},{2... | collective-permute-start | bytes 589832 | tf_op jit(solution)/shard_map/ppermute | solution.py:351
  19.1 0.0 copy-done
  19.1 0.0 copy-start.2
  19.1 0.7 copy-done.2
  19.8 0.7 shard_map.56
  20.5 2.4 %collective-permute-start.2 = (f32[11,32,256]{2,1,0:T(8,128)S(1)}, f32[11,32,256]{2,1,0:T(8,128)S(1)}, u32[]{:S(2)}, u32[]{:S(2)}) collective-permute-start(f32[11,32,256]{2,1,0:T(8,128)S(1)} %get-tuple-element.37.e_a), channel_id=1, source_target_pairs={{8,0},{16,8},{24,16},{32,24},{40,32},{48,40},{56,48},{64,56},{72,6... | collective-permute-start | bytes 1081352 | tf_op jit(solution)/shard_map/ppermute | solution.py:357
  22.9 5.0 %collective-permute-start.1 = (f32[11,32,256]{2,1,0:T(8,128)S(1)}, f32[11,32,256]{2,1,0:T(8,128)S(1)}, u32[]{:S(2)}, u32[]{:S(2)}) collective-permute-start(f32[11,32,256]{2,1,0:T(8,128)S(1)} %get-tuple-element.38.e_b), channel_id=1, source_target_pairs={{0,8},{8,16},{16,24},{24,32},{32,40},{40,48},{48,56},{56,64},{64,7... | collective-permute-start | bytes 1081352 | tf_op jit(solution)/shard_map/ppermute | solution.py:357
  27.9 0.0 copy-done.1
  28.0 0.8 shard_map.61
  28.8 2.2 %all-gather.1 = f32[8,64,256]{2,1,0:T(8,128)S(1)} all-gather(f32[4,64,256]{2,1,0:T(8,128)S(1)} %get-tuple-element.43), channel_id=3, replica_groups=mesh['view'=2,'gz'=32,'gy'=8] {'view'}, dimensions={0}, use_global_device_ids=true | all-gather | bytes 786432 | tf_op jit(solution)/shard_map/all_gather | solution.py:354
  30.9 0.0 copy-start.4
  30.9 0.0 copy-start.5
  30.9 2.3 %all-gather.2 = f32[8,64,256]{2,1,0:T(8,128)S(1)} all-gather(f32[4,64,256]{2,1,0:T(8,128)S(1)} %get-tuple-element.44), channel_id=4, replica_groups=mesh['view'=2,'gz'=32,'gy'=8] {'view'}, dimensions={0}, use_global_device_ids=true | all-gather | bytes 786432 | tf_op jit(solution)/shard_map/all_gather | solution.py:354
  33.2 0.6 shard_map.62
  33.9 1.9 %collective-permute-start.5 = (f32[2,8,16,256]{3,2,1,0:T(8,128)S(1)}, f32[2,8,16,256]{3,2,1,0:T(8,128)S(1)}, u32[]{:S(2)}, u32[]{:S(2)}) collective-permute-start(f32[2,8,16,256]{3,2,1,0:T(8,128)S(1)} %get-tuple-element.46), channel_id=1, source_target_pairs={{0,8},{8,16},{16,24},{24,32},{32,40},{40,48},{48,56},{56,64},{64,7... | collective-permute-start | bytes 786440 | tf_op jit(solution)/shard_map/ppermute | solution.py:357
  35.8 3.4 %collective-permute-start.6 = (f32[2,8,16,256]{3,2,1,0:T(8,128)S(1)}, f32[2,8,16,256]{3,2,1,0:T(8,128)S(1)}, u32[]{:S(2)}, u32[]{:S(2)}) collective-permute-start(f32[2,8,16,256]{3,2,1,0:T(8,128)S(1)} %get-tuple-element.47), channel_id=1, source_target_pairs={{8,0},{16,8},{24,16},{32,24},{40,32},{48,40},{56,48},{64,56},{72,6... | collective-permute-start | bytes 786440 | tf_op jit(solution)/shard_map/ppermute | solution.py:357
  39.2 0.0 copy-done.4
  39.2 0.0 copy-done.5
  39.2 0.0 copy-done.6
  39.2 2.4 %all-gather = f32[16,256]{1,0:T(8,128)S(1)} all-gather(f32[8,256]{1,0:T(8,128)S(1)} %shard_map.57), channel_id=2, replica_groups=mesh['view'=2,'gz'=32,'gy'=8] {'view'}, dimensions={0}, use_global_device_ids=true | all-gather | bytes 24576 | tf_op jit(solution)/shard_map/all_gather | solution.py:354
  41.6 1.8 %shard_map.58 = (bf16[384,256]{1,0:T(8,128)(2,1)S(1)}, bf16[2,128,192]{2,1,0:T(8,128)(2,1)S(1)}, bf16[2,2,256,256]{3,2,1,0:T(8,128)(2,1)S(1)}, bf16[2,2,256,256]{3,2,1,0:T(8,128)(2,1)S(1)}, f32[16,256]{1,0:T(8,128)S(1)}) custom-call(s32[3]{0:T(128)S(1)} %copy-done.2, f32[2,8,256]{2,1,0:T(8,128)S(1)} %bitcast.20), custom_call_target="tpu_custom_call" | custom-call | tf_op jit(solution)/shard_map/pallas_call | solution.py:19
  43.4 2.1 %collective-permute-done.2.e_high = f32[11,32,256]{2,1,0:T(8,128)S(1)} collective-permute-done((f32[11,32,256]{2,1,0:T(8,128)S(1)}, f32[11,32,256]{2,1,0:T(8,128)S(1)}, u32[]{:S(2)}, u32[]{:S(2)}) %collective-permute-start.2) | collective-permute-done | bytes 360480 | tf_op jit(solution)/shard_map/ppermute | solution.py:357
  45.6 0.0 collective-permute-done.1.e_low
  45.6 0.7 shard_map.59._.ze
  46.3 0.0 collective-permute-done.far.f
  46.3 3.9 %collective-permute-start.3 = (f32[3,32,256]{2,1,0:T(8,128)S(1)}, f32[3,32,256]{2,1,0:T(8,128)S(1)}, u32[]{:S(2)}, u32[]{:S(2)}) collective-permute-start(f32[3,32,256]{2,1,0:T(8,128)S(1)} %get-tuple-element.40), channel_id=1, source_target_pairs={{0,8},{8,16},{16,24},{24,32},{32,40},{40,48},{48,56},{56,64},{64,7... | collective-permute-start | bytes 294920 | tf_op jit(solution)/shard_map/ppermute | solution.py:357
  50.3 1.9 %collective-permute-start.4 = (f32[3,32,256]{2,1,0:T(8,128)S(1)}, f32[3,32,256]{2,1,0:T(8,128)S(1)}, u32[]{:S(2)}, u32[]{:S(2)}) collective-permute-start(f32[3,32,256]{2,1,0:T(8,128)S(1)} %get-tuple-element.41), channel_id=1, source_target_pairs={{8,0},{16,8},{24,16},{32,24},{40,32},{48,40},{56,48},{64,56},{72,6... | collective-permute-start | bytes 294920 | tf_op jit(solution)/shard_map/ppermute | solution.py:357
  52.2 0.0 collective-permute-done.5.o_low
  52.2 0.0 collective-permute-done.6.o_high
  52.2 1.8 %shard_map.63.bx.bx3 = f32[2,3,64,256]{3,2,1,0:T(8,128)S(1)} custom-call(s32[3]{0:T(128)S(1)} %copy-done.2, f32[2,11,96,256]{3,2,1,0:T(8,128)S(1)} %shard_map.59._.ze, f32[2,8,64,256]{3,2,1,0:T(8,128)S(1)} %get-tuple-element.45.obs, f32[2,8,16,256]{3,2,1,0:T(8,128)S(1)} %collective-permute-done.5.o_low, f32[2,8,16,256]{3,2,1,0:T(8,128)S(1)} %collective-permute-done.6.o_high, ...), custom_call_target="tpu_custom_call" | custom-call | tf_op jit(solution)/shard_map/pallas_call | solution.py:19
  54.0 0.0 collective-permute-done.3.f_low
  54.0 3.7 %collective-permute-done.4.f_high = f32[3,32,256]{2,1,0:T(8,128)S(1)} collective-permute-done((f32[3,32,256]{2,1,0:T(8,128)S(1)}, f32[3,32,256]{2,1,0:T(8,128)S(1)}, u32[]{:S(2)}, u32[]{:S(2)}) %collective-permute-start.4) | collective-permute-done | bytes 98336 | tf_op jit(solution)/shard_map/ppermute | solution.py:357
  57.7 2.1 %shard_map.64 = (f32[6,64,256]{2,1,0:T(8,128)S(1)}, f32[2,3,64,256]{3,2,1,0:T(8,128)S(1)}) custom-call(s32[3]{0:T(128)S(1)} %copy-done.2, f32[3,64,256]{2,1,0:T(8,128)S(1)} %collective-permute-done.far.f, f32[3,32,256]{2,1,0:T(8,128)S(1)} %collective-permute-done.3.f_low, f32[3,32,256]{2,1,0:T(8,128)S(1)} %collective-permute-done.4.f_high, ...), custom_call_target="tpu_custom_call" | custom-call | tf_op jit(solution)/shard_map/pallas_call | solution.py:19
  59.9 6.7 %collective-permute-start.7 = (f32[6,64,256]{2,1,0:T(8,128)S(1)}, f32[6,64,256]{2,1,0:T(8,128)S(1)}, u32[]{:S(2)}, u32[]{:S(2)}) collective-permute-start(f32[6,64,256]{2,1,0:T(8,128)S(1)} %get-tuple-element.52.c), channel_id=1, source_target_pairs={{256,1},{257,2},{258,3},{259,4},{260,5},{261,6},{262,7},{1,256},{2... | collective-permute-start | bytes 1179656 | tf_op jit(solution)/shard_map/ppermute | solution.py:351
  66.5 1.7 %shard_map.66 = (f32[2,64,256]{2,1,0:T(8,128)S(1)}, f32[6,64,256]{2,1,0:T(8,128)S(1)}) custom-call(s32[3]{0:T(128)S(1)} %copy-done.2, f32[2,11,96,256]{3,2,1,0:T(8,128)S(1)} %shard_map.59._.ze, f32[2,3,64,256]{3,2,1,0:T(8,128)S(1)} %get-tuple-element.55.bx0, f32[2,3,64,256]{3,2,1,0:T(8,128)S(1)} %shard_map.63.bx.bx3, ...), custom_call_target="tpu_custom_call" | custom-call | tf_op jit(solution)/shard_map/pallas_call | solution.py:19
  68.2 2.4 %all-gather.3 = f32[12,64,256]{2,1,0:T(8,128)S(1)} all-gather(f32[6,64,256]{2,1,0:T(8,128)S(1)} %get-tuple-element.57.c_part), channel_id=5, replica_groups=mesh['view'=2,'gz'=32,'gy'=8] {'view'}, dimensions={0}, use_global_device_ids=true | all-gather | bytes 1179648 | tf_op jit(solution)/shard_map/all_gather | solution.py:354
  70.6 0.6 shard_map.67
  71.2 1.9 %collective-permute-start.10 = (f32[5,32,256]{2,1,0:T(8,128)S(1)}, f32[5,32,256]{2,1,0:T(8,128)S(1)}, u32[]{:S(2)}, u32[]{:S(2)}) collective-permute-start(f32[5,32,256]{2,1,0:T(8,128)S(1)} %get-tuple-element.60), channel_id=1, source_target_pairs={{0,8},{8,16},{16,24},{24,32},{32,40},{40,48},{48,56},{56,64},{64,7... | collective-permute-start | bytes 491528 | tf_op jit(solution)/shard_map/ppermute | solution.py:357
  73.1 0.0 copy-start.3
  73.1 3.4 %collective-permute-start.11 = (f32[5,32,256]{2,1,0:T(8,128)S(1)}, f32[5,32,256]{2,1,0:T(8,128)S(1)}, u32[]{:S(2)}, u32[]{:S(2)}) collective-permute-start(f32[5,32,256]{2,1,0:T(8,128)S(1)} %get-tuple-element.61), channel_id=1, source_target_pairs={{8,0},{16,8},{24,16},{32,24},{40,32},{48,40},{56,48},{64,56},{72,6... | collective-permute-start | bytes 491528 | tf_op jit(solution)/shard_map/ppermute | solution.py:357
  76.5 30.9 %collective-permute-done.7.got = f32[6,64,256]{2,1,0:T(8,128)S(1)} collective-permute-done((f32[6,64,256]{2,1,0:T(8,128)S(1)}, f32[6,64,256]{2,1,0:T(8,128)S(1)}, u32[]{:S(2)}, u32[]{:S(2)}) %collective-permute-start.7) | collective-permute-done | bytes 393248 | tf_op jit(solution)/shard_map/ppermute | solution.py:351
  107.4 0.1 shard_map.65
  107.5 1.9 %collective-permute-start.9 = (f32[6,32,256]{2,1,0:T(8,128)S(1)}, f32[6,32,256]{2,1,0:T(8,128)S(1)}, u32[]{:S(2)}, u32[]{:S(2)}) collective-permute-start(f32[6,32,256]{2,1,0:T(8,128)S(1)} %get-tuple-element.53.f_a), channel_id=1, source_target_pairs={{8,0},{16,8},{24,16},{32,24},{40,32},{48,40},{56,48},{64,56},{72,6... | collective-permute-start | bytes 589832 | tf_op jit(solution)/shard_map/ppermute | solution.py:357
  109.4 5.5 %collective-permute-start.8 = (f32[6,32,256]{2,1,0:T(8,128)S(1)}, f32[6,32,256]{2,1,0:T(8,128)S(1)}, u32[]{:S(2)}, u32[]{:S(2)}) collective-permute-start(f32[6,32,256]{2,1,0:T(8,128)S(1)} %get-tuple-element.54.f_b), channel_id=1, source_target_pairs={{0,8},{8,16},{16,24},{24,32},{32,40},{40,48},{48,56},{56,64},{64,7... | collective-permute-start | bytes 589832 | tf_op jit(solution)/shard_map/ppermute | solution.py:357
  114.9 0.0 collective-permute-done.10.low.e_low
  114.9 0.0 collective-permute-done.11.high.e_high
  114.9 2.9 %all-gather.4 = f32[6,64,256]{2,1,0:T(8,128)S(1)} all-gather(f32[3,64,256]{2,1,0:T(8,128)S(1)} %shard_map.68), channel_id=6, replica_groups=mesh['view'=2,'gz'=32,'gy'=8] {'view'}, dimensions={0}, use_global_device_ids=true | all-gather | bytes 589824 | tf_op jit(solution)/shard_map/all_gather | solution.py:354
  117.9 0.0 copy-done.3
  117.9 2.0 %shard_map.69 = (f32[2,6,96,256]{3,2,1,0:T(8,128)S(1)}, f32[2,2,64,256]{3,2,1,0:T(8,128)S(1)}) custom-call(s32[3]{0:T(128)S(1)} %copy-done.3, f32[8,32,256]{2,1,0:T(8,128)S(1)} %get-tuple-element.58.e_a, f32[8,32,256]{2,1,0:T(8,128)S(1)} %get-tuple-element.59.e_b, f32[5,32,256]{2,1,0:T(8,128)S(1)} %collective-permute-done.10.low.e_low, ...), custom_call_target="tpu_custom_call" | custom-call | tf_op jit(solution)/shard_map/pallas_call | solution.py:19
  119.8 0.0 collective-permute-done.9.f_high
  119.8 0.0 collective-permute-done.8.f_low
  119.8 2.1 %shard_map.70 = (f32[3,64,256]{2,1,0:T(8,128)S(1)}, f32[2,6,96,256]{3,2,1,0:T(8,128)S(1)}, f32[2,3,64,256]{3,2,1,0:T(8,128)S(1)}) custom-call(s32[3]{0:T(128)S(1)} %copy-done.3, f32[6,32,256]{2,1,0:T(8,128)S(1)} %get-tuple-element.53.f_a, f32[6,32,256]{2,1,0:T(8,128)S(1)} %get-tuple-element.54.f_b, f32[6,32,256]{2,1,0:T(8,128)S(1)} %collective-permute-done.8.f_low, ...), custom_call_target="tpu_custom_call" | custom-call | tf_op jit(solution)/shard_map/pallas_call | solution.py:19
  122.0 1.9 %collective-permute-start.12 = (f32[3,64,256]{2,1,0:T(8,128)S(1)}, f32[3,64,256]{2,1,0:T(8,128)S(1)}, u32[]{:S(2)}, u32[]{:S(2)}) collective-permute-start(f32[3,64,256]{2,1,0:T(8,128)S(1)} %get-tuple-element.67), channel_id=1, source_target_pairs={{256,1},{257,2},{258,3},{259,4},{260,5},{261,6},{262,7},{1,256},{2... | collective-permute-start | bytes 589832 | tf_op jit(solution)/shard_map/ppermute | solution.py:351
  123.9 2.0 %shard_map.71 = (f32[8,64,256]{2,1,0:T(8,128)S(1)}, f32[3,64,256]{2,1,0:T(8,128)S(1)}) custom-call(s32[3]{0:T(128)S(1)} %copy-done.3, f32[2,6,96,256]{3,2,1,0:T(8,128)S(1)} %get-tuple-element.63.zn, f32[2,6,96,256]{3,2,1,0:T(8,128)S(1)} %get-tuple-element.62.ze, f32[2,3,64,256]{3,2,1,0:T(8,128)S(1)} %get-tuple-element.64.bx0, ...), custom_call_target="tpu_custom_call" | custom-call | tf_op jit(solution)/shard_map/pallas_call | solution.py:19
  125.9 2.1 %all-gather.6 = f32[6,64,256]{2,1,0:T(8,128)S(1)} all-gather(f32[3,64,256]{2,1,0:T(8,128)S(1)} %get-tuple-element.68), channel_id=8, replica_groups=mesh['view'=2,'gz'=32,'gy'=8] {'view'}, dimensions={0}, use_global_device_ids=true | all-gather | bytes 589824 | tf_op jit(solution)/shard_map/all_gather | solution.py:354
  128.0 0.6 shard_map.73
  128.6 2.3 %all-gather.7 = f32[10,64,256]{2,1,0:T(8,128)S(1)} all-gather(f32[5,64,256]{2,1,0:T(8,128)S(1)} %shard_map.73), channel_id=9, replica_groups=mesh['view'=2,'gz'=32,'gy'=8] {'view'}, dimensions={0}, use_global_device_ids=true | all-gather | bytes 983040 | tf_op jit(solution)/shard_map/all_gather | solution.py:354
  130.9 9.3 %collective-permute-done.12.got = f32[3,64,256]{2,1,0:T(8,128)S(1)} collective-permute-done((f32[3,64,256]{2,1,0:T(8,128)S(1)}, f32[3,64,256]{2,1,0:T(8,128)S(1)}, u32[]{:S(2)}, u32[]{:S(2)}) %collective-permute-start.12) | collective-permute-done | bytes 196640 | tf_op jit(solution)/shard_map/ppermute | solution.py:351
  140.2 9.4 %all-gather.5 = f32[6,64,256]{2,1,0:T(8,128)S(1)} all-gather(f32[3,64,256]{2,1,0:T(8,128)S(1)} %shard_map.72), channel_id=7, replica_groups=mesh['view'=2,'gz'=32,'gy'=8] {'view'}, dimensions={0}, use_global_device_ids=true | all-gather | bytes 589824 | tf_op jit(solution)/shard_map/all_gather | solution.py:354
  149.6 1.6 %shard_map.74 = f32[64,16,256]{2,1,0:T(8,128)} custom-call(f32[2,3,64,256]{3,2,1,0:T(8,128)S(1)} %bitcast.17, f32[2,5,64,256]{3,2,1,0:T(8,128)S(1)} %bitcast.13), custom_call_target="tpu_custom_call" | custom-call | tf_op jit(solution)/shard_map/pallas_call | solution.py:432
  (5 shorter events, 0.1 us)
Async XLA Ops:
  0.0 19.1 %copy-start = (f32[64,16,256]{2,1,0:T(8,128)S(1)}, f32[64,16,256]{2,1,0:T(8,128)}, u32[]{:S(2)}) copy-start(f32[64,16,256]{2,1,0:T(8,128)} %start.3) | copy-start | bytes 3145732
  0.0 27.9 %copy-start.1 = (f32[1,64,16,256]{3,2,1,0:T(8,128)S(1)}, f32[1,64,16,256]{3,2,1,0:T(8,128)}, u32[]{:S(2)}) copy-start(f32[1,64,16,256]{3,2,1,0:T(8,128)} %param.5) | copy-start | bytes 3145732
  3.1 43.2 %collective-permute-start = (f32[3,64,256]{2,1,0:T(8,128)}, f32[3,64,256]{2,1,0:T(8,128)S(1)}, u32[]{:S(2)}, u32[]{:S(2)}) collective-permute-start(f32[3,64,256]{2,1,0:T(8,128)} %shard_map.55), channel_id=1, source_target_pairs={{256,1},{257,2},{258,3},{259,4},{260,5},{261,6},{262,7},{1,256},{2... | collective-permute-start | bytes 589832 | tf_op jit(solution)/shard_map/ppermute | solution.py:351
  19.1 0.7 copy-start.2
  20.5 25.0 %collective-permute-start.2 = (f32[11,32,256]{2,1,0:T(8,128)S(1)}, f32[11,32,256]{2,1,0:T(8,128)S(1)}, u32[]{:S(2)}, u32[]{:S(2)}) collective-permute-start(f32[11,32,256]{2,1,0:T(8,128)S(1)} %get-tuple-element.37.e_a), channel_id=1, source_target_pairs={{8,0},{16,8},{24,16},{32,24},{40,32},{48,40},{56,48},{64,56},{72,6... | collective-permute-start | bytes 1081352 | tf_op jit(solution)/shard_map/ppermute | solution.py:357
  22.9 22.6 %collective-permute-start.1 = (f32[11,32,256]{2,1,0:T(8,128)S(1)}, f32[11,32,256]{2,1,0:T(8,128)S(1)}, u32[]{:S(2)}, u32[]{:S(2)}) collective-permute-start(f32[11,32,256]{2,1,0:T(8,128)S(1)} %get-tuple-element.38.e_b), channel_id=1, source_target_pairs={{0,8},{8,16},{16,24},{24,32},{32,40},{40,48},{48,56},{56,64},{64,7... | collective-permute-start | bytes 1081352 | tf_op jit(solution)/shard_map/ppermute | solution.py:357
  30.9 8.3 %copy-start.4 = (f32[1,31]{1,0:T(1,128)S(1)}, f32[1,31]{1,0:T(1,128)}, u32[]{:S(2)}) copy-start(f32[1,31]{1,0:T(1,128)} %sz.1) | copy-start | bytes 376
  30.9 8.3 %copy-start.5 = (f32[1,7]{1,0:T(1,128)S(1)}, f32[1,7]{1,0:T(1,128)}, u32[]{:S(2)}) copy-start(f32[1,7]{1,0:T(1,128)} %sy.1) | copy-start | bytes 88
  30.9 8.3 %copy-start.6 = (f32[1,7]{1,0:T(1,128)S(1)}, f32[1,7]{1,0:T(1,128)}, u32[]{:S(2)}) copy-start(f32[1,7]{1,0:T(1,128)} %sx.1) | copy-start | bytes 88
  33.9 18.3 %collective-permute-start.5 = (f32[2,8,16,256]{3,2,1,0:T(8,128)S(1)}, f32[2,8,16,256]{3,2,1,0:T(8,128)S(1)}, u32[]{:S(2)}, u32[]{:S(2)}) collective-permute-start(f32[2,8,16,256]{3,2,1,0:T(8,128)S(1)} %get-tuple-element.46), channel_id=1, source_target_pairs={{0,8},{8,16},{16,24},{24,32},{32,40},{40,48},{48,56},{56,64},{64,7... | collective-permute-start | bytes 786440 | tf_op jit(solution)/shard_map/ppermute | solution.py:357
  35.8 16.4 %collective-permute-start.6 = (f32[2,8,16,256]{3,2,1,0:T(8,128)S(1)}, f32[2,8,16,256]{3,2,1,0:T(8,128)S(1)}, u32[]{:S(2)}, u32[]{:S(2)}) collective-permute-start(f32[2,8,16,256]{3,2,1,0:T(8,128)S(1)} %get-tuple-element.47), channel_id=1, source_target_pairs={{8,0},{16,8},{24,16},{32,24},{40,32},{48,40},{56,48},{64,56},{72,6... | collective-permute-start | bytes 786440 | tf_op jit(solution)/shard_map/ppermute | solution.py:357
  46.3 7.7 %collective-permute-start.3 = (f32[3,32,256]{2,1,0:T(8,128)S(1)}, f32[3,32,256]{2,1,0:T(8,128)S(1)}, u32[]{:S(2)}, u32[]{:S(2)}) collective-permute-start(f32[3,32,256]{2,1,0:T(8,128)S(1)} %get-tuple-element.40), channel_id=1, source_target_pairs={{0,8},{8,16},{16,24},{24,32},{32,40},{40,48},{48,56},{56,64},{64,7... | collective-permute-start | bytes 294920 | tf_op jit(solution)/shard_map/ppermute | solution.py:357
  50.3 7.5 %collective-permute-start.4 = (f32[3,32,256]{2,1,0:T(8,128)S(1)}, f32[3,32,256]{2,1,0:T(8,128)S(1)}, u32[]{:S(2)}, u32[]{:S(2)}) collective-permute-start(f32[3,32,256]{2,1,0:T(8,128)S(1)} %get-tuple-element.41), channel_id=1, source_target_pairs={{8,0},{16,8},{24,16},{32,24},{40,32},{48,40},{56,48},{64,56},{72,6... | collective-permute-start | bytes 294920 | tf_op jit(solution)/shard_map/ppermute | solution.py:357
  59.9 47.5 %collective-permute-start.7 = (f32[6,64,256]{2,1,0:T(8,128)S(1)}, f32[6,64,256]{2,1,0:T(8,128)S(1)}, u32[]{:S(2)}, u32[]{:S(2)}) collective-permute-start(f32[6,64,256]{2,1,0:T(8,128)S(1)} %get-tuple-element.52.c), channel_id=1, source_target_pairs={{256,1},{257,2},{258,3},{259,4},{260,5},{261,6},{262,7},{1,256},{2... | collective-permute-start | bytes 1179656 | tf_op jit(solution)/shard_map/ppermute | solution.py:351
  71.2 43.7 %collective-permute-start.10 = (f32[5,32,256]{2,1,0:T(8,128)S(1)}, f32[5,32,256]{2,1,0:T(8,128)S(1)}, u32[]{:S(2)}, u32[]{:S(2)}) collective-permute-start(f32[5,32,256]{2,1,0:T(8,128)S(1)} %get-tuple-element.60), channel_id=1, source_target_pairs={{0,8},{8,16},{16,24},{24,32},{32,40},{40,48},{48,56},{56,64},{64,7... | collective-permute-start | bytes 491528 | tf_op jit(solution)/shard_map/ppermute | solution.py:357
  73.1 44.7 %copy-start.3 = (s32[3]{0:T(128)S(1)}, s32[3]{0:T(128)}, u32[]{:S(2)}) copy-start(s32[3]{0:T(128)} %pad_add_fusion.meta) | copy-start | bytes 40
  73.1 41.8 %collective-permute-start.11 = (f32[5,32,256]{2,1,0:T(8,128)S(1)}, f32[5,32,256]{2,1,0:T(8,128)S(1)}, u32[]{:S(2)}, u32[]{:S(2)}) collective-permute-start(f32[5,32,256]{2,1,0:T(8,128)S(1)} %get-tuple-element.61), channel_id=1, source_target_pairs={{8,0},{16,8},{24,16},{32,24},{40,32},{48,40},{56,48},{64,56},{72,6... | collective-permute-start | bytes 491528 | tf_op jit(solution)/shard_map/ppermute | solution.py:357
  107.5 12.4 %collective-permute-start.9 = (f32[6,32,256]{2,1,0:T(8,128)S(1)}, f32[6,32,256]{2,1,0:T(8,128)S(1)}, u32[]{:S(2)}, u32[]{:S(2)}) collective-permute-start(f32[6,32,256]{2,1,0:T(8,128)S(1)} %get-tuple-element.53.f_a), channel_id=1, source_target_pairs={{8,0},{16,8},{24,16},{32,24},{40,32},{48,40},{56,48},{64,56},{72,6... | collective-permute-start | bytes 589832 | tf_op jit(solution)/shard_map/ppermute | solution.py:357
  109.4 10.5 %collective-permute-start.8 = (f32[6,32,256]{2,1,0:T(8,128)S(1)}, f32[6,32,256]{2,1,0:T(8,128)S(1)}, u32[]{:S(2)}, u32[]{:S(2)}) collective-permute-start(f32[6,32,256]{2,1,0:T(8,128)S(1)} %get-tuple-element.54.f_b), channel_id=1, source_target_pairs={{0,8},{8,16},{16,24},{24,32},{32,40},{40,48},{48,56},{56,64},{64,7... | collective-permute-start | bytes 589832 | tf_op jit(solution)/shard_map/ppermute | solution.py:357
  122.0 18.2 %collective-permute-start.12 = (f32[3,64,256]{2,1,0:T(8,128)S(1)}, f32[3,64,256]{2,1,0:T(8,128)S(1)}, u32[]{:S(2)}, u32[]{:S(2)}) collective-permute-start(f32[3,64,256]{2,1,0:T(8,128)S(1)} %get-tuple-element.67), channel_id=1, source_target_pairs={{256,1},{257,2},{258,3},{259,4},{260,5},{261,6},{262,7},{1,256},{2... | collective-permute-start | bytes 589832 | tf_op jit(solution)/shard_map/ppermute | solution.py:351
